TPU v7x, 32 devices: a whole 2x2x4 slice. The times are simulated.
32 devices in a mesh: fsdp: 4 (over y, x), ctx: 4 (over z), tp: 2 (over core).
Axes of the slice: x: 2, y: 2, z: 4, core: 2. Of those that a mesh axis runs over, the one named last changes fastest.
Arguments:
- layer_input: float32 [8, 1024, 2048], P(None, ('fsdp', 'ctx')), may hold values from -6 to 6
- cotangent: float32 [8, 1024, 2048], P(None, ('fsdp', 'ctx')), may hold values from -6 to 6
- seq_lengths: int32 [8], replicated, may hold values from 512 to 1024, as said below
- dealing: int32 [8], replicated, may hold values from 0 to 7, each once
- attn_gain: bfloat16 [2048], P('fsdp'), may hold values from 0.5 to 1.5
- attn_shift: bfloat16 [2048], P('fsdp'), may hold values from -1 to 1
- query_weight: bfloat16 [2048, 2048], P('fsdp', 'tp')
- query_bias: bfloat16 [16, 128], P('tp', 'fsdp'), may hold values from -1.5 to 1.5
- key_weight: bfloat16 [2048, 2048], P('fsdp', 'tp'), may hold values from -0.125 to 0.125
- value_weight: bfloat16 [2048, 2048], P('fsdp', 'tp'), may hold values from -0.125 to 0.125
- value_bias: bfloat16 [16, 128], P('tp', 'fsdp'), may hold values from -0.29882812 to 0.29882812
- out_weight: bfloat16 [2048, 2048], P('tp', 'fsdp'), may hold values from -2 to 2
- out_bias: bfloat16 [2048], P('fsdp'), may hold values from -1 to 1
- mlp_gain: bfloat16 [2048], P('fsdp'), may hold values from 0.5 to 1.5
- mlp_shift: bfloat16 [2048], P('fsdp'), may hold values from -1 to 1
- up_weight: bfloat16 [2048, 8192], P('fsdp', 'tp'), may hold values from -0.125 to 0.125
- up_bias: bfloat16 [4, 2048], P('tp', 'fsdp'), may hold values from -1 to 1
- down_weight: bfloat16 [8192, 2048], P('tp', 'fsdp'), may hold values from -0.0625 to 0.0625
- down_bias: bfloat16 [2048], P('fsdp'), may hold values from -1 to 1
- clip_level: float32 [1], replicated, may hold values from 5 to 9
Outputs:
- layer_output: float32 [8, 1024, 2048], P(None, ('fsdp', 'ctx'))
- input_grad: float32 [8, 1024, 2048], P(None, ('fsdp', 'ctx'))
- attn_gain_grad: float32 [2048], P('fsdp')
- attn_shift_grad: float32 [2048], P('fsdp')
- query_weight_grad: float32 [2048, 2048], P('fsdp', 'tp')
- query_bias_grad: float32 [16, 128], P('tp', 'fsdp')
- key_weight_grad: float32 [2048, 2048], P('fsdp', 'tp')
- value_weight_grad: float32 [2048, 2048], P('fsdp', 'tp')
- value_bias_grad: float32 [16, 128], P('tp', 'fsdp')
- out_weight_grad: float32 [2048, 2048], P('tp', 'fsdp')
- out_bias_grad: float32 [2048], P('fsdp')
- mlp_gain_grad: float32 [2048], P('fsdp')
- mlp_shift_grad: float32 [2048], P('fsdp')
- up_weight_grad: float32 [2048, 8192], P('fsdp', 'tp')
- up_bias_grad: float32 [4, 2048], P('tp', 'fsdp')
- down_weight_grad: float32 [8192, 2048], P('tp', 'fsdp')
- down_bias_grad: float32 [2048], P('fsdp')
- head_peak: float32 [16], P('tp')
- query_clipped: bfloat16 [2048, 2048], P('fsdp', 'tp')
- key_clipped: bfloat16 [2048, 2048], P('fsdp', 'tp')
Inputs may be any that keep to these rules, and one draw needn't show every extreme that they name: `seq_lengths`: valid tokens of each slot; its places from the length on are padding. `dealing`: a permutation of the 8 slots; dealt places j with j // 2 = g go to index g of fsdp.
All inputs are finite; a program needn't handle non-finite values.
Results may differ from a plain program's by a relative error of at most 0.019.
Values may be sent and summed in bfloat16 or wider, within the bound.
A program may use at most 320 MiB of HBM per device.

v0:
```python
import math

import jax
import jax.numpy as jnp
from jax import lax
from jax.sharding import PartitionSpec as P

EPS = 1e-05
NEG = -1e30
INV_ROOT_TWO = 0.7071067811865476
INV_ROOT_TWO_PI = 0.3989422804014327


def normalize(values, scale_vec, offset_vec):
    center = values - jnp.mean(values, -1, keepdims=True)
    inverse = lax.rsqrt(jnp.mean(center * center, -1, keepdims=True) + EPS)
    normed = center * inverse
    return (normed * scale_vec + offset_vec, normed, inverse)


def norm_back(upstream, normed, inverse, scale_vec):
    scaled = upstream * scale_vec
    inner = (
        scaled
        - jnp.mean(scaled, -1, keepdims=True)
        - normed * jnp.mean(scaled * normed, -1, keepdims=True)
    )
    return (inverse * inner, jnp.sum(upstream * normed, 0), jnp.sum(upstream, 0))


def matmul(left, right):
    return jnp.dot(left, right, preferred_element_type=jnp.float32)


def weight_product(left, right):
    return jnp.einsum("td,te->de", left, right, preferred_element_type=jnp.float32)


def back_product(left, right):
    return jnp.einsum("te,de->td", left, right, preferred_element_type=jnp.float32)


def body(
    layer_input,
    cotangent,
    seq_lengths,
    dealing,
    attn_gain,
    attn_shift,
    query_weight,
    query_bias,
    key_weight,
    value_weight,
    value_bias,
    out_weight,
    out_bias,
    mlp_gain,
    mlp_shift,
    up_weight,
    up_bias,
    down_weight,
    down_bias,
    clip_level,
):
    shard_count = lax.axis_size("fsdp")
    ctx_count = lax.axis_size("ctx")
    my_group = lax.axis_index("fsdp")
    ctx_place = lax.axis_index("ctx")
    slot_count, block_rows, width = layer_input.shape
    per_group = slot_count // shard_count
    local_rows = shard_count * block_rows
    tokens = per_group * local_rows
    dealt_input = jnp.take(layer_input, dealing, axis=0).reshape(
        shard_count, per_group, block_rows, width
    )
    dealt_grad = cotangent.reshape(shard_count, per_group, block_rows, width)
    arrived_input, arrived_grad = (
        lax.all_to_all(dealt_input, "fsdp", split_axis=0, concat_axis=2, tiled=True),
        lax.all_to_all(dealt_grad, "fsdp", split_axis=0, concat_axis=2, tiled=True),
    )
    resid = arrived_input.reshape(tokens, width)
    upstream = arrived_grad.reshape(tokens, width)
    seq_lens = lax.dynamic_slice_in_dim(
        jnp.take(seq_lengths, dealing), my_group * per_group, per_group
    )
    gathered = (
        lax.all_gather(attn_gain, "fsdp", axis=0, tiled=True),
        lax.all_gather(attn_shift, "fsdp", axis=0, tiled=True),
        lax.all_gather(query_weight, "fsdp", axis=0, tiled=True),
        lax.all_gather(query_bias, "fsdp", axis=1, tiled=True),
        lax.all_gather(key_weight, "fsdp", axis=0, tiled=True),
        lax.all_gather(value_weight, "fsdp", axis=0, tiled=True),
        lax.all_gather(value_bias, "fsdp", axis=1, tiled=True),
        lax.all_gather(out_weight, "fsdp", axis=1, tiled=True),
        lax.all_gather(out_bias, "fsdp", axis=0, tiled=True),
        lax.all_gather(mlp_gain, "fsdp", axis=0, tiled=True),
        lax.all_gather(mlp_shift, "fsdp", axis=0, tiled=True),
        lax.all_gather(up_weight, "fsdp", axis=0, tiled=True),
        lax.all_gather(up_bias, "fsdp", axis=1, tiled=True),
        lax.all_gather(down_weight, "fsdp", axis=1, tiled=True),
        lax.all_gather(down_bias, "fsdp", axis=0, tiled=True),
    )
    (
        gain_one,
        shift_one,
        query_mat,
        query_vec,
        key_mat,
        value_mat,
        value_vec,
        out_mat,
        out_vec,
        gain_two,
        shift_two,
        up_mat,
        up_vec,
        down_mat,
        down_vec,
    ) = gathered
    head_count, head_size = query_vec.shape
    features = head_count * head_size
    scale_of_scores = 1.0 / math.sqrt(head_size)
    row_ids = jnp.arange(local_rows, dtype=jnp.int32)
    query_pos = (row_ids // block_rows * ctx_count + ctx_place) * block_rows + row_ids % block_rows
    key_ids = jnp.arange(ctx_count * local_rows, dtype=jnp.int32)
    key_rows = key_ids % local_rows
    key_pos = (
        key_rows // block_rows * ctx_count + key_ids // local_rows
    ) * block_rows + key_rows % block_rows
    allowed = (key_pos[None, None, :] <= query_pos[None, :, None]) & (
        key_pos[None, None, :] < seq_lens[:, None, None]
    )
    query_live = query_pos[None, :] < seq_lens[:, None]
    normed_a, unit_one, inverse_one = normalize(
        resid, gain_one.astype(jnp.float32), shift_one.astype(jnp.float32)
    )
    act_one = normed_a.astype(jnp.bfloat16)
    queries = (
        (matmul(act_one, query_mat) + query_vec.reshape(features).astype(jnp.float32))
        .astype(jnp.bfloat16)
        .reshape(per_group, local_rows, features)
    )
    keys_mine = (
        matmul(act_one, key_mat).astype(jnp.bfloat16).reshape(per_group, local_rows, features)
    )
    values_mine = (
        (matmul(act_one, value_mat) + value_vec.reshape(features).astype(jnp.float32))
        .astype(jnp.bfloat16)
        .reshape(per_group, local_rows, features)
    )
    keys_all, values_all = (
        lax.all_gather(keys_mine, "ctx", axis=1, tiled=True),
        lax.all_gather(values_mine, "ctx", axis=1, tiled=True),
    )

    def head_cut(array, head_index):
        return lax.dynamic_slice_in_dim(array, head_index * head_size, head_size, 2)

    def head_scores(head_queries, head_keys):
        return (
            jnp.einsum("sqd,skd->sqk", head_queries, head_keys, preferred_element_type=jnp.float32)
            * scale_of_scores
        )

    def forward_head(head_index):
        logit_scores = head_scores(head_cut(queries, head_index), head_cut(keys_all, head_index))
        masked = jnp.where(allowed, logit_scores, NEG)
        row_top = jnp.max(masked, -1, keepdims=True)
        exp_terms = jnp.where(allowed, jnp.exp(masked - row_top), 0.0)
        total = jnp.sum(exp_terms, -1, keepdims=True)
        attention_probabilities = exp_terms / total
        attended_rows = jnp.einsum(
            "sqk,skd->sqd",
            attention_probabilities.astype(jnp.bfloat16),
            head_cut(values_all, head_index),
            preferred_element_type=jnp.float32,
        )
        log_total = row_top[..., 0] + jnp.log(total[..., 0])
        peak = jnp.max(jnp.where(query_live, row_top[..., 0], NEG))
        return (attended_rows, log_total, peak)

    attended_rows, log_totals, peaks = lax.map(forward_head, jnp.arange(head_count))
    attn_low = attended_rows.transpose(1, 2, 0, 3).reshape(tokens, features).astype(jnp.bfloat16)
    attn_sum = lax.psum(matmul(attn_low, out_mat), "tp")
    hidden = resid + attn_sum + out_vec.astype(jnp.float32)
    normed_b, unit_two, inverse_two = normalize(
        hidden, gain_two.astype(jnp.float32), shift_two.astype(jnp.float32)
    )
    act_two = normed_b.astype(jnp.bfloat16)
    pre = matmul(act_two, up_mat) + up_vec.reshape(-1).astype(jnp.float32)
    gelu_low = jax.nn.gelu(pre, approximate=False).astype(jnp.bfloat16)
    mlp_sum = lax.psum(matmul(gelu_low, down_mat).astype(jnp.bfloat16), "tp").astype(jnp.float32)
    layer_output = hidden + mlp_sum + down_vec.astype(jnp.float32)
    peak_all = lax.pmax(peaks, ("fsdp", "ctx"))
    level = clip_level[0]
    factor = jnp.repeat(jnp.sqrt(level / jnp.maximum(peak_all, level)), head_size)
    query_clipped = (query_weight.astype(jnp.float32) * factor[None, :]).astype(jnp.bfloat16)
    key_clipped = (key_weight.astype(jnp.float32) * factor[None, :]).astype(jnp.bfloat16)
    grad_low = upstream.astype(jnp.bfloat16)
    down_weight_grad = weight_product(gelu_low, grad_low)
    down_bias_grad = jnp.sum(upstream, 0)
    cdf = 0.5 * (1.0 + lax.erf(pre * INV_ROOT_TWO))
    density = jnp.exp(-0.5 * pre * pre) * INV_ROOT_TWO_PI
    pre_grad = back_product(grad_low, down_mat) * (cdf + pre * density)
    pre_low = pre_grad.astype(jnp.bfloat16)
    up_weight_grad = weight_product(act_two, pre_low)
    up_bias_grad = jnp.sum(pre_grad, 0).reshape(up_vec.shape)
    normed_two_grad = lax.psum(back_product(pre_low, up_mat), "tp")
    hidden_in, mlp_gain_grad, mlp_shift_grad = norm_back(
        normed_two_grad, unit_two, inverse_two, gain_two.astype(jnp.float32)
    )
    hidden_grad = upstream + hidden_in
    hidden_low = hidden_grad.astype(jnp.bfloat16)
    out_weight_grad = weight_product(attn_low, hidden_low)
    out_bias_grad = jnp.sum(hidden_grad, 0)
    attended_grad = (
        back_product(hidden_low, out_mat)
        .astype(jnp.bfloat16)
        .reshape(per_group, local_rows, features)
    )

    def backward_head(head_index):
        head_queries = head_cut(queries, head_index)
        head_keys = head_cut(keys_all, head_index)
        head_values = head_cut(values_all, head_index)
        grad_head = head_cut(attended_grad, head_index)
        logit_scores = head_scores(head_queries, head_keys)
        masked = jnp.where(allowed, logit_scores, NEG)
        attention_probabilities = jnp.where(
            allowed, jnp.exp(masked - log_totals[head_index][..., None]), 0.0
        )
        prob_grad = jnp.einsum(
            "sqd,skd->sqk", grad_head, head_values, preferred_element_type=jnp.float32
        )
        inner = jnp.sum(attention_probabilities * prob_grad, -1, keepdims=True)
        score_grad = (attention_probabilities * (prob_grad - inner)).astype(jnp.bfloat16)
        query_grad = (
            jnp.einsum("sqk,skd->sqd", score_grad, head_keys, preferred_element_type=jnp.float32)
            * scale_of_scores
        )
        key_grad = (
            jnp.einsum("sqk,sqd->skd", score_grad, head_queries, preferred_element_type=jnp.float32)
            * scale_of_scores
        )
        value_grad = jnp.einsum(
            "sqk,sqd->skd",
            attention_probabilities.astype(jnp.bfloat16),
            grad_head,
            preferred_element_type=jnp.float32,
        )
        return (query_grad, key_grad, value_grad)

    query_parts, key_parts, value_parts = lax.map(backward_head, jnp.arange(head_count))
    query_grads = query_parts.transpose(1, 2, 0, 3).reshape(tokens, features)
    key_whole = key_parts.transpose(1, 2, 0, 3).reshape(per_group, ctx_count * local_rows, features)
    value_whole = value_parts.transpose(1, 2, 0, 3).reshape(
        per_group, ctx_count * local_rows, features
    )
    key_summed, value_summed = (
        lax.psum_scatter(key_whole, "ctx", scatter_dimension=1, tiled=True),
        lax.psum_scatter(value_whole, "ctx", scatter_dimension=1, tiled=True),
    )
    key_grads = key_summed.reshape(tokens, features)
    value_grads = value_summed.reshape(tokens, features)
    query_bias_grad = jnp.sum(query_grads, 0).reshape(head_count, head_size)
    value_bias_grad = jnp.sum(value_grads, 0).reshape(head_count, head_size)
    query_low = query_grads.astype(jnp.bfloat16)
    key_low = key_grads.astype(jnp.bfloat16)
    value_low = value_grads.astype(jnp.bfloat16)
    query_weight_grad = weight_product(act_one, query_low)
    key_weight_grad = weight_product(act_one, key_low)
    value_weight_grad = weight_product(act_one, value_low)
    normed_one_grad = lax.psum(
        (
            back_product(query_low, query_mat)
            + back_product(key_low, key_mat)
            + back_product(value_low, value_mat)
        ).astype(jnp.bfloat16),
        "tp",
    ).astype(jnp.float32)
    input_in, attn_gain_grad, attn_shift_grad = norm_back(
        normed_one_grad, unit_one, inverse_one, gain_one.astype(jnp.float32)
    )
    input_grad = hidden_grad + input_in
    partial_sums = (
        lax.psum_scatter(
            attn_gain_grad.astype(jnp.bfloat16), "fsdp", scatter_dimension=0, tiled=True
        ).astype(jnp.float32),
        lax.psum_scatter(
            attn_shift_grad.astype(jnp.bfloat16), "fsdp", scatter_dimension=0, tiled=True
        ).astype(jnp.float32),
        lax.psum_scatter(
            query_weight_grad.astype(jnp.bfloat16), "fsdp", scatter_dimension=0, tiled=True
        ).astype(jnp.float32),
        lax.psum_scatter(
            query_bias_grad.astype(jnp.bfloat16), "fsdp", scatter_dimension=1, tiled=True
        ).astype(jnp.float32),
        lax.psum_scatter(
            key_weight_grad.astype(jnp.bfloat16), "fsdp", scatter_dimension=0, tiled=True
        ).astype(jnp.float32),
        lax.psum_scatter(
            value_weight_grad.astype(jnp.bfloat16), "fsdp", scatter_dimension=0, tiled=True
        ).astype(jnp.float32),
        lax.psum_scatter(
            value_bias_grad.astype(jnp.bfloat16), "fsdp", scatter_dimension=1, tiled=True
        ).astype(jnp.float32),
        lax.psum_scatter(
            out_weight_grad.astype(jnp.bfloat16), "fsdp", scatter_dimension=1, tiled=True
        ).astype(jnp.float32),
        lax.psum_scatter(
            out_bias_grad.astype(jnp.bfloat16), "fsdp", scatter_dimension=0, tiled=True
        ).astype(jnp.float32),
        lax.psum_scatter(
            mlp_gain_grad.astype(jnp.bfloat16), "fsdp", scatter_dimension=0, tiled=True
        ).astype(jnp.float32),
        lax.psum_scatter(
            mlp_shift_grad.astype(jnp.bfloat16), "fsdp", scatter_dimension=0, tiled=True
        ).astype(jnp.float32),
        lax.psum_scatter(
            up_weight_grad.astype(jnp.bfloat16), "fsdp", scatter_dimension=0, tiled=True
        ).astype(jnp.float32),
        lax.psum_scatter(
            up_bias_grad.astype(jnp.bfloat16), "fsdp", scatter_dimension=1, tiled=True
        ).astype(jnp.float32),
        lax.psum_scatter(
            down_weight_grad.astype(jnp.bfloat16), "fsdp", scatter_dimension=1, tiled=True
        ).astype(jnp.float32),
        lax.psum_scatter(
            down_bias_grad.astype(jnp.bfloat16), "fsdp", scatter_dimension=0, tiled=True
        ).astype(jnp.float32),
    )
    shards = (
        lax.psum(partial_sums[0].astype(jnp.bfloat16), "ctx").astype(jnp.float32),
        lax.psum(partial_sums[1].astype(jnp.bfloat16), "ctx").astype(jnp.float32),
        lax.psum(partial_sums[2].astype(jnp.bfloat16), "ctx").astype(jnp.float32),
        lax.psum(partial_sums[3].astype(jnp.bfloat16), "ctx").astype(jnp.float32),
        lax.psum(partial_sums[4].astype(jnp.bfloat16), "ctx").astype(jnp.float32),
        lax.psum(partial_sums[5].astype(jnp.bfloat16), "ctx").astype(jnp.float32),
        lax.psum(partial_sums[6].astype(jnp.bfloat16), "ctx").astype(jnp.float32),
        lax.psum(partial_sums[7].astype(jnp.bfloat16), "ctx").astype(jnp.float32),
        lax.psum(partial_sums[8].astype(jnp.bfloat16), "ctx").astype(jnp.float32),
        lax.psum(partial_sums[9].astype(jnp.bfloat16), "ctx").astype(jnp.float32),
        lax.psum(partial_sums[10].astype(jnp.bfloat16), "ctx").astype(jnp.float32),
        lax.psum(partial_sums[11].astype(jnp.bfloat16), "ctx").astype(jnp.float32),
        lax.psum(partial_sums[12].astype(jnp.bfloat16), "ctx").astype(jnp.float32),
        lax.psum(partial_sums[13].astype(jnp.bfloat16), "ctx").astype(jnp.float32),
        lax.psum(partial_sums[14].astype(jnp.bfloat16), "ctx").astype(jnp.float32),
    )
    sent_output = layer_output.reshape(1, per_group, local_rows, width)
    sent_grad = input_grad.reshape(1, per_group, local_rows, width)
    back_output, back_grad = (
        lax.all_to_all(
            sent_output.astype(jnp.bfloat16), "fsdp", split_axis=2, concat_axis=0, tiled=True
        ).astype(sent_output.dtype),
        lax.all_to_all(
            sent_grad.astype(jnp.bfloat16), "fsdp", split_axis=2, concat_axis=0, tiled=True
        ).astype(sent_grad.dtype),
    )
    final_output = back_output.reshape(slot_count, block_rows, width)
    final_grad = back_grad.reshape(slot_count, block_rows, width)
    return (
        final_output,
        final_grad,
        shards[0],
        shards[1],
        shards[2],
        shards[3],
        shards[4],
        shards[5],
        shards[6],
        shards[7],
        shards[8],
        shards[9],
        shards[10],
        shards[11],
        shards[12],
        shards[13],
        shards[14],
        peak_all,
        query_clipped,
        key_clipped,
    )


def solution(mesh):
    return jax.shard_map(
        body,
        mesh=mesh,
        in_specs=(
            P(None, ("fsdp", "ctx"), None),
            P(None, ("fsdp", "ctx"), None),
            P(),
            P(),
            P("fsdp"),
            P("fsdp"),
            P("fsdp", "tp"),
            P("tp", "fsdp"),
            P("fsdp", "tp"),
            P("fsdp", "tp"),
            P("tp", "fsdp"),
            P("tp", "fsdp"),
            P("fsdp"),
            P("fsdp"),
            P("fsdp"),
            P("fsdp", "tp"),
            P("tp", "fsdp"),
            P("tp", "fsdp"),
            P("fsdp"),
            P(),
        ),
        out_specs=(
            P(None, ("fsdp", "ctx"), None),
            P(None, ("fsdp", "ctx"), None),
            P("fsdp"),
            P("fsdp"),
            P("fsdp", "tp"),
            P("tp", "fsdp"),
            P("fsdp", "tp"),
            P("fsdp", "tp"),
            P("tp", "fsdp"),
            P("tp", "fsdp"),
            P("fsdp"),
            P("fsdp"),
            P("fsdp"),
            P("fsdp", "tp"),
            P("tp", "fsdp"),
            P("tp", "fsdp"),
            P("fsdp"),
            P("tp"),
            P("fsdp", "tp"),
            P("fsdp", "tp"),
        ),
        check_vma=False,
    )
```

profile of v0, /device:TPU:0, one launch (start us, length us, event | category | flops | bytes accessed | tf_op | source)
XLA Modules:
  0.0 2476.1 jit_solution(5312229255279213892)
XLA Ops:
  27.0 66.8 %all-gather = bf16[4,1,512]{2,1,0:T(2,128)(2,1)S(1)} all-gather(bf16[1,1,512]{2,1,0:T(2,128)(2,1)S(1)} %reshape.514), channel_id=1, replica_groups=mesh['fsdp'=4,'ctx'=4,'tp'=2] {'fsdp'}, dimensions={0}, use_global_device_ids=true | all-gather | bytes 5120 | tf_op jit(solution)/shard_map/all_gather | solution.py:87
  93.8 8.2 all-gather.1
  126.2 31.2 %all-gather.19.cloned.1.call-done = bf16[2048,1024]{1,0:T(8,128)(2,1)} async-done(((bf16[512,1024]{1,0:T(8,128)(2,1)}), bf16[2048,1024]{1,0:T(8,128)(2,1)}) %all-gather.19.cloned.1.call-update) | async-done | bytes 4194320 | tf_op jit(solution)/shard_map/all_gather | solution.py:91
  163.8 8.2 all-gather.2
  173.2 38.8 %all-gather.17.cloned.1.call-done = bf16[2048,1024]{1,0:T(8,128)(2,1)} async-done(((bf16[512,1024]{1,0:T(8,128)(2,1)}), bf16[2048,1024]{1,0:T(8,128)(2,1)}) %all-gather.17.cloned.1.call-update) | async-done | bytes 4194320 | tf_op jit(solution)/shard_map/all_gather | solution.py:89
  217.5 77.3 %all-gather.25.cloned.1.call-done = bf16[2,1024,1024]{2,1,0:T(8,128)(2,1)} async-done(((bf16[2,256,1024]{2,1,0:T(8,128)(2,1)}), bf16[2,1024,1024]{2,1,0:T(8,128)(2,1)}) %all-gather.25.cloned.1.call-update) | async-done | bytes 4194320 | tf_op jit(solution)/shard_map/all_gather | solution.py:153
  294.8 81.3 %all-gather.21.cloned.1.call-done = bf16[2,1024,1024]{2,1,0:T(8,128)(2,1)} async-done(((bf16[2,256,1024]{2,1,0:T(8,128)(2,1)}), bf16[2,1024,1024]{2,1,0:T(8,128)(2,1)}) %all-gather.21.cloned.1.call-update) | async-done | bytes 4194320 | tf_op jit(solution)/shard_map/all_gather | solution.py:152
  376.1 72.1 %while.32 = (s32[]{:T(128)}, bf16[8,2,256,128]{3,2,1,0:T(8,128)(2,1)S(1)}, f32[8,2,256]{2,1,0:T(2,128)}, f32[8]{0:T(128)S(1)}, s32[8]{0:T(128)S(1)}, /*index=5*/...) while((s32[]{:T(128)}, ...), condition=%wide.region_6.7_spmd.clone.clone, body=%wide.region_2.6_spmd.clone.sunk.clone | while | flops 277349376 | bytes 8549587 | solution.py:182
  462.7 61.4 %all-gather.4 = bf16[4,1,512]{2,1,0:T(2,128)(2,1)S(1)} all-gather(bf16[1,1,512]{2,1,0:T(2,128)(2,1)S(1)} %reshape.522), channel_id=1, replica_groups=mesh['fsdp'=4,'ctx'=4,'tp'=2] {'fsdp'}, dimensions={0}, use_global_device_ids=true | all-gather | bytes 5120 | tf_op jit(solution)/shard_map/all_gather | solution.py:95
  558.7 92.0 %all-gather.29.cloned.1.call-done = bf16[2048,4096]{1,0:T(8,128)(2,1)} async-done(((bf16[512,4096]{1,0:T(8,128)(2,1)}), bf16[2048,4096]{1,0:T(8,128)(2,1)}) %all-gather.29.cloned.1.call-update) | async-done | bytes 16777232 | tf_op jit(solution)/shard_map/all_gather | solution.py:98
  650.6 34.4 %fusion.47 = (bf16[512,4096]{1,0:T(8,128)(2,1)}, f32[512,4096]{1,0:T(8,128)}) fusion(f32[4096]{0:T(1024)S(1)} %bitcast.242, bf16[2048,4096]{1,0:T(8,128)(2,1)} %all-gather.29.cloned.1.call-done, f32[512,2048]{1,0:T(8,128)} %copy-done.5, f32[2048]{0:T(1024)S(1)} %bitcast.246, f32[2048]{0:T(1024)S(1)} %bitcast.236, f32[512]{0:T(512)S(1)} %add_rsqrt_fusion.1, ...), kind=kOutput, calls=%fused_computation.65 | convolution fusion | flops 8733589504 | bytes 33591296 | tf_op jit(solution)/shard_map/dot_general | solution.py:32
  685.1 124.9 %all-gather.31.cloned.1.call-done = bf16[4096,2048]{1,0:T(8,128)(2,1)} async-done(((bf16[4096,512]{1,0:T(8,128)(2,1)}), bf16[4096,2048]{1,0:T(8,128)(2,1)}) %all-gather.31.cloned.1.call-update) | async-done | bytes 16777232 | tf_op jit(solution)/shard_map/all_gather | solution.py:100
  809.9 18.2 fusion.115
  828.1 15.1 fusion.72
  843.4 28.5 %all-reduce.17.cloned.1.call-done = f32[512,2048]{1,0:T(8,128)} async-done(((f32[512,2048]{1,0:T(8,128)}), f32[512,2048]{1,0:T(8,128)}) %all-reduce.17.cloned.1.call-update) | async-done | bytes 4194320 | tf_op jit(solution)/shard_map/psum | solution.py:208
  885.4 173.7 %while.33 = (s32[]{:T(128)}, f32[8,2,256,128]{3,2,1,0:T(8,128)}, f32[8,2,1024,128]{2,3,0,1:T(8,128)}, f32[8,2,1024,128]{2,3,0,1:T(8,128)}, s32[8]{0:T(128)S(1)},...) while((s32[]{:T(128)}, f32[8,2,256,128]{3,2,1,0:T(8,128)}, ...), condition=%wide.region_16.17_spmd.clone.clone, body=%wide.region_14.16_spmd.clone.sunk.clone | while | flops 677182976 | bytes 33046268 | solution.py:253
  1078.5 126.4 %reduce-scatter.20.cloned.1.call-done = f32[2,256,1024]{1,2,0:T(8,128)} async-done(((f32[2,1024,1024]{1,2,0:T(8,128)}), f32[2,256,1024]{1,2,0:T(8,128)}) %reduce-scatter.20.cloned.1.call-update) | async-done | bytes 2097168 | tf_op jit(solution)/shard_map/reduce_scatter | solution.py:261
  1214.4 138.5 %reduce-scatter.18.cloned.1.call-done = f32[2,256,1024]{1,2,0:T(8,128)} async-done(((f32[2,1024,1024]{1,2,0:T(8,128)}), f32[2,256,1024]{1,2,0:T(8,128)}) %reduce-scatter.18.cloned.1.call-update) | async-done | bytes 2097168 | tf_op jit(solution)/shard_map/reduce_scatter | solution.py:260
  1362.0 16.2 convolution_convert_fusion.1
  1379.8 14.8 convolution_convert_fusion
  1394.9 14.8 convolution_convert_fusion.6
  1423.8 41.3 %reduce-scatter.28.cloned.1.call-done = bf16[1024,512]{1,0:T(8,128)(2,1)} async-done(((bf16[1024,2048]{1,0:T(8,128)(2,1)}), bf16[1024,512]{1,0:T(8,128)(2,1)}) %reduce-scatter.28.cloned.1.call-update) | async-done | bytes 1048592 | tf_op jit(solution)/shard_map/reduce_scatter | solution.py:307
  1465.0 56.1 %reduce-scatter.26.cloned.1.call-done = bf16[512,1024]{1,0:T(8,128)(2,1)} async-done(((bf16[2048,1024]{1,0:T(8,128)(2,1)}), bf16[512,1024]{1,0:T(8,128)(2,1)}) %reduce-scatter.26.cloned.1.call-update) | async-done | bytes 1048592 | tf_op jit(solution)/shard_map/reduce_scatter | solution.py:301
  1521.2 56.4 %reduce-scatter.24.cloned.1.call-done = bf16[512,1024]{1,0:T(8,128)(2,1)} async-done(((bf16[2048,1024]{1,0:T(8,128)(2,1)}), bf16[512,1024]{1,0:T(8,128)(2,1)}) %reduce-scatter.24.cloned.1.call-update) | async-done | bytes 1048592 | tf_op jit(solution)/shard_map/reduce_scatter | solution.py:298
  1577.6 156.8 %reduce-scatter.30.cloned.1.call-done = bf16[512,4096]{1,0:T(8,128)(2,1)} async-done(((bf16[2048,4096]{1,0:T(8,128)(2,1)}), bf16[512,4096]{1,0:T(8,128)(2,1)}) %reduce-scatter.30.cloned.1.call-update) | async-done | bytes 4194320 | tf_op jit(solution)/shard_map/reduce_scatter | solution.py:319
  1734.3 156.7 %reduce-scatter.32.cloned.1.call-done = bf16[4096,512]{1,0:T(8,128)(2,1)} async-done(((bf16[4096,2048]{1,0:T(8,128)(2,1)}), bf16[4096,512]{1,0:T(8,128)(2,1)}) %reduce-scatter.32.cloned.1.call-update) | async-done | bytes 4194320 | tf_op jit(solution)/shard_map/reduce_scatter | solution.py:325
  1891.1 32.2 %all-reduce.21.cloned.1.call-done = (bf16[512,2048]{1,0:T(8,128)(2,1)}, bf16[512,2048]{1,0:T(8,128)(2,1)}) async-done(((bf16[512,2048]{1,0:T(8,128)(2,1)}, bf16[512,2048]{1,0:T(8,128)(2,1)}), (bf16[512,2048]{1,0:T(8,128)(2,1)}, bf16[512,2048]{1,0:T(8,128)(2,1)})) %all-reduce.21.cloned.1.call-update) | async-done | bytes 4194320 | tf_op jit(solution)/shard_map/psum | solution.py:192
  1939.5 30.1 %all-gather.7 = bf16[4,1,512]{2,1,0:T(2,128)(2,1)S(1)} all-gather(bf16[1,1,512]{2,1,0:T(2,128)(2,1)S(1)} %reshape.528), channel_id=1, replica_groups=mesh['fsdp'=4,'ctx'=4,'tp'=2] {'fsdp'}, dimensions={0}, use_global_device_ids=true | all-gather | bytes 5120 | tf_op jit(solution)/shard_map/all_gather | solution.py:101
  1985.7 43.0 %pmax.7 = f32[8]{0:T(128)S(1)} all-reduce(f32[8]{0:T(128)S(1)} %copy-done.57), channel_id=1, replica_groups=mesh['fsdp'=4,'ctx'=4,'tp'=2] {'fsdp','ctx'}, use_global_device_ids=true, to_apply=%region_61.62 | all-reduce | flops 8 | bytes 64 | tf_op jit(solution)/shard_map/pmax | solution.py:194
  2034.9 14.0 all-reduce.8
  2049.3 18.5 all-reduce.6
  2090.0 361.4 %all-reduce.19.cloned.1.call-done = (bf16[512,1024]{1,0:T(8,128)(2,1)}, bf16[512,1024]{1,0:T(8,128)(2,1)}, bf16[512,1024]{1,0:T(8,128)(2,1)}, bf16[1024,512]{1,0...) async-done(((bf16[512,1024]{1,0:T(8,128)(2,1)}, bf16[512,1024]{1,0:T(8,128)(2,1)}, bf16[512,1024]{1,0:T(8,128)(2,1)}, bf16[1024,512]{1,0:T(8,128)(2,1)}, ...) | async-done | bytes 12582928 | tf_op jit(solution)/shard_map/psum | solution.py:335
  (452 shorter events, 469.6 us)
Async XLA Ops:
  7.2 113.4 %all-gather.23.cloned.1.call-start = ((), (), s32[]{:S(2)}) async-start(), calls=%async_computation.18 | async-start | bytes 5242880 | tf_op jit(solution)/shard_map/all_gather | solution.py:92
  7.9 149.4 %all-gather.19.cloned.1.call-start = ((), (), s32[]{:S(2)}) async-start(), calls=%async_computation.16 | async-start | bytes 5242880 | tf_op jit(solution)/shard_map/all_gather | solution.py:91
  8.7 203.3 %all-gather.17.cloned.1.call-start = ((), (), s32[]{:S(2)}) async-start(), calls=%async_computation.15 | async-start | bytes 5242880 | tf_op jit(solution)/shard_map/all_gather | solution.py:89
  21.4 72.4 %copy-start.45 = (bf16[512]{0:T(512)(128)(2,1)S(1)}, bf16[512]{0:T(512)(128)(2,1)}, u32[]{:S(2)}) copy-start(bf16[512]{0:T(512)(128)(2,1)} %param.29) | copy-start | bytes 3076
  21.4 80.7 %copy-start.41 = (bf16[8,32]{1,0:T(8,128)(2,1)S(1)}, bf16[8,32]{1,0:T(8,128)(2,1)}, u32[]{:S(2)}) copy-start(bf16[8,32]{1,0:T(8,128)(2,1)} %param.34) | copy-start | bytes 1540
  21.4 87.7 %all-to-all-start = ((f32[4,2,64,2048]{3,2,1,0:T(8,128)}), f32[4,2,64,2048]{3,2,1,0:T(8,128)}, u32[]{:S(2)}, u32[]{:S(2)}) async-start(f32[4,2,64,2048]{3,2,1,0:T(8,128)} %broadcast_select_fusion), calls=%async_computation | async-start | bytes 8388608 | tf_op jit(solution)/shard_map/all_to_all | solution.py:78
  27.0 267.7 %all-gather.25.cloned.1.call-start = ((), (), s32[]{:S(2)}) async-start(), calls=%async_computation.19 | async-start | bytes 5242880 | tf_op jit(solution)/shard_map/all_gather | solution.py:153
  126.1 249.9 %all-gather.21.cloned.1.call-start = ((), (), s32[]{:S(2)}) async-start(), calls=%async_computation.17 | async-start | bytes 5242880 | tf_op jit(solution)/shard_map/all_gather | solution.py:152
  162.9 286.0 %all-gather.27.cloned.1.call-start = ((), (), s32[]{:S(2)}) async-start(), calls=%async_computation.20 | async-start | bytes 5242880 | tf_op jit(solution)/shard_map/all_gather | solution.py:94
  163.5 387.9 %all-reduce.15.cloned.1.call-start = ((), (), s32[]{:S(2)}) async-start(), calls=%async_computation.21 | async-start | bytes 8388608 | tf_op jit(solution)/shard_map/psum | solution.py:184
  455.9 194.8 %all-gather.29.cloned.1.call-start = ((), (), s32[]{:S(2)}) async-start(), calls=%async_computation.22 | async-start | bytes 20971520 | tf_op jit(solution)/shard_map/all_gather | solution.py:98
  456.6 353.3 %all-gather.31.cloned.1.call-start = ((), (), s32[]{:S(2)}) async-start(), calls=%async_computation.23 | async-start | bytes 20971520 | tf_op jit(solution)/shard_map/all_gather | solution.py:100
  457.4 74.0 %copy-start.43 = (bf16[2,512]{1,0:T(2,128)(2,1)S(1)}, bf16[2,512]{1,0:T(2,128)(2,1)}, u32[]{:S(2)}) copy-start(bf16[2,512]{1,0:T(2,128)(2,1)} %param.40) | copy-start | bytes 6148
  457.4 82.0 %copy-start.48 = (bf16[512]{0:T(512)(128)(2,1)S(1)}, bf16[512]{0:T(512)(128)(2,1)}, u32[]{:S(2)}) copy-start(bf16[512]{0:T(512)(128)(2,1)} %param.38) | copy-start | bytes 3076
  457.4 89.2 %all-to-all-start.2 = ((f32[4,2,64,2048]{3,2,1,0:T(8,128)}), f32[4,2,64,2048]{3,2,1,0:T(8,128)}, u32[]{:S(2)}, u32[]{:S(2)}) async-start(f32[4,2,64,2048]{3,2,1,0:T(8,128)} %bitcast.209), calls=%async_computation.2 | async-start | bytes 8388608 | tf_op jit(solution)/shard_map/all_to_all | solution.py:79
  462.7 409.2 %all-reduce.17.cloned.1.call-start = ((), (), s32[]{:S(2)}) async-start(), calls=%async_computation.24 | async-start | bytes 8388608 | tf_op jit(solution)/shard_map/psum | solution.py:208
  551.3 258.6 %copy-start.13 = (bf16[512,2048]{1,0:T(8,128)(2,1)}, bf16[512,2048]{1,0:T(8,128)(2,1)S(1)}, u32[]{:S(2)}) copy-start(bf16[512,2048]{1,0:T(8,128)(2,1)S(1)} %bitcast_convert_fusion) | copy-start | bytes 6291460
  843.3 361.6 %reduce-scatter.20.cloned.1.call-start = ((), (), s32[]{:S(2)}) async-start(), calls=%async_computation.26 | async-start | bytes 10485760 | tf_op jit(solution)/shard_map/reduce_scatter | solution.py:261
  1059.0 293.8 %reduce-scatter.18.cloned.1.call-start = ((), (), s32[]{:S(2)}) async-start(), calls=%async_computation.25 | async-start | bytes 10485760 | tf_op jit(solution)/shard_map/reduce_scatter | solution.py:260
  1059.6 364.2 %reduce-scatter.22.cloned.1.call-start = ((), (), s32[]{:S(2)}) async-start(), calls=%async_computation.27 | async-start | bytes 5242880 | tf_op jit(solution)/shard_map/reduce_scatter | solution.py:292
  1070.6 394.4 %reduce-scatter.28.cloned.1.call-start = ((), (), s32[]{:S(2)}) async-start(), calls=%async_computation.30 | async-start | bytes 5242880 | tf_op jit(solution)/shard_map/reduce_scatter | solution.py:307
  1078.4 442.8 %reduce-scatter.26.cloned.1.call-start = ((), (), s32[]{:S(2)}) async-start(), calls=%async_computation.29 | async-start | bytes 5242880 | tf_op jit(solution)/shard_map/reduce_scatter | solution.py:301
  1214.3 363.2 %reduce-scatter.24.cloned.1.call-start = ((), (), s32[]{:S(2)}) async-start(), calls=%async_computation.28 | async-start | bytes 5242880 | tf_op jit(solution)/shard_map/reduce_scatter | solution.py:298
  1361.5 372.8 %reduce-scatter.30.cloned.1.call-start = ((), (), s32[]{:S(2)}) async-start(), calls=%async_computation.31 | async-start | bytes 20971520 | tf_op jit(solution)/shard_map/reduce_scatter | solution.py:319
  1378.3 512.8 %reduce-scatter.32.cloned.1.call-start = ((), (), s32[]{:S(2)}) async-start(), calls=%async_computation.32 | async-start | bytes 20971520 | tf_op jit(solution)/shard_map/reduce_scatter | solution.py:325
  1394.7 528.6 %all-reduce.21.cloned.1.call-start = ((), (), s32[]{:S(2)}) async-start(), calls=%async_computation.37 | async-start | bytes 8388608 | tf_op jit(solution)/shard_map/psum | solution.py:192
  1418.4 613.5 %reduce-scatter.38.cloned.1.call-start = ((), (), s32[]{:S(2)}) async-start(), calls=%async_computation.35 | async-start | bytes 655360
  1420.2 612.7 %reduce-scatter.34.cloned.1.call-start = ((), (), s32[]{:S(2)}) async-start(), calls=%async_computation.33 | async-start | bytes 40960
  1422.7 611.0 %reduce-scatter.36.cloned.1.call-start = ((), (), s32[]{:S(2)}) async-start(), calls=%async_computation.34 | async-start | bytes 40960
  1423.5 1027.9 %all-reduce.19.cloned.1.call-start = ((), (), s32[]{:S(2)}) async-start(), calls=%async_computation.36 | async-start | bytes 25165824 | tf_op jit(solution)/shard_map/psum | solution.py:335
  1935.0 41.8 %all-to-all-start.3 = ((bf16[1,2,256,2048]{3,1,0,2:T(2,128)(2,1)}), bf16[1,2,256,2048]{3,1,0,2:T(2,128)(2,1)}, u32[]{:S(2)}, u32[]{:S(2)}) async-start(bf16[1,2,256,2048]{3,1,0,2:T(2,128)(2,1)} %copy.105), calls=%async_computation.5 | async-start | bytes 4194304 | tf_op jit(solution)/shard_map/all_to_all | solution.py:355
  1976.8 104.8 %all-to-all-start.1 = ((bf16[1,2,256,2048]{3,1,0,2:T(2,128)(2,1)}), bf16[1,2,256,2048]{3,1,0,2:T(2,128)(2,1)}, u32[]{:S(2)}, u32[]{:S(2)}) async-start(bf16[1,2,256,2048]{3,1,0,2:T(2,128)(2,1)} %copy.97), calls=%async_computation.1 | async-start | bytes 4194304 | tf_op jit(solution)/shard_map/all_to_all | solution.py:352
  (60 other events, 669.7 us)
Sparse Core Ops, SparseCore 0:
  9.9 92.8 all-gather.22
  104.6 52.7 all-gather.18
  159.2 52.7 all-gather.16
  214.0 80.7 all-gather.24
  296.7 79.2 all-gather.20
  377.8 51.0 all-gather.26
  456.0 26.8 all-reduce.14
  484.9 165.7 all-gather.28
  652.6 157.2 all-gather.30
  843.4 28.4 all-reduce.16
  1059.2 145.6 reduce-scatter.19
  1207.6 145.1 reduce-scatter.17
  1355.8 53.4 reduce-scatter.21
  1412.4 52.6 reduce-scatter.27
  1468.4 52.6 reduce-scatter.25
  1524.8 52.6 reduce-scatter.23
  1580.5 153.8 reduce-scatter.29
  1737.3 153.7 reduce-scatter.31
  1894.7 28.5 all-reduce.20
  1926.8 31.6 reduce-scatter.37
  1961.3 23.0 reduce-scatter.33
  1987.3 30.8 reduce-scatter.35
  2021.4 429.8 all-reduce.18
where the time goes:
time: 2490 us; the launch traced here: 2480 us
  waiting for transfers between devices  1600 us (64%)
  matrix products  303 us (12%)
  blocking collectives  279 us (11%)
  other arithmetic  115 us (5%)
  local copies, waits for them, and re-layouts  109 us (4%)
  loops' own time  26.3 us (1%)
    psum x1, waiting for transfers between devices, body(): lax.psum(partial_sums[2].astype(jnp.bfloat16), 'ctx').astype(jnp.float32)  361 us
    reduce_scatter x1, waiting for transfers between devices, body(): lax.psum_scatter(up_weight_grad.astype(jnp.bfloat16), 'fsdp', scatter_dim...  157 us
    reduce_scatter x1, waiting for transfers between devices, body(): lax.psum_scatter(down_weight_grad.astype(jnp.bfloat16), 'fsdp', scatter_d...  157 us
    reduce_scatter x1, waiting for transfers between devices, body(): lax.psum_scatter(key_whole, 'ctx', scatter_dimension=1, tiled=True)  138 us
    reduce_scatter x1, waiting for transfers between devices, body(): lax.psum_scatter(value_whole, 'ctx', scatter_dimension=1, tiled=True)  126 us
    all_gather x1, waiting for transfers between devices, body(): lax.all_gather(down_weight, 'fsdp', axis=1, tiled=True)  125 us
    all_gather x1, waiting for transfers between devices, body(): lax.all_gather(up_weight, 'fsdp', axis=0, tiled=True)  92 us
    all_gather x1, waiting for transfers between devices, body(): lax.all_gather(keys_mine, 'ctx', axis=1, tiled=True)  81.3 us
  transfers between devices with their start and end apart: 27, of which 16 were waited for; matrix products, arithmetic and copies ran while one was open for 12% of the time, Pallas kernels for 0%

commit v1 on v0

--- a/solution.py
+++ b/solution.py
@@ -1,8 +1,11 @@
+import functools
 import math
 
 import jax
 import jax.numpy as jnp
 from jax import lax
+from jax.experimental import pallas as pl
+from jax.experimental.pallas import tpu as pltpu
 from jax.sharding import PartitionSpec as P
 
 EPS = 1e-05
@@ -28,6 +31,12 @@
     return (inverse * inner, jnp.sum(upstream * normed, 0), jnp.sum(upstream, 0))
 
 
+def pick_slots(rows, dealing, first, count):
+    return jnp.concatenate(
+        [lax.dynamic_slice_in_dim(rows, dealing[first + j], 1, 0) for j in range(count)], 0
+    )
+
+
 def matmul(left, right):
     return jnp.dot(left, right, preferred_element_type=jnp.float32)
 
@@ -40,7 +49,7 @@
     return jnp.einsum("te,de->td", left, right, preferred_element_type=jnp.float32)
 
 
-def body(
+def gathered_body(
     layer_input,
     cotangent,
     seq_lengths,
@@ -70,7 +79,7 @@
     per_group = slot_count // shard_count
     local_rows = shard_count * block_rows
     tokens = per_group * local_rows
-    dealt_input = jnp.take(layer_input, dealing, axis=0).reshape(
+    dealt_input = pick_slots(layer_input, dealing, 0, slot_count).reshape(
         shard_count, per_group, block_rows, width
     )
     dealt_grad = cotangent.reshape(shard_count, per_group, block_rows, width)
@@ -382,9 +391,436 @@
     )
 
 
+def attention_probs(query_block, key_rows, block, length):
+    rows, cols = query_block.shape[0], key_rows.shape[0]
+    scores = lax.dot_general(
+        query_block, key_rows, (((1,), (1,)), ((), ())), preferred_element_type=jnp.float32
+    ) * (1.0 / math.sqrt(query_block.shape[1]))
+    row_pos = block * rows + lax.broadcasted_iota(jnp.int32, (rows, cols), 0)
+    col_pos = lax.broadcasted_iota(jnp.int32, (rows, cols), 1)
+    scores = jnp.where((col_pos <= row_pos) & (col_pos < length), scores, NEG)
+    top = jnp.max(scores, -1, keepdims=True)
+    terms = jnp.exp(scores - top)
+    return terms / jnp.sum(terms, -1, keepdims=True), top
+
+
+def attention_forward_kernel(ranks, info, q_ref, k_ref, v_ref, out_ref, peak_ref, keys, values):
+    rows = keys.shape[0] // ranks
+    length = info[ranks]
+    for block in range(ranks):
+        at = pl.ds(pl.multiple_of(info[block], rows), rows)
+        keys[pl.ds(block * rows, rows), :] = k_ref[at, :]
+        values[pl.ds(block * rows, rows), :] = v_ref[at, :]
+    peak = jnp.full((1, 1), NEG, jnp.float32)
+    for block in range(ranks):
+        at = pl.ds(pl.multiple_of(info[block], rows), rows)
+        extent = (block + 1) * rows
+        probs, top = attention_probs(q_ref[at, :], keys[pl.ds(0, extent), :], block, length)
+        out_ref[at, :] = jnp.dot(
+            probs.astype(jnp.bfloat16),
+            values[pl.ds(0, extent), :],
+            preferred_element_type=jnp.float32,
+        ).astype(out_ref.dtype)
+        live = block * rows + lax.broadcasted_iota(jnp.int32, top.shape, 0) < length
+        peak = jnp.maximum(peak, jnp.max(jnp.where(live, top, NEG), 0, keepdims=True))
+    peak_ref[...] = jnp.broadcast_to(peak[None], peak_ref.shape)
+
+
+def attention_forward(info, qkv, head_size):
+    tokens, features = qkv.shape[0], qkv.shape[1] // 3
+    heads, ranks = features // head_size, info.shape[0] - 1
+
+    def part(k):
+        return pl.BlockSpec((tokens, head_size), lambda h, info: (0, k * heads + h))
+
+    attended, peaks = pl.pallas_call(
+        functools.partial(attention_forward_kernel, ranks),
+        out_shape=(
+            jax.ShapeDtypeStruct((tokens, features), jnp.bfloat16),
+            jax.ShapeDtypeStruct((heads, 8, 128), jnp.float32),
+        ),
+        grid_spec=pltpu.PrefetchScalarGridSpec(
+            num_scalar_prefetch=1,
+            grid=(heads,),
+            in_specs=[part(0), part(1), part(2)],
+            out_specs=(
+                pl.BlockSpec((tokens, head_size), lambda h, info: (0, h)),
+                pl.BlockSpec((1, 8, 128), lambda h, info: (h, 0, 0)),
+            ),
+            scratch_shapes=[pltpu.VMEM((tokens, head_size), jnp.bfloat16)] * 2,
+        ),
+        compiler_params=pltpu.CompilerParams(vmem_limit_bytes=40 << 20),
+        cost_estimate=pl.CostEstimate(
+            flops=4 * tokens * tokens * features, bytes_accessed=8 * tokens * features, transcendentals=0
+        ),
+    )(info, qkv, qkv, qkv)
+    return attended, peaks[:, 0, 0]
+
+
+def attention_backward_kernel(
+    ranks, heads, info, q_ref, k_ref, v_ref, g_ref, out_ref, bias_ref, keys, values, key_sum, value_sum
+):
+    tokens, size = keys.shape
+    rows = tokens // ranks
+    scale = 1.0 / math.sqrt(size)
+    head = pl.program_id(0)
+    length = info[ranks]
+
+    def lanes(k):
+        return pl.ds(pl.multiple_of((k * heads + head) * size, size), size)
+
+    for block in range(ranks):
+        at = pl.ds(pl.multiple_of(info[block], rows), rows)
+        keys[pl.ds(block * rows, rows), :] = k_ref[at, :]
+        values[pl.ds(block * rows, rows), :] = v_ref[at, :]
+    key_sum[...] = jnp.zeros_like(key_sum)
+    value_sum[...] = jnp.zeros_like(value_sum)
+    query_bias = jnp.zeros((1, size), jnp.float32)
+    for block in range(ranks):
+        at = pl.ds(pl.multiple_of(info[block], rows), rows)
+        extent = (block + 1) * rows
+        part = pl.ds(0, extent)
+        queries, grads = q_ref[at, :], g_ref[at, :]
+        probs, _ = attention_probs(queries, keys[part, :], block, length)
+        prob_grad = lax.dot_general(
+            grads, values[part, :], (((1,), (1,)), ((), ())), preferred_element_type=jnp.float32
+        )
+        inner = jnp.sum(probs * prob_grad, -1, keepdims=True)
+        score_grad = (probs * (prob_grad - inner)).astype(jnp.bfloat16)
+        query_grad = (
+            jnp.dot(score_grad, keys[part, :], preferred_element_type=jnp.float32) * scale
+        )
+        query_bias += jnp.sum(query_grad, 0, keepdims=True)
+        out_ref[at, lanes(0)] = query_grad.astype(out_ref.dtype)
+        key_sum[part, :] += lax.dot_general(
+            score_grad, queries, (((0,), (0,)), ((), ())), preferred_element_type=jnp.float32
+        )
+        value_sum[part, :] += lax.dot_general(
+            probs.astype(jnp.bfloat16), grads, (((0,), (0,)), ((), ())), preferred_element_type=jnp.float32
+        )
+    for block in range(ranks):
+        at = pl.ds(pl.multiple_of(info[block], rows), rows)
+        out_ref[at, lanes(1)] = (key_sum[pl.ds(block * rows, rows), :] * scale).astype(out_ref.dtype)
+        out_ref[at, lanes(2)] = value_sum[pl.ds(block * rows, rows), :].astype(out_ref.dtype)
+    bias_ref[0, pl.ds(0, 1), :] = query_bias
+    bias_ref[0, pl.ds(1, 1), :] = jnp.sum(value_sum[...], 0, keepdims=True)
+
+
+def attention_backward(info, qkv, grads, head_size):
+    tokens, features = grads.shape
+    heads, ranks = features // head_size, info.shape[0] - 1
+
+    def part(k):
+        return pl.BlockSpec((tokens, head_size), lambda h, info: (0, k * heads + h))
+
+    return pl.pallas_call(
+        functools.partial(attention_backward_kernel, ranks, heads),
+        out_shape=(
+            jax.ShapeDtypeStruct((tokens, 3 * features), jnp.bfloat16),
+            jax.ShapeDtypeStruct((heads, 8, head_size), jnp.float32),
+        ),
+        grid_spec=pltpu.PrefetchScalarGridSpec(
+            num_scalar_prefetch=1,
+            grid=(heads,),
+            in_specs=[part(0), part(1), part(2), part(0)],
+            out_specs=(
+                pl.BlockSpec((tokens, 3 * features), lambda h, info: (0, 0)),
+                pl.BlockSpec((1, 8, head_size), lambda h, info: (h, 0, 0)),
+            ),
+            scratch_shapes=[pltpu.VMEM((tokens, head_size), jnp.bfloat16)] * 2
+            + [pltpu.VMEM((tokens, head_size), jnp.float32)] * 2,
+        ),
+        compiler_params=pltpu.CompilerParams(vmem_limit_bytes=48 << 20),
+        cost_estimate=pl.CostEstimate(
+            flops=10 * tokens * tokens * features, bytes_accessed=14 * tokens * features, transcendentals=0
+        ),
+    )(info, qkv, qkv, qkv, grads)
+
+
+def split_body(
+    layer_input,
+    cotangent,
+    seq_lengths,
+    dealing,
+    attn_gain,
+    attn_shift,
+    query_weight,
+    query_bias,
+    key_weight,
+    value_weight,
+    value_bias,
+    out_weight,
+    out_bias,
+    mlp_gain,
+    mlp_shift,
+    up_weight,
+    up_bias,
+    down_weight,
+    down_bias,
+    clip_level,
+):
+    f32, bf16 = jnp.float32, jnp.bfloat16
+    f = lax.axis_index("fsdp")
+    z = lax.axis_index("ctx")
+    t = lax.axis_index("tp")
+    y, x = f // 2, f % 2
+    depth = lax.axis_size("ctx")
+    slots, block_rows, width = layer_input.shape
+    local_heads = query_bias.shape[0] // 2
+    head_size = 4 * query_bias.shape[1]
+    features = local_heads * head_size
+    hidden_units = up_weight.shape[1] // 2
+    strip = query_weight.shape[0]
+    own_rows = depth * block_rows
+
+    over_x = [(0, 1), (1, 0), (2, 3), (3, 2)]
+    over_y = [(0, 2), (2, 0), (1, 3), (3, 1)]
+    x_core = [(0, 0), (1, 2), (2, 1), (3, 3), (4, 4), (5, 6), (6, 5), (7, 7)]
+
+    def across_x(v):
+        return lax.ppermute(v, "fsdp", over_x)
+
+    def across_y(v):
+        return lax.ppermute(v, "fsdp", over_y)
+
+    def across_core(v):
+        return lax.ppermute(v, "tp", [(0, 1), (1, 0)])
+
+    def half(v, which, axis):
+        size = v.shape[axis] // 2
+        return lax.dynamic_slice_in_dim(v, which * size, size, axis)
+
+    def deal_rows(part):
+        part = lax.ppermute(part, ("fsdp", "tp"), x_core)
+        part = lax.all_to_all(part, "ctx", split_axis=0, concat_axis=0, tiled=True)
+        return part.reshape(own_rows, part.shape[-1])
+
+    def return_rows(rows):
+        part = rows.reshape(depth, block_rows, rows.shape[-1])
+        part = lax.all_to_all(part, "ctx", split_axis=0, concat_axis=0, tiled=True)
+        part = lax.ppermute(part, ("fsdp", "tp"), x_core)
+        other = across_core(part)
+        both = jnp.where(t == 0, jnp.stack([part, other]), jnp.stack([other, part]))
+        return both.reshape(slots, block_rows, rows.shape[-1]).astype(f32)
+
+    def gather_rows(own):
+        peer = across_core(own)
+        far = across_y(own)
+        far_peer = across_core(far)
+        return jnp.concatenate([own, peer], 0), jnp.concatenate([far, far_peer], 0)
+
+    def scatter_rows(near, far):
+        far_mine = far[:own_rows] + across_core(far[own_rows:].astype(bf16)).astype(f32)
+        arrived = across_y(far_mine.astype(bf16)).astype(f32)
+        return near[:own_rows] + across_core(near[own_rows:].astype(bf16)).astype(f32) + arrived
+
+    def gather_weight(shard, column_split):
+        cut = 1 if column_split else 0
+        own, sent = half(shard, y, cut), half(shard, 1 - y, cut)
+        far = across_y(sent)
+        own_x, far_x = across_x(own), across_x(far)
+        axis = 1 - cut
+        shape = list(own.shape)
+        shape[axis] *= 4
+        whole = jnp.zeros(shape, shard.dtype)
+        for piece, home in ((own, f), (own_x, 2 * y + 1 - x), (far, 2 * (1 - y) + x), (far_x, 2 * (1 - y) + 1 - x)):
+            whole = lax.dynamic_update_slice_in_dim(whole, piece, home * strip, axis)
+        return whole
+
+    def z_sum(v):
+        first = lax.ppermute(v, "ctx", [(0, 1), (3, 2)])
+        pair = lax.optimization_barrier((v.astype(f32) + first.astype(f32)).astype(bf16))
+        second = lax.ppermute(pair, "ctx", [(1, 2), (2, 1)])
+        total = lax.optimization_barrier((pair.astype(f32) + second.astype(f32)).astype(bf16))
+        back = lax.ppermute(total, "ctx", [(1, 0), (2, 3)])
+        return jnp.where((z == 1) | (z == 2), total, back)
+
+    def strip_of(v, home):
+        return lax.dynamic_slice_in_dim(v, home * strip, strip, 1)
+
+    def reduce_weight(product, cut, join):
+        near_send = product(2 * y + 1 - x).astype(bf16)
+        far_send = product(2 * (1 - y) + 1 - x).astype(bf16)
+        near_got, far_got = across_x(near_send), across_x(far_send)
+        near = (product(f) + near_got.astype(f32)).astype(bf16)
+        far = (product(2 * (1 - y) + x) + far_got.astype(f32)).astype(bf16)
+        other = across_y(far)
+        mine, other = z_sum(near), z_sum(other)
+        return join(mine, other)
+
+    def join_on(axis):
+        def join(mine, other):
+            return jnp.where(
+                y == 0,
+                jnp.concatenate([mine, other], axis),
+                jnp.concatenate([other, mine], axis),
+            ).astype(f32)
+
+        return join
+
+    slot = x * depth + z
+    length = seq_lengths[dealing[slot]]
+    own_rank = 2 * y + t
+    near_rank = 2 * y + 1 - t
+    far_rank = 2 * (1 - y) + t
+    places = jnp.zeros((4,), jnp.int32)
+    for k, rank in enumerate((own_rank, near_rank, far_rank, 2 * (1 - y) + 1 - t)):
+        places = places.at[rank].set(k * own_rows)
+    info = jnp.concatenate([places, length[None]])
+
+    small = jnp.stack([attn_gain, attn_shift, out_bias, mlp_gain, mlp_shift, down_bias])
+    small = lax.all_gather(small, "fsdp", axis=1, tiled=True).astype(f32)
+    gain_one, shift_one, out_vec, gain_two, shift_two, down_vec = [small[k] for k in range(6)]
+    vectors = jnp.concatenate([query_bias, value_bias, up_bias.reshape(-1, query_bias.shape[1])], 0)
+    vectors = lax.all_gather(vectors, "fsdp", axis=0, tiled=False)
+    nb = query_bias.shape[0]
+    query_vec = half(vectors[:, :nb].transpose(1, 0, 2).reshape(-1), y, 0).astype(f32)
+    value_vec = half(vectors[:, nb : 2 * nb].transpose(1, 0, 2).reshape(-1), y, 0).astype(f32)
+    up_vec = half(
+        vectors[:, 2 * nb :].reshape(4, up_bias.shape[0], -1).transpose(1, 0, 2).reshape(-1), y, 0
+    ).astype(f32)
+
+    arrived = pick_slots(layer_input, dealing, t * depth, depth)
+    cot_part = lax.dynamic_slice_in_dim(cotangent, t * depth, depth, 0)
+    down_bias_part = jnp.sum(cot_part, (0, 1))
+    act_part = normalize(arrived, gain_one, shift_one)[0].astype(bf16)
+    act_own = deal_rows(act_part)
+    act_near, act_far = gather_rows(act_own)
+    act_one = jnp.concatenate([act_near, act_far], 0)
+    qkv_shard = jnp.concatenate([query_weight, key_weight, value_weight], 1)
+    qkv_shard = qkv_shard.reshape(strip, 3, 2, features).transpose(0, 2, 1, 3).reshape(strip, 6 * features)
+    qkv_mat = gather_weight(qkv_shard, True)
+    out_mat = gather_weight(out_weight, False)
+    up_mat = gather_weight(up_weight, True)
+    down_mat = gather_weight(down_weight, False)
+    resid = deal_rows(arrived)
+    cot_own = deal_rows(cot_part.astype(bf16))
+    cot_low = jnp.concatenate(gather_rows(cot_own), 0)
+
+    qkv_vec = jnp.concatenate([query_vec, jnp.zeros_like(query_vec), value_vec])
+    qkv = jnp.concatenate(
+        [(matmul(rows, qkv_mat) + qkv_vec).astype(bf16) for rows in (act_near, act_far)], 0
+    )
+    attended, peaks = attention_forward(info, qkv, head_size)
+    chip_rows = 2 * own_rows
+    attn_far = matmul(attended[chip_rows:], out_mat)
+    attn_near = matmul(attended[:chip_rows], out_mat)
+    hidden = resid + scatter_rows(attn_near, attn_far) + out_vec
+    normed_b, unit_two, inverse_two = normalize(hidden, gain_two, shift_two)
+    act_two = jnp.concatenate(gather_rows(normed_b.astype(bf16)), 0)
+
+    pre = matmul(act_two, up_mat) + up_vec
+    cdf = 0.5 * (1.0 + lax.erf(pre * INV_ROOT_TWO))
+    gelu_low = (pre * cdf).astype(bf16)
+    slope = cdf + pre * (jnp.exp(-0.5 * pre * pre) * INV_ROOT_TWO_PI)
+    pre_grad = back_product(cot_low, down_mat) * slope
+    pre_low = pre_grad.astype(bf16)
+    up_bias_part = jnp.sum(pre_grad, 0)
+    two_far = back_product(pre_low[chip_rows:], up_mat)
+    two_near = back_product(pre_low[:chip_rows], up_mat)
+    normed_two_grad = scatter_rows(two_near, two_far)
+    hidden_in, mlp_gain_part, mlp_shift_part = norm_back(
+        normed_two_grad, unit_two, inverse_two, gain_two
+    )
+    hidden_grad = cot_own.astype(f32) + hidden_in
+    out_bias_part = jnp.sum(hidden_grad, 0)
+    hidden_low = jnp.concatenate(gather_rows(hidden_grad.astype(bf16)), 0)
+    attended_grad = back_product(hidden_low, out_mat).astype(bf16)
+    qkv_low, bias_parts = attention_backward(info, qkv, attended_grad, head_size)
+
+    down_weight_grad = reduce_weight(
+        lambda home: weight_product(gelu_low, strip_of(cot_low, home)), 0, join_on(0)
+    )
+    up_weight_grad = reduce_weight(
+        lambda home: weight_product(strip_of(act_two, home), pre_low), 1, join_on(1)
+    )
+    out_weight_grad = reduce_weight(
+        lambda home: weight_product(attended, strip_of(hidden_low, home)), 0, join_on(0)
+    )
+    mlp_far = matmul(gelu_low[chip_rows:], down_mat)
+    mlp_near = matmul(gelu_low[:chip_rows], down_mat)
+    layer_output = hidden + scatter_rows(mlp_near, mlp_far) + down_vec
+    final_output = return_rows(layer_output.astype(bf16))
+
+    one_far = back_product(qkv_low[chip_rows:], qkv_mat)
+    one_near = back_product(qkv_low[:chip_rows], qkv_mat)
+    normed_one_grad = scatter_rows(one_near, one_far)
+    _, unit_one, inverse_one = normalize(resid, gain_one, shift_one)
+    input_in, attn_gain_part, attn_shift_part = norm_back(
+        normed_one_grad, unit_one, inverse_one, gain_one
+    )
+    final_grad = return_rows((hidden_grad + input_in).astype(bf16))
+
+    def join_qkv(mine, other):
+        mine, other = mine.reshape(strip, 3, features), other.reshape(strip, 3, features)
+        both = jnp.where(
+            y == 0, jnp.concatenate([mine, other], 2), jnp.concatenate([other, mine], 2)
+        ).astype(f32)
+        return both[:, 0], both[:, 1], both[:, 2]
+
+    query_weight_grad, key_weight_grad, value_weight_grad = reduce_weight(
+        lambda home: weight_product(strip_of(act_one, home), qkv_low), 1, join_qkv
+    )
+
+    def placed(v, which):
+        whole = jnp.zeros((4,) + v.shape, f32)
+        return lax.dynamic_update_slice_in_dim(whole, v[None], which, 0)
+
+    column = 2 * t + y
+    rows_sum = jnp.stack(
+        [attn_gain_part, attn_shift_part, out_bias_part, mlp_gain_part, mlp_shift_part, down_bias_part]
+    )
+    head_sum = placed(jnp.stack([bias_parts[:, 0].reshape(-1), bias_parts[:, 1].reshape(-1)]), column)
+    unit_sum = placed(up_bias_part, column)
+    flat = jnp.concatenate([rows_sum.reshape(-1), head_sum.reshape(-1), unit_sum.reshape(-1)])
+    flat = lax.psum(flat, ("fsdp", "ctx", "tp"))
+    cut_one, cut_two = rows_sum.size, rows_sum.size + head_sum.size
+    rows_sum = lax.dynamic_slice_in_dim(flat[:cut_one].reshape(6, width), f * strip, strip, 1)
+    head_sum = lax.dynamic_slice_in_dim(flat[cut_one:cut_two].reshape(4, 2, features), 2 * t, 2, 0)
+    head_sum = head_sum.transpose(1, 0, 2).reshape(2, 2 * local_heads, head_size)
+    head_sum = lax.dynamic_slice_in_dim(head_sum, f * query_bias.shape[1], query_bias.shape[1], 2)
+    unit_sum = lax.dynamic_slice_in_dim(
+        flat[cut_two:].reshape(2, up_bias.shape[0], width), t, 1, 0
+    )[0]
+    unit_sum = lax.dynamic_slice_in_dim(unit_sum, f * strip, strip, 1)
+
+    my_peaks = lax.dynamic_update_slice_in_dim(
+        jnp.full((2, local_heads), NEG, f32), peaks[None], y, 0
+    ).reshape(-1)
+    peak_all = lax.pmax(my_peaks, ("fsdp", "ctx"))
+    level = clip_level[0]
+    factor = jnp.repeat(jnp.sqrt(level / jnp.maximum(peak_all, level)), head_size)
+    query_clipped = (query_weight.astype(f32) * factor[None, :]).astype(bf16)
+    key_clipped = (key_weight.astype(f32) * factor[None, :]).astype(bf16)
+    return (
+        final_output,
+        final_grad,
+        rows_sum[0],
+        rows_sum[1],
+        query_weight_grad,
+        head_sum[0],
+        key_weight_grad,
+        value_weight_grad,
+        head_sum[1],
+        out_weight_grad,
+        rows_sum[2],
+        rows_sum[3],
+        rows_sum[4],
+        up_weight_grad,
+        unit_sum,
+        down_weight_grad,
+        rows_sum[5],
+        peak_all,
+        query_clipped,
+        key_clipped,
+    )
+
+
 def solution(mesh):
+    sizes = dict(mesh.shape)
+    small_slice = sizes == {"fsdp": 4, "ctx": 4, "tp": 2}
     return jax.shard_map(
-        body,
+        split_body if small_slice else gathered_body,
         mesh=mesh,
         in_specs=(
             P(None, ("fsdp", "ctx"), None),

time: 2490 us -> 1360 us (0.55)
  waiting for transfers between devices: 1600 us -> 661 us
  blocking collectives: 279 us -> 93.3 us
  matrix products: 303 us -> 150 us
  starting transfers between devices: 21.8 us -> 171 us
  Pallas kernels: 0 us -> 26.5 us
  loops' own time: 26.3 us -> 0 us
    reduce_scatter x8 -> x0, waiting for transfers between devices: 732 us -> none  [the longest x1 157 us: body(): lax.psum_scatter(up_weight_grad.astype(jnp.bfloat16), 'fsdp', scatter_dim...]
    ppermute x0 -> x79, waiting for transfers between devices: none -> 618 us  [the longest x16 247 us: across_x(): return lax.ppermute(v, 'fsdp', over_x)]
    all_gather x8 -> x0, waiting for transfers between devices: 445 us -> none  [the longest x1 125 us: body(): lax.all_gather(down_weight, 'fsdp', axis=1, tiled=True)]
    psum x4 -> x1, waiting for transfers between devices: 422 us -> 42.8 us  [split_body(): flat = lax.psum(flat, ('fsdp', 'ctx', 'tp'))]
    all_gather x9 -> x2, blocking collectives: 204 us -> 53 us  [the longest x1 43.4 us: split_body(): vectors = lax.all_gather(vectors, 'fsdp', axis=0, tiled=False)]
    ppermute x0 -> x79, starting transfers between devices: none -> 147 us  [the longest x8 38.1 us: z_sum(): first = lax.ppermute(v, 'ctx', [(0, 1), (3, 2)])]
    dot_general x56 -> x0, matrix products: 132 us -> none  [the longest x16 37.4 us: head_scores(): jnp.einsum('sqd,skd->sqk', head_queries, head_keys, preferred_element_typ...]
    pallas_call x0 -> x2, Pallas kernels: none -> 26.5 us  [the longest x1 15.9 us: attention_backward(): pl.pallas_call(functools.partial(attention_backward_kernel, ranks, heads)...]
  transfers between devices with their start and end apart: 27 -> 85, of which waited for: 16 -> 29; matrix products, arithmetic and copies ran while one was open for 12% -> 20% of each run, Pallas kernels for 0% -> 2%
where the time goes in v1:
time: 1360 us; the launch traced here: 1340 us
  waiting for transfers between devices  661 us (49%)
  starting transfers between devices  171 us (13%)
  matrix products  150 us (11%)
  other arithmetic  116 us (9%)
  local copies, waits for them, and re-layouts  99.8 us (7%)
  blocking collectives  93.3 us (7%)
  Pallas kernels  26.5 us (2%)
  between operations  26.3 us (2%)
    ppermute x16, waiting for transfers between devices, across_x(): return lax.ppermute(v, 'fsdp', over_x)  247 us
    ppermute x8, waiting for transfers between devices, z_sum(): back = lax.ppermute(total, 'ctx', [(1, 0), (2, 3)])  193 us
    ppermute x16, waiting for transfers between devices, across_y(): return lax.ppermute(v, 'fsdp', over_y)  108 us
    ppermute x8, waiting for transfers between devices, z_sum(): first = lax.ppermute(v, 'ctx', [(0, 1), (3, 2)])  69.3 us
    dot_general x16, matrix products, weight_product(): jnp.einsum('td,te->de', left, right, preferred_element_type=jnp.float32)  52.2 us
    dot_general x7, matrix products, matmul(): return jnp.dot(left, right, preferred_element_type=jnp.float32)  49.8 us
    dot_general x6, matrix products, back_product(): jnp.einsum('te,de->td', left, right, preferred_element_type=jnp.float32)  47.7 us
    all_gather x1, blocking collectives, split_body(): vectors = lax.all_gather(vectors, 'fsdp', axis=0, tiled=False)  43.4 us
  transfers between devices with their start and end apart: 85, of which 29 were waited for; matrix products, arithmetic and copies ran while one was open for 20% of the time, Pallas kernels for 2%

profile of v1, /device:TPU:0, one launch (start us, length us, event | category | flops | bytes accessed | tf_op | source)
XLA Modules:
  0.0 1344.1 jit_solution(8807531756086864743)
XLA Ops:
  18.0 9.6 all_gather.9
  79.5 43.4 %all-gather.1 = bf16[4,48,32]{1,2,0:T(8,128)(2,1)S(1)} all-gather(bf16[1,48,32]{1,2,0:T(8,128)(2,1)S(1)} %bitcast.166), channel_id=2, replica_groups=mesh['fsdp'=4,'ctx'=4,'tp'=2] {'fsdp'}, dimensions={0}, use_global_device_ids=true | all-gather | bytes 15360 | tf_op jit(solution)/shard_map/all_gather | solution.py:675
  152.3 26.2 %collective-permute-done.10 = bf16[512,512]{1,0:T(8,128)(2,1)} collective-permute-done((bf16[512,512]{1,0:T(8,128)(2,1)}, bf16[512,512]{1,0:T(8,128)(2,1)}, u32[]{:S(2)}, u32[]{:S(2)}) %collective-permute-start.10) | collective-permute-done | bytes 524320 | tf_op jit(solution)/shard_map/ppermute | solution.py:581
  178.5 17.3 %collective-permute-start = (f32[4,64,2048]{2,1,0:T(8,128)}, f32[4,64,2048]{2,1,0:T(8,128)}, u32[]{:S(2)}, u32[]{:S(2)}) collective-permute-start(f32[4,64,2048]{2,1,0:T(8,128)} %get-tuple-element.191), channel_id=1, source_target_pairs={{0,0},{1,8},{8,1},{9,9},{16,16},{17,24},{24,17},{25,25},{2,2},{3,1... | collective-permute-start | bytes 6291464 | tf_op jit(solution)/shard_map/ppermute | solution.py:594
  221.3 10.6 shard_map.347
  269.7 33.1 %collective-permute-done.20 = bf16[2048,512]{1,0:T(8,128)(2,1)} collective-permute-done((bf16[2048,512]{1,0:T(8,128)(2,1)}, bf16[2048,512]{1,0:T(8,128)(2,1)}, u32[]{:S(2)}, u32[]{:S(2)}) %collective-permute-start.20) | collective-permute-done | bytes 2097184 | tf_op jit(solution)/shard_map/ppermute | solution.py:581
  319.2 28.6 %collective-permute-done.19 = bf16[512,2048]{1,0:T(8,128)(2,1)} collective-permute-done((bf16[512,2048]{1,0:T(8,128)(2,1)}, bf16[512,2048]{1,0:T(8,128)(2,1)}, u32[]{:S(2)}, u32[]{:S(2)}) %collective-permute-start.19) | collective-permute-done | bytes 2097184 | tf_op jit(solution)/shard_map/ppermute | solution.py:581
  360.3 25.6 %collective-permute-done.22 = bf16[2048,512]{1,0:T(8,128)(2,1)} collective-permute-done((bf16[2048,512]{1,0:T(8,128)(2,1)}, bf16[2048,512]{1,0:T(8,128)(2,1)}, u32[]{:S(2)}, u32[]{:S(2)}) %collective-permute-start.22) | collective-permute-done | bytes 2097184 | tf_op jit(solution)/shard_map/ppermute | solution.py:581
  389.0 40.3 %pmax.7 = f32[8]{0:T(128)S(1)} all-reduce(f32[8]{0:T(128)S(1)} %reshape.350), channel_id=1, replica_groups=mesh['fsdp'=4,'ctx'=4,'tp'=2] {'fsdp','ctx'}, use_global_device_ids=true, to_apply=%region_18.19 | all-reduce | flops 8 | bytes 64 | tf_op jit(solution)/shard_map/pmax | solution.py:790
  441.1 17.8 %multiply_convert_fusion = (bf16[1024,2048]{1,0:T(8,128)(2,1)}, f32[1024,2048]{1,0:T(8,128)}) fusion(f32[2048]{0:T(1024)S(1)} %dynamic-slice_convert_fusion.1, bf16[2048,2048]{1,0:T(8,128)(2,1)} %constant_dynamic-update-slice_fusion.5, bf16[256,2048]{1,0:T(8,128)(2,1)} %collective-permute-done.16, bf16[256,2048]{1,0:T(8,128)(2,1)} %collective-permute-done.15, ...), kind=kOutput, calls=%fused_computation.6 | convolution fusion | flops 8619294720 | bytes 25174016 | tf_op jit(solution)/shard_map/dot_general | solution.py:41
  458.9 18.1 %fusion.96 = (f32[2048]{0:T(1024)S(1)}, bf16[1024,2048]{1,0:T(8,128)(2,1)S(1)}) fusion(f32[1024,2048]{1,0:T(8,128)} %get-tuple-element.221, f32[2048]{0:T(1024)S(1)} %dynamic-slice_convert_fusion.1, bf16[2048,2048]{1,0:T(8,128)(2,1)} %constant_dynamic-update-slice_fusion.1, bf16[256,2048]{1,0:T(8,128)(2,1)} %collective-permute-done.31, ...), kind=kOutput, calls=%fused_computation.255 | convolution fusion | flops 8631875584 | bytes 25182208 | tf_op jit(solution)/shard_map/te,de->td/dot_general | solution.py:49
  536.7 16.8 %collective-permute-done.34 = bf16[256,2048]{1,0:T(8,128)(2,1)} collective-permute-done((bf16[256,2048]{1,0:T(8,128)(2,1)}, bf16[256,2048]{1,0:T(8,128)(2,1)}, u32[]{:S(2)}, u32[]{:S(2)}) %collective-permute-start.34) | collective-permute-done | bytes 1048608 | tf_op jit(solution)/shard_map/ppermute | solution.py:584
  559.1 16.1 %collective-permute-done.25 = bf16[256,2048]{1,0:T(8,128)(2,1)} collective-permute-done((bf16[256,2048]{1,0:T(8,128)(2,1)}, bf16[256,2048]{1,0:T(8,128)(2,1)}, u32[]{:S(2)}, u32[]{:S(2)}) %collective-permute-start.25) | collective-permute-done | bytes 1048608 | tf_op jit(solution)/shard_map/ppermute | solution.py:584
  593.2 63.8 %collective-permute-done.70 = bf16[2048,512]{1,0:T(8,128)(2,1)} collective-permute-done((bf16[2048,512]{1,0:T(8,128)(2,1)}, bf16[2048,512]{1,0:T(8,128)(2,1)}, u32[]{:S(2)}, u32[]{:S(2)}) %collective-permute-start.70) | collective-permute-done | bytes 2097184 | tf_op jit(solution)/shard_map/ppermute | solution.py:581
  673.5 27.7 %collective-permute-done.74 = bf16[2048,512]{1,0:T(8,128)(2,1)} collective-permute-done((bf16[2048,512]{1,0:T(8,128)(2,1)}, bf16[2048,512]{1,0:T(8,128)(2,1)}, u32[]{:S(2)}, u32[]{:S(2)}) %collective-permute-start.74) | collective-permute-done | bytes 2097184 | tf_op jit(solution)/shard_map/ppermute | solution.py:581
  706.6 10.0 collective-permute-start.26
  727.6 15.9 %shard_map.348 = (bf16[1024,1536]{1,0:T(8,128)(2,1)S(1)}, f32[4,8,128]{2,1,0:T(8,128)S(1)}) custom-call(s32[5]{0:T(128)S(1)} %pad_add_fusion.info, bf16[1024,1536]{1,0:T(8,128)(2,1)} %copy-done, bf16[1024,1536]{1,0:T(8,128)(2,1)} %copy-done, bf16[1024,1536]{1,0:T(8,128)(2,1)} %copy-done, bf16[1024,512]{1,0:T(8,128)(2,1)S(1)} %convolution_convert_fusion.6.g_ref), custom_call_target="tpu_custom_call" | custom-call | flops 5368709120 | bytes 7340032 | tf_op jit(solution)/shard_map/pallas_call | solution.py:516
  768.8 10.4 collective-permute-done.52
  799.5 11.5 collective-permute-done.58
  820.4 25.8 %collective-permute-done.43 = bf16[512,1536]{1,0:T(8,128)(2,1)S(1)} collective-permute-done((bf16[512,1536]{1,0:T(8,128)(2,1)S(1)}, bf16[512,1536]{1,0:T(8,128)(2,1)S(1)}, u32[]{:S(2)}, u32[]{:S(2)}) %collective-permute-start.43) | collective-permute-done | bytes 1572896 | tf_op jit(solution)/shard_map/ppermute | solution.py:581
  861.6 43.0 %collective-permute-done.75 = bf16[2048,512]{1,0:T(8,128)(2,1)} collective-permute-done((bf16[2048,512]{1,0:T(8,128)(2,1)S(1)}, bf16[2048,512]{1,0:T(8,128)(2,1)}, u32[]{:S(2)}, u32[]{:S(2)}) %collective-permute-start.75) | collective-permute-done | bytes 2097184 | tf_op jit(solution)/shard_map/ppermute | solution.py:584
  912.9 12.8 collective-permute-done.40
  940.2 15.3 %collective-permute-done.67 = bf16[512,2048]{1,0:T(8,128)(2,1)} collective-permute-done((bf16[512,2048]{1,0:T(8,128)(2,1)}, bf16[512,2048]{1,0:T(8,128)(2,1)}, u32[]{:S(2)}, u32[]{:S(2)}) %collective-permute-start.67) | collective-permute-done | bytes 2097184 | tf_op jit(solution)/shard_map/ppermute | solution.py:631
  965.5 36.2 %collective-permute-done.76 = bf16[2048,512]{1,0:T(8,128)(2,1)} collective-permute-done((bf16[2048,512]{1,0:T(8,128)(2,1)}, bf16[2048,512]{1,0:T(8,128)(2,1)}, u32[]{:S(2)}, u32[]{:S(2)}) %collective-permute-start.76) | collective-permute-done | bytes 2097184 | tf_op jit(solution)/shard_map/ppermute | solution.py:631
  1022.4 42.8 %all-reduce.2.cloned.1.call-done = f32[24576]{0:T(1024)} async-done(((f32[24576]{0:T(1024)}), f32[24576]{0:T(1024)}) %all-reduce.2.cloned.1.call-update) | async-done | bytes 98320 | tf_op jit(solution)/shard_map/psum | solution.py:776
  1080.2 12.0 collective-permute-start.49
  1101.2 20.0 %collective-permute-done.64 = bf16[512,2048]{1,0:T(8,128)(2,1)} collective-permute-done((bf16[512,2048]{1,0:T(8,128)(2,1)}, bf16[512,2048]{1,0:T(8,128)(2,1)}, u32[]{:S(2)}, u32[]{:S(2)}) %collective-permute-start.64) | collective-permute-done | bytes 2097184 | tf_op jit(solution)/shard_map/ppermute | solution.py:635
  1124.3 41.8 %collective-permute-done.73 = bf16[2048,512]{1,0:T(8,128)(2,1)} collective-permute-done((bf16[2048,512]{1,0:T(8,128)(2,1)}, bf16[2048,512]{1,0:T(8,128)(2,1)}, u32[]{:S(2)}, u32[]{:S(2)}) %collective-permute-start.73) | collective-permute-done | bytes 2097184 | tf_op jit(solution)/shard_map/ppermute | solution.py:635
  1179.3 31.7 %collective-permute-done.69 = bf16[512,2048]{1,0:T(8,128)(2,1)S(1)} collective-permute-done((bf16[512,2048]{1,0:T(8,128)(2,1)S(1)}, bf16[512,2048]{1,0:T(8,128)(2,1)S(1)}, u32[]{:S(2)}, u32[]{:S(2)}) %collective-permute-start.69) | collective-permute-done | bytes 2097184 | tf_op jit(solution)/shard_map/ppermute | solution.py:635
  1217.1 38.9 %collective-permute-done.78 = bf16[2048,512]{1,0:T(8,128)(2,1)S(1)} collective-permute-done((bf16[2048,512]{1,0:T(8,128)(2,1)S(1)}, bf16[2048,512]{1,0:T(8,128)(2,1)S(1)}, u32[]{:S(2)}, u32[]{:S(2)}) %collective-permute-start.78) | collective-permute-done | bytes 2097184 | tf_op jit(solution)/shard_map/ppermute | solution.py:635
  1260.1 29.5 %collective-permute-done.46 = bf16[512,1536]{1,0:T(8,128)(2,1)S(1)} collective-permute-done((bf16[512,1536]{1,0:T(8,128)(2,1)S(1)}, bf16[512,1536]{1,0:T(8,128)(2,1)S(1)}, u32[]{:S(2)}, u32[]{:S(2)}) %collective-permute-start.46) | collective-permute-done | bytes 1572896 | tf_op jit(solution)/shard_map/ppermute | solution.py:635
  1292.7 28.4 %collective-permute-done.51 = bf16[512,1536]{1,0:T(8,128)(2,1)} collective-permute-done((bf16[512,1536]{1,0:T(8,128)(2,1)S(1)}, bf16[512,1536]{1,0:T(8,128)(2,1)}, u32[]{:S(2)}, u32[]{:S(2)}) %collective-permute-start.51) | collective-permute-done | bytes 1572896 | tf_op jit(solution)/shard_map/ppermute | solution.py:635
  (461 shorter events, 496.9 us)
Async XLA Ops:
  57.1 86.7 %all-to-all-start.1 = ((bf16[4,64,2048]{2,1,0:T(8,128)(2,1)}), bf16[4,64,2048]{2,1,0:T(8,128)(2,1)S(1)}, u32[]{:S(2)}, u32[]{:S(2)}) async-start(bf16[4,64,2048]{2,1,0:T(8,128)(2,1)} %collective-permute-done.1), calls=%async_computation.1 | async-start | bytes 2097152 | tf_op jit(solution)/shard_map/all_to_all | solution.py:595
  65.1 131.7 %collective-permute-start.3 = (bf16[512,1536]{0,1:T(8,128)(2,1)}, bf16[512,1536]{0,1:T(8,128)(2,1)}, u32[]{:S(2)}, u32[]{:S(2)}) collective-permute-start(bf16[512,1536]{0,1:T(8,128)(2,1)} %get-tuple-element.175), channel_id=1, source_target_pairs={{0,8},{8,0},{16,24},{24,16},{1,9},{9,1},{17,25},{25,17},{2,10},{10... | collective-permute-start | bytes 4718600 | tf_op jit(solution)/shard_map/ppermute | solution.py:581
  207.3 95.5 %collective-permute-start.20 = (bf16[2048,512]{1,0:T(8,128)(2,1)}, bf16[2048,512]{1,0:T(8,128)(2,1)}, u32[]{:S(2)}, u32[]{:S(2)}) collective-permute-start(bf16[2048,512]{1,0:T(8,128)(2,1)} %get-tuple-element.173), channel_id=1, source_target_pairs={{0,8},{8,0},{16,24},{24,16},{1,9},{9,1},{17,25},{25,17},{2,10},{10... | collective-permute-start | bytes 6291464 | tf_op jit(solution)/shard_map/ppermute | solution.py:581
  215.9 93.2 %collective-permute-start.21 = (bf16[2048,512]{1,0:T(8,128)(2,1)}, bf16[2048,512]{1,0:T(8,128)(2,1)}, u32[]{:S(2)}, u32[]{:S(2)}) collective-permute-start(bf16[2048,512]{1,0:T(8,128)(2,1)} %get-tuple-element.184), channel_id=1, source_target_pairs={{0,16},{16,0},{8,24},{24,8},{1,17},{17,1},{9,25},{25,9},{2,18},{18... | collective-permute-start | bytes 6291464 | tf_op jit(solution)/shard_map/ppermute | solution.py:584
  231.9 119.3 %all-to-all-start = ((f32[4,64,2048]{2,1,0:T(8,128)}), f32[4,64,2048]{2,1,0:T(8,128)S(1)}, u32[]{:S(2)}, u32[]{:S(2)}) async-start(f32[4,64,2048]{2,1,0:T(8,128)} %collective-permute-done), calls=%async_computation | async-start | bytes 4194304 | tf_op jit(solution)/shard_map/all_to_all | solution.py:595
  251.8 96.0 %collective-permute-start.19 = (bf16[512,2048]{1,0:T(8,128)(2,1)}, bf16[512,2048]{1,0:T(8,128)(2,1)}, u32[]{:S(2)}, u32[]{:S(2)}) collective-permute-start(bf16[512,2048]{1,0:T(8,128)(2,1)} %collective-permute-done.18), channel_id=1, source_target_pairs={{0,8},{8,0},{16,24},{24,16},{1,9},{9,1},{17,25},{25,17},{2,10},{10... | collective-permute-start | bytes 6291464 | tf_op jit(solution)/shard_map/ppermute | solution.py:581
  266.7 84.5 %collective-permute-start.11 = (bf16[256,2048]{1,0:T(8,128)(2,1)}, bf16[256,2048]{1,0:T(8,128)(2,1)S(1)}, u32[]{:S(2)}, u32[]{:S(2)}) collective-permute-start(bf16[256,2048]{1,0:T(8,128)(2,1)} %slice.385), channel_id=1, source_target_pairs={{0,1},{1,0},{2,3},{3,2},{4,5},{5,4},{6,7},{7,6},{8,9},{9,8},{10,11... | collective-permute-start | bytes 3145736 | tf_op jit(solution)/shard_map/ppermute | solution.py:587
  319.2 116.3 %collective-permute-start.29 = (bf16[256,2048]{1,0:T(8,128)(2,1)}, bf16[256,2048]{1,0:T(8,128)(2,1)}, u32[]{:S(2)}, u32[]{:S(2)}) collective-permute-start(bf16[256,2048]{1,0:T(8,128)(2,1)} %bitcast.27), channel_id=1, source_target_pairs={{0,1},{1,0},{2,3},{3,2},{4,5},{5,4},{6,7},{7,6},{8,9},{9,8},{10,11... | collective-permute-start | bytes 3145736 | tf_op jit(solution)/shard_map/ppermute | solution.py:587
  347.8 87.7 %collective-permute-start.31 = (bf16[256,2048]{1,0:T(8,128)(2,1)}, bf16[256,2048]{1,0:T(8,128)(2,1)}, u32[]{:S(2)}, u32[]{:S(2)}) collective-permute-start(bf16[256,2048]{1,0:T(8,128)(2,1)} %collective-permute-done.30), channel_id=1, source_target_pairs={{0,1},{1,0},{2,3},{3,2},{4,5},{5,4},{6,7},{7,6},{8,9},{9,8},{10,11... | collective-permute-start | bytes 3145736 | tf_op jit(solution)/shard_map/ppermute | solution.py:587
  534.6 130.5 %collective-permute-start.65 = (bf16[512,2048]{1,0:T(8,128)(2,1)}, bf16[512,2048]{1,0:T(8,128)(2,1)}, u32[]{:S(2)}, u32[]{:S(2)}) collective-permute-start(bf16[512,2048]{1,0:T(8,128)(2,1)} %convolution_convert_fusion.2), channel_id=1, source_target_pairs={{0,8},{8,0},{16,24},{24,16},{1,9},{9,1},{17,25},{25,17},{2,10},{10... | collective-permute-start | bytes 6291464 | tf_op jit(solution)/shard_map/ppermute | solution.py:581
  553.5 103.5 %collective-permute-start.70 = (bf16[2048,512]{1,0:T(8,128)(2,1)}, bf16[2048,512]{1,0:T(8,128)(2,1)}, u32[]{:S(2)}, u32[]{:S(2)}) collective-permute-start(bf16[2048,512]{1,0:T(8,128)(2,1)} %convolution_convert_fusion.1), channel_id=1, source_target_pairs={{0,8},{8,0},{16,24},{24,16},{1,9},{9,1},{17,25},{25,17},{2,10},{10... | collective-permute-start | bytes 6291464 | tf_op jit(solution)/shard_map/ppermute | solution.py:581
  559.1 142.1 %collective-permute-start.74 = (bf16[2048,512]{1,0:T(8,128)(2,1)}, bf16[2048,512]{1,0:T(8,128)(2,1)}, u32[]{:S(2)}, u32[]{:S(2)}) collective-permute-start(bf16[2048,512]{1,0:T(8,128)(2,1)} %convolution_convert_fusion), channel_id=1, source_target_pairs={{0,8},{8,0},{16,24},{24,16},{1,9},{9,1},{17,25},{25,17},{2,10},{10... | collective-permute-start | bytes 6291464 | tf_op jit(solution)/shard_map/ppermute | solution.py:581
  579.9 126.7 %all-to-all-start.2 = ((bf16[4,64,2048]{2,1,0:T(8,128)(2,1)}), bf16[4,64,2048]{2,1,0:T(8,128)(2,1)}, u32[]{:S(2)}, u32[]{:S(2)}) async-start(bf16[4,64,2048]{2,1,0:T(8,128)(2,1)} %bitcast.23), calls=%async_computation.2 | async-start | bytes 2097152 | tf_op jit(solution)/shard_map/all_to_all | solution.py:600
  586.0 130.5 %collective-permute-start.35 = (bf16[256,2048]{1,0:T(8,128)(2,1)}, bf16[256,2048]{1,0:T(8,128)(2,1)}, u32[]{:S(2)}, u32[]{:S(2)}) collective-permute-start(bf16[256,2048]{1,0:T(8,128)(2,1)} %convert_element_type.383), channel_id=1, source_target_pairs={{0,1},{1,0},{2,3},{3,2},{4,5},{5,4},{6,7},{7,6},{8,9},{9,8},{10,11... | collective-permute-start | bytes 3145736 | tf_op jit(solution)/shard_map/ppermute | solution.py:587
  657.0 100.0 %collective-permute-start.62 = (bf16[512,2048]{1,0:T(8,128)(2,1)}, bf16[512,2048]{1,0:T(8,128)(2,1)}, u32[]{:S(2)}, u32[]{:S(2)}) collective-permute-start(bf16[512,2048]{1,0:T(8,128)(2,1)} %add_convert_fusion.11), channel_id=1, source_target_pairs={{0,2},{6,4},{1,3},{7,5},{8,10},{14,12},{9,11},{15,13},{16,18},{22,... | collective-permute-start | bytes 6291464 | tf_op jit(solution)/shard_map/ppermute | solution.py:631
  665.1 115.5 %collective-permute-start.71 = (bf16[2048,512]{1,0:T(8,128)(2,1)}, bf16[2048,512]{1,0:T(8,128)(2,1)}, u32[]{:S(2)}, u32[]{:S(2)}) collective-permute-start(bf16[2048,512]{1,0:T(8,128)(2,1)} %add_convert_fusion.5), channel_id=1, source_target_pairs={{0,2},{6,4},{1,3},{7,5},{8,10},{14,12},{9,11},{15,13},{16,18},{22,... | collective-permute-start | bytes 6291464 | tf_op jit(solution)/shard_map/ppermute | solution.py:631
  812.5 92.0 %collective-permute-start.75 = (bf16[2048,512]{1,0:T(8,128)(2,1)S(1)}, bf16[2048,512]{1,0:T(8,128)(2,1)}, u32[]{:S(2)}, u32[]{:S(2)}) collective-permute-start(bf16[2048,512]{1,0:T(8,128)(2,1)S(1)} %copy-done.49), channel_id=1, source_target_pairs={{0,16},{16,0},{8,24},{24,8},{1,17},{17,1},{9,25},{25,9},{2,18},{18... | collective-permute-start | bytes 6291464 | tf_op jit(solution)/shard_map/ppermute | solution.py:584
  813.4 96.9 %collective-permute-start.38 = (bf16[256,2048]{1,0:T(8,128)(2,1)S(1)}, bf16[256,2048]{1,0:T(8,128)(2,1)S(1)}, u32[]{:S(2)}, u32[]{:S(2)}) collective-permute-start(bf16[256,2048]{1,0:T(8,128)(2,1)S(1)} %slice.379), channel_id=1, source_target_pairs={{0,1},{1,0},{2,3},{3,2},{4,5},{5,4},{6,7},{7,6},{8,9},{9,8},{10,11... | collective-permute-start | bytes 3145736 | tf_op jit(solution)/shard_map/ppermute | solution.py:587
  815.4 190.4 %collective-permute-start.63 = (bf16[512,2048]{1,0:T(8,128)(2,1)}, bf16[512,2048]{1,0:T(8,128)(2,1)}, u32[]{:S(2)}, u32[]{:S(2)}) collective-permute-start(bf16[512,2048]{1,0:T(8,128)(2,1)} %add_convert_fusion.10), channel_id=1, source_target_pairs={{2,4},{4,2},{3,5},{5,3},{10,12},{12,10},{11,13},{13,11},{18,20},{2... | collective-permute-start | bytes 6291464 | tf_op jit(solution)/shard_map/ppermute | solution.py:633
  859.6 152.0 %collective-permute-start.72 = (bf16[2048,512]{1,0:T(8,128)(2,1)}, bf16[2048,512]{1,0:T(8,128)(2,1)}, u32[]{:S(2)}, u32[]{:S(2)}) collective-permute-start(bf16[2048,512]{1,0:T(8,128)(2,1)} %add_convert_fusion.4), channel_id=1, source_target_pairs={{2,4},{4,2},{3,5},{5,3},{10,12},{12,10},{11,13},{13,11},{18,20},{2... | collective-permute-start | bytes 6291464 | tf_op jit(solution)/shard_map/ppermute | solution.py:633
  910.3 91.4 %collective-permute-start.76 = (bf16[2048,512]{1,0:T(8,128)(2,1)}, bf16[2048,512]{1,0:T(8,128)(2,1)}, u32[]{:S(2)}, u32[]{:S(2)}) collective-permute-start(bf16[2048,512]{1,0:T(8,128)(2,1)} %collective-permute-done.75), channel_id=1, source_target_pairs={{0,2},{6,4},{1,3},{7,5},{8,10},{14,12},{9,11},{15,13},{16,18},{22,... | collective-permute-start | bytes 6291464 | tf_op jit(solution)/shard_map/ppermute | solution.py:631
  930.3 166.3 %all-to-all-start.4 = ((bf16[4,64,2048]{2,1,0:T(8,128)(2,1)}), bf16[4,64,2048]{2,1,0:T(8,128)(2,1)}, u32[]{:S(2)}, u32[]{:S(2)}) async-start(bf16[4,64,2048]{2,1,0:T(8,128)(2,1)} %bitcast.28), calls=%async_computation.4 | async-start | bytes 2097152 | tf_op jit(solution)/shard_map/all_to_all | solution.py:600
  936.0 129.2 %all-reduce.2.cloned.1.call-start = ((), (), s32[]{:S(2)}) async-start(), calls=%async_computation.5 | async-start | bytes 196608 | tf_op jit(solution)/shard_map/psum | solution.py:776
  936.8 141.6 %collective-permute-start.48 = (bf16[512,1536]{1,0:T(8,128)(2,1)}, bf16[512,1536]{1,0:T(8,128)(2,1)}, u32[]{:S(2)}, u32[]{:S(2)}) collective-permute-start(bf16[512,1536]{1,0:T(8,128)(2,1)} %fusion.9), channel_id=1, source_target_pairs={{0,16},{16,0},{8,24},{24,8},{1,17},{17,1},{9,25},{25,9},{2,18},{18... | collective-permute-start | bytes 4718600 | tf_op jit(solution)/shard_map/ppermute | solution.py:584
  955.5 118.1 %collective-permute-start.44 = (bf16[512,1536]{1,0:T(8,128)(2,1)}, bf16[512,1536]{1,0:T(8,128)(2,1)}, u32[]{:S(2)}, u32[]{:S(2)}) collective-permute-start(bf16[512,1536]{1,0:T(8,128)(2,1)} %fusion.8), channel_id=1, source_target_pairs={{0,2},{6,4},{1,3},{7,5},{8,10},{14,12},{9,11},{15,13},{16,18},{22,... | collective-permute-start | bytes 4718600 | tf_op jit(solution)/shard_map/ppermute | solution.py:631
  1073.6 92.5 %collective-permute-start.73 = (bf16[2048,512]{1,0:T(8,128)(2,1)}, bf16[2048,512]{1,0:T(8,128)(2,1)}, u32[]{:S(2)}, u32[]{:S(2)}) collective-permute-start(bf16[2048,512]{1,0:T(8,128)(2,1)} %add_convert_fusion.3), channel_id=1, source_target_pairs={{2,0},{4,6},{3,1},{5,7},{10,8},{12,14},{11,9},{13,15},{18,16},{20,... | collective-permute-start | bytes 6291464 | tf_op jit(solution)/shard_map/ppermute | solution.py:635
  1078.4 94.1 %collective-permute-start.45 = (bf16[512,1536]{1,0:T(8,128)(2,1)}, bf16[512,1536]{1,0:T(8,128)(2,1)}, u32[]{:S(2)}, u32[]{:S(2)}) collective-permute-start(bf16[512,1536]{1,0:T(8,128)(2,1)} %add_convert_fusion.15), channel_id=1, source_target_pairs={{2,4},{4,2},{3,5},{5,3},{10,12},{12,10},{11,13},{13,11},{18,20},{2... | collective-permute-start | bytes 4718600 | tf_op jit(solution)/shard_map/ppermute | solution.py:633
  1080.2 89.2 %collective-permute-start.49 = (bf16[512,1536]{1,0:T(8,128)(2,1)}, bf16[512,1536]{1,0:T(8,128)(2,1)}, u32[]{:S(2)}, u32[]{:S(2)}) collective-permute-start(bf16[512,1536]{1,0:T(8,128)(2,1)} %collective-permute-done.48), channel_id=1, source_target_pairs={{0,2},{6,4},{1,3},{7,5},{8,10},{14,12},{9,11},{15,13},{16,18},{22,... | collective-permute-start | bytes 4718600 | tf_op jit(solution)/shard_map/ppermute | solution.py:631
  1121.2 89.8 %collective-permute-start.69 = (bf16[512,2048]{1,0:T(8,128)(2,1)S(1)}, bf16[512,2048]{1,0:T(8,128)(2,1)S(1)}, u32[]{:S(2)}, u32[]{:S(2)}) collective-permute-start(bf16[512,2048]{1,0:T(8,128)(2,1)S(1)} %copy-done.19), channel_id=1, source_target_pairs={{2,0},{4,6},{3,1},{5,7},{10,8},{12,14},{11,9},{13,15},{18,16},{20,... | collective-permute-start | bytes 6291464 | tf_op jit(solution)/shard_map/ppermute | solution.py:635
  1166.2 89.8 %collective-permute-start.78 = (bf16[2048,512]{1,0:T(8,128)(2,1)S(1)}, bf16[2048,512]{1,0:T(8,128)(2,1)S(1)}, u32[]{:S(2)}, u32[]{:S(2)}) collective-permute-start(bf16[2048,512]{1,0:T(8,128)(2,1)S(1)} %add_convert_fusion), channel_id=1, source_target_pairs={{2,0},{4,6},{3,1},{5,7},{10,8},{12,14},{11,9},{13,15},{18,16},{20,... | collective-permute-start | bytes 6291464 | tf_op jit(solution)/shard_map/ppermute | solution.py:635
  1174.7 115.0 %collective-permute-start.46 = (bf16[512,1536]{1,0:T(8,128)(2,1)S(1)}, bf16[512,1536]{1,0:T(8,128)(2,1)S(1)}, u32[]{:S(2)}, u32[]{:S(2)}) collective-permute-start(bf16[512,1536]{1,0:T(8,128)(2,1)S(1)} %add_convert_fusion.14), channel_id=1, source_target_pairs={{2,0},{4,6},{3,1},{5,7},{10,8},{12,14},{11,9},{13,15},{18,16},{20,... | collective-permute-start | bytes 4718600 | tf_op jit(solution)/shard_map/ppermute | solution.py:635
  1215.8 105.3 %collective-permute-start.51 = (bf16[512,1536]{1,0:T(8,128)(2,1)S(1)}, bf16[512,1536]{1,0:T(8,128)(2,1)}, u32[]{:S(2)}, u32[]{:S(2)}) collective-permute-start(bf16[512,1536]{1,0:T(8,128)(2,1)S(1)} %add_convert_fusion.12), channel_id=1, source_target_pairs={{2,0},{4,6},{3,1},{5,7},{10,8},{12,14},{11,9},{13,15},{18,16},{20,... | collective-permute-start | bytes 4718600 | tf_op jit(solution)/shard_map/ppermute | solution.py:635
  (111 other events, 3803.2 us)
Sparse Core Ops, SparseCore 0:
  942.4 122.7 all-reduce.1

commit v2 on v1

--- a/solution.py
+++ b/solution.py
@@ -535,6 +535,583 @@
             flops=10 * tokens * tokens * features, bytes_accessed=14 * tokens * features, transcendentals=0
         ),
     )(info, qkv, qkv, qkv, grads)
+
+
+def entry_barrier(targets):
+    barrier = pltpu.get_barrier_semaphore()
+    for target in targets:
+        pl.semaphore_signal(barrier, inc=1, device_id=target, device_id_type=pl.DeviceIdType.MESH)
+    pl.semaphore_wait(barrier, len(targets))
+
+
+def gather_kernel(
+    q_ref,
+    k_ref,
+    v_ref,
+    o_ref,
+    u_ref,
+    d_ref,
+    act_ref,
+    cot_ref,
+    res_ref,
+    qkv_all,
+    out_all,
+    up_all,
+    down_all,
+    act_all,
+    cot_all,
+    res_own,
+    local_sem,
+    send_sem,
+    recv_sem,
+    row_send,
+    row_recv,
+    join_send,
+    join_recv,
+):
+    f = lax.axis_index("fsdp")
+    z = lax.axis_index("ctx")
+    t = lax.axis_index("tp")
+    y, x = f // 2, f % 2
+    depth = act_ref.shape[0]
+    block_rows = act_ref.shape[1]
+    own_rows = depth * block_rows
+    strip = q_ref.shape[0]
+    features = q_ref.shape[1] // 2
+    hidden = u_ref.shape[1] // 2
+    even = z % 2 == 0
+    mate_z = z + 1 - 2 * (z % 2)
+    over_x = {"fsdp": 2 * y + 1 - x, "ctx": z, "tp": t}
+    over_y = {"fsdp": 2 * (1 - y) + x, "ctx": z, "tp": t}
+    over_z = {"fsdp": f, "ctx": mate_z, "tp": t}
+    over_core = {"fsdp": f, "ctx": z, "tp": 1 - t}
+    turned = x != t
+
+    def row_target(k):
+        return {"fsdp": 2 * y + t, "ctx": k, "tp": x}
+
+    targets = [over_x, over_y, over_z, over_core]
+    targets += [row_target(lax.rem(z + k, depth)) for k in range(1, depth)]
+    targets.append({"fsdp": 2 * y + 1 - x, "ctx": z, "tp": 1 - t})
+    entry_barrier(targets)
+
+    def at(start, size):
+        return pl.ds(pl.multiple_of(start, 128), size)
+
+    chunks = []
+    for k, ref in enumerate((q_ref, k_ref, v_ref)):
+        chunks.append(
+            (
+                lambda w, ref=ref: ref.at[:, at(w * features, features)],
+                lambda home, k=k: qkv_all.at[at(home * strip, strip), pl.ds(k * features, features)],
+            )
+        )
+    chunks.append(
+        (
+            lambda w: o_ref.at[at(w * features, features), :],
+            lambda home: out_all.at[:, at(home * strip, strip)],
+        )
+    )
+    pieces = 4
+    for k in range(pieces):
+        size = strip // pieces
+        chunks.append(
+            (
+                lambda w, k=k, size=size: u_ref.at[pl.ds(k * size, size), at(w * hidden, hidden)],
+                lambda home, k=k, size=size: up_all.at[at(home * strip + k * size, size), :],
+            )
+        )
+    for k in range(pieces):
+        size = hidden // pieces
+        chunks.append(
+            (
+                lambda w, k=k, size=size: d_ref.at[at(w * hidden + k * size, size), :],
+                lambda home, k=k, size=size: down_all.at[pl.ds(k * size, size), at(home * strip, strip)],
+            )
+        )
+    count = len(chunks)
+
+    def remote(src, dst, send, recv, target):
+        return pltpu.make_async_remote_copy(
+            src_ref=src,
+            dst_ref=dst,
+            send_sem=send,
+            recv_sem=recv,
+            device_id=target,
+            device_id_type=pl.DeviceIdType.MESH,
+        )
+
+    far_home = 2 * (1 - y) + x
+
+    def own_copy(i):
+        source, place = chunks[i]
+        return pltpu.make_async_copy(source(y), place(f), local_sem.at[i])
+
+    def y_copy(i):
+        source, place = chunks[i]
+        return remote(source(1 - y), place(f), send_sem.at[0, i], recv_sem.at[0, i], over_y)
+
+    def x_copy(i, is_even):
+        source, place = chunks[i]
+        if is_even:
+            return remote(source(y), place(f), send_sem.at[1, i], recv_sem.at[1, i], over_x)
+        return remote(
+            place(far_home), place(far_home), send_sem.at[1, i], recv_sem.at[1, i], over_x
+        )
+
+    def z_copy(i, is_even):
+        source, place = chunks[i]
+        home = 2 * y + 1 - x if is_even else 2 * (1 - y) + 1 - x
+        return remote(place(home), place(home), send_sem.at[2, i], recv_sem.at[2, i], over_z)
+
+    rows_of = ((act_ref, act_all), (cot_ref, cot_all), (res_ref, res_own))
+
+    def row_copy(a, k):
+        source, place = rows_of[a]
+        return remote(
+            source.at[k],
+            place.at[pl.ds(pl.multiple_of(z * block_rows, block_rows), block_rows), :],
+            row_send.at[a, k],
+            row_recv.at[a, z],
+            row_target(k),
+        )
+
+    def row_arrival(a, k):
+        source, place = rows_of[a]
+        return remote(
+            source.at[k],
+            place.at[pl.ds(k * block_rows, block_rows), :],
+            row_send.at[a, k],
+            row_recv.at[a, k],
+            row_target(k),
+        )
+
+    def row_stay(a, k):
+        source, place = rows_of[a]
+        return pltpu.make_async_copy(
+            source.at[k], place.at[pl.ds(k * block_rows, block_rows), :], row_send.at[a, k]
+        )
+
+    def rows_start(a):
+        for k in range(depth):
+            stays = (z == k) & (x == t)
+            pl.when(stays)(lambda k=k: row_stay(a, k).start())
+            pl.when(jnp.logical_not(stays))(lambda k=k: row_copy(a, k).start())
+
+    def rows_wait(a):
+        for k in range(depth):
+            stays = (z == k) & (x == t)
+            pl.when(stays)(lambda k=k: row_stay(a, k).wait())
+
+            @pl.when(jnp.logical_not(stays))
+            def _(k=k):
+                row_copy(a, k).wait_send()
+                row_arrival(a, k).wait_recv()
+
+    def block(a, k):
+        return rows_of[a][1].at[pl.ds(k * own_rows, own_rows), :]
+
+    def join_copy(a, step):
+        source, place, target = (
+            (0, 1, over_core),
+            (0, 2, over_y),
+            (2, 3, over_core),
+        )[step]
+        return remote(
+            block(a, source), block(a, place), join_send.at[a, step], join_recv.at[a, step], target
+        )
+
+    def join_start(a):
+        rows_wait(a)
+        join_copy(a, 0).start()
+        join_copy(a, 1).start()
+
+    def join_pass(a):
+        join_copy(a, 1).wait_recv()
+        join_copy(a, 2).start()
+
+    events = {
+        0: [lambda: rows_start(0)],
+        2: [lambda: rows_start(1), lambda: join_start(0)],
+        4: [lambda: rows_start(2), lambda: join_pass(0)],
+        6: [lambda: join_start(1)],
+        9: [lambda: join_pass(1)],
+    }
+    lag = 2
+    for i in range(count + 2 * lag):
+        for event in events.get(i, ()):
+            event()
+        if i < count:
+            y_copy(i).start()
+            pl.when(even)(lambda i=i: x_copy(i, True).start())
+            own_copy(i).start()
+        j = i - lag
+        if 0 <= j < count:
+            y_copy(j).wait_recv()
+
+            @pl.when(even)
+            def _(j=j):
+                x_copy(j, True).wait_recv()
+                z_copy(j, True).start()
+
+            pl.when(jnp.logical_not(even))(lambda j=j: x_copy(j, False).start())
+        j = i - 2 * lag
+        if 0 <= j < count:
+
+            @pl.when(jnp.logical_not(even))
+            def _(j=j):
+                x_copy(j, False).wait_recv()
+                z_copy(j, False).start()
+
+    for i in range(count):
+        own_copy(i).wait()
+        y_copy(i).wait_send()
+        x_copy(i, True).wait_send()
+        z_copy(i, True).wait()
+    for a in range(2):
+        join_copy(a, 0).wait()
+        join_copy(a, 1).wait_send()
+        join_copy(a, 2).wait()
+    rows_wait(2)
+
+
+def gather_all(query_weight, key_weight, value_weight, out_weight, up_weight, down_weight, act, cot, res):
+    strip, features, hidden = query_weight.shape[0], query_weight.shape[1] // 2, up_weight.shape[1] // 2
+    width = 4 * strip
+    own_rows = act.shape[0] * act.shape[1]
+    bf16 = jnp.bfloat16
+    hbm = pl.BlockSpec(memory_space=pl.ANY)
+    count = 12
+    dma = pltpu.SemaphoreType.DMA
+    return pl.pallas_call(
+        gather_kernel,
+        out_shape=(
+            jax.ShapeDtypeStruct((width, 3 * features), bf16),
+            jax.ShapeDtypeStruct((features, width), bf16),
+            jax.ShapeDtypeStruct((width, hidden), bf16),
+            jax.ShapeDtypeStruct((hidden, width), bf16),
+            jax.ShapeDtypeStruct((4 * own_rows, width), bf16),
+            jax.ShapeDtypeStruct((4 * own_rows, width), bf16),
+            jax.ShapeDtypeStruct((own_rows, width), jnp.float32),
+        ),
+        in_specs=[hbm] * 9,
+        out_specs=(hbm,) * 7,
+        scratch_shapes=[
+            dma((count,)),
+            dma((3, count)),
+            dma((3, count)),
+            dma((3, act.shape[0])),
+            dma((3, act.shape[0])),
+            dma((2, 3)),
+            dma((2, 3)),
+        ],
+        compiler_params=pltpu.CompilerParams(collective_id=0, has_side_effects=True),
+        cost_estimate=pl.CostEstimate(flops=0, bytes_accessed=64 << 20, transcendentals=0),
+    )(query_weight, key_weight, value_weight, out_weight, up_weight, down_weight, act, cot, res)
+
+
+def reduce_kernel(
+    down_parts, up_parts, out_parts, qkv_parts, down_sum, up_sum, out_sum, qkv_sums, scratch
+):
+    (
+        x_slot,
+        own_slot,
+        pair_slot,
+        y_slot,
+        z_slot,
+        z_pair,
+        inner_slot,
+        total_slot,
+        x_send,
+        x_recv,
+        own_sem,
+        y_send,
+        y_recv,
+        outer_send,
+        outer_recv,
+        inner_send,
+        inner_recv,
+        out_sem,
+        x_free,
+        y_free,
+        outer_free,
+        inner_free,
+    ) = scratch
+    f = lax.axis_index("fsdp")
+    z = lax.axis_index("ctx")
+    t = lax.axis_index("tp")
+    y, x = f // 2, f % 2
+    outer = (z == 0) | (z == 3)
+    inner = (z == 1) | (z == 2)
+    over_x = {"fsdp": 2 * y + 1 - x, "ctx": z, "tp": t}
+    over_y = {"fsdp": 2 * (1 - y) + x, "ctx": z, "tp": t}
+    mate = {"fsdp": f, "ctx": z + 1 - 2 * (z % 2), "tp": t}
+    middle = {"fsdp": f, "ctx": 3 - z, "tp": t}
+    entry_barrier([over_x, over_y, mate, middle])
+    slots, rows, cols = x_slot.shape
+
+    def remote(src, dst, send, recv, target):
+        return pltpu.make_async_remote_copy(
+            src_ref=src,
+            dst_ref=dst,
+            send_sem=send,
+            recv_sem=recv,
+            device_id=target,
+            device_id_type=pl.DeviceIdType.MESH,
+        )
+
+    def grant(semaphore, target):
+        pl.semaphore_signal(semaphore, inc=1, device_id=target, device_id_type=pl.DeviceIdType.MESH)
+
+    def at(start, size):
+        return pl.ds(pl.multiple_of(start, 128), size)
+
+    near_items, far_items = [], []
+
+    def add_items(parts, row_count, col_count, place):
+        near_send, far_send, near_own, far_own = parts
+        for r in range(row_count):
+            for c in range(col_count):
+                cut = (pl.ds(r * rows, rows), pl.ds(c * cols, cols))
+                near_items.append((near_send.at[cut], near_own.at[cut], place(y, r, c)))
+                far_items.append((far_send.at[cut], far_own.at[cut], place(1 - y, r, c)))
+
+    down_rows = down_sum.shape[0] // 2
+    add_items(
+        down_parts,
+        down_rows // rows,
+        1,
+        lambda h, r, c: down_sum.at[at(h * down_rows + r * rows, rows), :],
+    )
+    up_cols = up_sum.shape[1] // 2
+    add_items(
+        up_parts,
+        up_sum.shape[0] // rows,
+        up_cols // cols,
+        lambda h, r, c: up_sum.at[pl.ds(r * rows, rows), at(h * up_cols + c * cols, cols)],
+    )
+    out_rows = out_sum.shape[0] // 2
+    add_items(
+        out_parts,
+        out_rows // rows,
+        1,
+        lambda h, r, c: out_sum.at[at(h * out_rows + r * rows, rows), :],
+    )
+    add_items(
+        qkv_parts,
+        out_sum.shape[1] // rows,
+        3,
+        lambda h, r, c: qkv_sums[c].at[pl.ds(r * rows, rows), at(h * cols, cols)],
+    )
+    items = []
+    for near, far in zip(near_items, far_items):
+        items += [(True, *far), (False, *near)]
+    count = len(items)
+    far_count = count // 2
+    far_slots = y_slot.shape[0]
+
+    def x_copy(i):
+        k = i % slots
+        return remote(items[i][1], x_slot.at[k], x_send.at[k], x_recv.at[k], over_x)
+
+    def own_copy(i):
+        k = i % slots
+        return pltpu.make_async_copy(items[i][2], own_slot.at[k], own_sem.at[k])
+
+    def y_copy(i):
+        k = i % slots
+        g = (i // 2) % far_slots
+        return remote(pair_slot.at[k], y_slot.at[g], y_send.at[g], y_recv.at[g], over_y)
+
+    def summed(i):
+        return y_slot.at[(i // 2) % far_slots] if items[i][0] else pair_slot.at[i % slots]
+
+    def outward(i):
+        k = i % slots
+        return remote(summed(i), z_slot.at[k], outer_send.at[k], outer_recv.at[k], mate)
+
+    def across(i):
+        k = i % slots
+        return remote(z_pair.at[k], inner_slot.at[k], inner_send.at[k], inner_recv.at[k], middle)
+
+    def backward(i):
+        k = i % slots
+        return remote(total_slot.at[k], z_slot.at[k], outer_send.at[k], outer_recv.at[k], mate)
+
+    def result_inner(i):
+        k = i % slots
+        return pltpu.make_async_copy(total_slot.at[k], items[i][3], out_sem.at[k])
+
+    def result_outer(i):
+        k = i % slots
+        return pltpu.make_async_copy(z_slot.at[k], items[i][3], out_sem.at[k])
+
+    def add(left, right, target):
+        target[...] = (left[...].astype(jnp.float32) + right[...].astype(jnp.float32)).astype(
+            target.dtype
+        )
+
+    def stage_send(i):
+        if i >= slots:
+            pl.semaphore_wait(x_free, 1)
+        x_copy(i).start()
+        own_copy(i).start()
+
+    def stage_pair(i):
+        x_copy(i).wait()
+        own_copy(i).wait()
+        k = i % slots
+        add(x_slot.at[k], own_slot.at[k], pair_slot.at[k])
+        if i + slots < count:
+            grant(x_free, over_x)
+        if items[i][0]:
+            if i // 2 >= far_slots:
+                pl.semaphore_wait(y_free, 1)
+            y_copy(i).start()
+
+    def stage_outward(i):
+        if items[i][0]:
+            y_copy(i).wait()
+
+        @pl.when(outer)
+        def _():
+            if i >= slots:
+                pl.semaphore_wait(outer_free, 1)
+            outward(i).start()
+
+    def stage_across(i):
+        k = i % slots
+
+        @pl.when(outer)
+        def _():
+            outward(i).wait_send()
+
+        @pl.when(inner)
+        def _():
+            outward(i).wait_recv()
+            add(summed(i), z_slot.at[k], z_pair.at[k])
+            if i + slots < count:
+                grant(outer_free, mate)
+            if i >= slots:
+                pl.semaphore_wait(inner_free, 1)
+            across(i).start()
+
+        if items[i][0] and i // 2 + far_slots < far_count:
+            grant(y_free, over_y)
+
+    def stage_total(i):
+        k = i % slots
+
+        @pl.when(inner)
+        def _():
+            across(i).wait()
+            add(z_pair.at[k], inner_slot.at[k], total_slot.at[k])
+            if i + slots < count:
+                grant(inner_free, middle)
+            if i >= slots:
+                pl.semaphore_wait(outer_free, 1)
+            backward(i).start()
+            result_inner(i).start()
+
+    def stage_result(i):
+        @pl.when(inner)
+        def _():
+            backward(i).wait_send()
+            result_inner(i).wait()
+
+        @pl.when(outer)
+        def _():
+            backward(i).wait_recv()
+            result_outer(i).start()
+
+    def stage_finish(i):
+        @pl.when(outer)
+        def _():
+            result_outer(i).wait()
+            if i + slots < count:
+                grant(outer_free, mate)
+
+    stages = (
+        (0, stage_send),
+        (2, stage_pair),
+        (4, stage_outward),
+        (6, stage_across),
+        (8, stage_total),
+        (10, stage_result),
+        (11, stage_finish),
+    )
+    for step in range(count + 12):
+        for lag, stage in reversed(stages):
+            if 0 <= step - lag < count:
+                stage(step - lag)
+
+
+def reduce_all(down_parts, up_parts, out_parts, qkv_parts):
+    bf16 = jnp.bfloat16
+    parts = (*down_parts, *up_parts, *out_parts, *qkv_parts)
+    hbm = pl.BlockSpec(memory_space=pl.ANY)
+    down_rows, strip = down_parts[0].shape
+    up_cols = up_parts[0].shape[1]
+    features = out_parts[0].shape[0]
+
+    def kernel(*refs):
+        reduce_kernel(
+            refs[0:4],
+            refs[4:8],
+            refs[8:12],
+            refs[12:16],
+            refs[16],
+            refs[17],
+            refs[18],
+            refs[19:22],
+            refs[22:],
+        )
+
+    slots, far_slots, rows, cols = 8, 8, 256, 512
+    dma, regular = pltpu.SemaphoreType.DMA, pltpu.SemaphoreType.REGULAR
+
+    def buffer(n):
+        return pltpu.VMEM((n, rows, cols), bf16)
+
+    return pl.pallas_call(
+        kernel,
+        out_shape=(
+            jax.ShapeDtypeStruct((2 * down_rows, strip), bf16),
+            jax.ShapeDtypeStruct((strip, 2 * up_cols), bf16),
+            jax.ShapeDtypeStruct((2 * features, strip), bf16),
+        )
+        + (jax.ShapeDtypeStruct((strip, 2 * features), bf16),) * 3,
+        in_specs=[hbm] * 16,
+        out_specs=(hbm,) * 6,
+        scratch_shapes=[
+            buffer(slots),
+            buffer(slots),
+            buffer(slots),
+            buffer(far_slots),
+            buffer(slots),
+            buffer(slots),
+            buffer(slots),
+            buffer(slots),
+            dma((slots,)),
+            dma((slots,)),
+            dma((slots,)),
+            dma((far_slots,)),
+            dma((far_slots,)),
+            dma((slots,)),
+            dma((slots,)),
+            dma((slots,)),
+            dma((slots,)),
+            dma((slots,)),
+            regular,
+            regular,
+            regular,
+            regular,
+        ],
+        compiler_params=pltpu.CompilerParams(
+            collective_id=1, has_side_effects=True, vmem_limit_bytes=40 << 20
+        ),
+        cost_estimate=pl.CostEstimate(flops=0, bytes_accessed=64 << 20, transcendentals=0),
+    )(*parts)
 
 
 def split_body(
@@ -590,11 +1167,6 @@
         size = v.shape[axis] // 2
         return lax.dynamic_slice_in_dim(v, which * size, size, axis)
 
-    def deal_rows(part):
-        part = lax.ppermute(part, ("fsdp", "tp"), x_core)
-        part = lax.all_to_all(part, "ctx", split_axis=0, concat_axis=0, tiled=True)
-        return part.reshape(own_rows, part.shape[-1])
-
     def return_rows(rows):
         part = rows.reshape(depth, block_rows, rows.shape[-1])
         part = lax.all_to_all(part, "ctx", split_axis=0, concat_axis=0, tiled=True)
@@ -614,49 +1186,13 @@
         arrived = across_y(far_mine.astype(bf16)).astype(f32)
         return near[:own_rows] + across_core(near[own_rows:].astype(bf16)).astype(f32) + arrived
 
-    def gather_weight(shard, column_split):
-        cut = 1 if column_split else 0
-        own, sent = half(shard, y, cut), half(shard, 1 - y, cut)
-        far = across_y(sent)
-        own_x, far_x = across_x(own), across_x(far)
-        axis = 1 - cut
-        shape = list(own.shape)
-        shape[axis] *= 4
-        whole = jnp.zeros(shape, shard.dtype)
-        for piece, home in ((own, f), (own_x, 2 * y + 1 - x), (far, 2 * (1 - y) + x), (far_x, 2 * (1 - y) + 1 - x)):
-            whole = lax.dynamic_update_slice_in_dim(whole, piece, home * strip, axis)
-        return whole
-
-    def z_sum(v):
-        first = lax.ppermute(v, "ctx", [(0, 1), (3, 2)])
-        pair = lax.optimization_barrier((v.astype(f32) + first.astype(f32)).astype(bf16))
-        second = lax.ppermute(pair, "ctx", [(1, 2), (2, 1)])
-        total = lax.optimization_barrier((pair.astype(f32) + second.astype(f32)).astype(bf16))
-        back = lax.ppermute(total, "ctx", [(1, 0), (2, 3)])
-        return jnp.where((z == 1) | (z == 2), total, back)
-
     def strip_of(v, home):
         return lax.dynamic_slice_in_dim(v, home * strip, strip, 1)
 
-    def reduce_weight(product, cut, join):
-        near_send = product(2 * y + 1 - x).astype(bf16)
-        far_send = product(2 * (1 - y) + 1 - x).astype(bf16)
-        near_got, far_got = across_x(near_send), across_x(far_send)
-        near = (product(f) + near_got.astype(f32)).astype(bf16)
-        far = (product(2 * (1 - y) + x) + far_got.astype(f32)).astype(bf16)
-        other = across_y(far)
-        mine, other = z_sum(near), z_sum(other)
-        return join(mine, other)
-
-    def join_on(axis):
-        def join(mine, other):
-            return jnp.where(
-                y == 0,
-                jnp.concatenate([mine, other], axis),
-                jnp.concatenate([other, mine], axis),
-            ).astype(f32)
-
-        return join
+    homes = (2 * y + 1 - x, 2 * (1 - y) + 1 - x, f, 2 * (1 - y) + x)
+
+    def products(product):
+        return tuple(product(home).astype(bf16) for home in homes)
 
     slot = x * depth + z
     length = seq_lengths[dealing[slot]]
@@ -684,23 +1220,21 @@
     cot_part = lax.dynamic_slice_in_dim(cotangent, t * depth, depth, 0)
     down_bias_part = jnp.sum(cot_part, (0, 1))
     act_part = normalize(arrived, gain_one, shift_one)[0].astype(bf16)
-    act_own = deal_rows(act_part)
-    act_near, act_far = gather_rows(act_own)
-    act_one = jnp.concatenate([act_near, act_far], 0)
-    qkv_shard = jnp.concatenate([query_weight, key_weight, value_weight], 1)
-    qkv_shard = qkv_shard.reshape(strip, 3, 2, features).transpose(0, 2, 1, 3).reshape(strip, 6 * features)
-    qkv_mat = gather_weight(qkv_shard, True)
-    out_mat = gather_weight(out_weight, False)
-    up_mat = gather_weight(up_weight, True)
-    down_mat = gather_weight(down_weight, False)
-    resid = deal_rows(arrived)
-    cot_own = deal_rows(cot_part.astype(bf16))
-    cot_low = jnp.concatenate(gather_rows(cot_own), 0)
+    qkv_mat, out_mat, up_mat, down_mat, act_one, cot_low, resid = gather_all(
+        query_weight,
+        key_weight,
+        value_weight,
+        out_weight,
+        up_weight,
+        down_weight,
+        act_part,
+        cot_part.astype(bf16),
+        arrived,
+    )
+    cot_own = cot_low[:own_rows]
 
     qkv_vec = jnp.concatenate([query_vec, jnp.zeros_like(query_vec), value_vec])
-    qkv = jnp.concatenate(
-        [(matmul(rows, qkv_mat) + qkv_vec).astype(bf16) for rows in (act_near, act_far)], 0
-    )
+    qkv = (matmul(act_one, qkv_mat) + qkv_vec).astype(bf16)
     attended, peaks = attention_forward(info, qkv, head_size)
     chip_rows = 2 * own_rows
     attn_far = matmul(attended[chip_rows:], out_mat)
@@ -728,15 +1262,10 @@
     attended_grad = back_product(hidden_low, out_mat).astype(bf16)
     qkv_low, bias_parts = attention_backward(info, qkv, attended_grad, head_size)
 
-    down_weight_grad = reduce_weight(
-        lambda home: weight_product(gelu_low, strip_of(cot_low, home)), 0, join_on(0)
-    )
-    up_weight_grad = reduce_weight(
-        lambda home: weight_product(strip_of(act_two, home), pre_low), 1, join_on(1)
-    )
-    out_weight_grad = reduce_weight(
-        lambda home: weight_product(attended, strip_of(hidden_low, home)), 0, join_on(0)
-    )
+    down_parts = products(lambda home: weight_product(gelu_low, strip_of(cot_low, home)))
+    up_parts = products(lambda home: weight_product(strip_of(act_two, home), pre_low))
+    out_parts = products(lambda home: weight_product(attended, strip_of(hidden_low, home)))
+    qkv_parts = products(lambda home: weight_product(strip_of(act_one, home), qkv_low))
     mlp_far = matmul(gelu_low[chip_rows:], down_mat)
     mlp_near = matmul(gelu_low[:chip_rows], down_mat)
     layer_output = hidden + scatter_rows(mlp_near, mlp_far) + down_vec
@@ -751,16 +1280,9 @@
     )
     final_grad = return_rows((hidden_grad + input_in).astype(bf16))
 
-    def join_qkv(mine, other):
-        mine, other = mine.reshape(strip, 3, features), other.reshape(strip, 3, features)
-        both = jnp.where(
-            y == 0, jnp.concatenate([mine, other], 2), jnp.concatenate([other, mine], 2)
-        ).astype(f32)
-        return both[:, 0], both[:, 1], both[:, 2]
-
-    query_weight_grad, key_weight_grad, value_weight_grad = reduce_weight(
-        lambda home: weight_product(strip_of(act_one, home), qkv_low), 1, join_qkv
-    )
+    sums = reduce_all(down_parts, up_parts, out_parts, qkv_parts)
+    down_weight_grad, up_weight_grad, out_weight_grad = [v.astype(f32) for v in sums[:3]]
+    query_weight_grad, key_weight_grad, value_weight_grad = [v.astype(f32) for v in sums[3:]]
 
     def placed(v, which):
         whole = jnp.zeros((4,) + v.shape, f32)

time: 1360 us -> 1170 us (0.86)
  Pallas kernels: 26.5 us -> 561 us
  waiting for transfers between devices: 661 us -> 242 us
  starting transfers between devices: 171 us -> 45.3 us
  local copies, waits for them, and re-layouts: 99.8 us -> 20.9 us
  other arithmetic: 116 us -> 61.3 us
  blocking collectives: 93.3 us -> 54.7 us
    pallas_call x0 -> x2, Pallas kernels: none -> 534 us  [the longest x1 306 us: reduce_all(): pl.pallas_call(kernel, out_shape=(jax.ShapeDtypeStruct((2 * down_rows, st...]
    ppermute x43 -> x0, waiting for transfers between devices: 510 us -> none  [the longest x16 247 us: across_x(): return lax.ppermute(v, 'fsdp', over_x)]
    ppermute x43 -> x0, starting transfers between devices: 111 us -> none  [the longest x8 38.1 us: z_sum(): first = lax.ppermute(v, 'ctx', [(0, 1), (3, 2)])]
    psum x1, waiting for transfers between devices: 42.8 us -> 117 us  [split_body(): flat = lax.psum(flat, ('fsdp', 'ctx', 'tp'))]
    dynamic_update_slice x16 -> x0, local copies, waits for them, and re-layouts: 41.6 us -> none  [gather_weight(): whole = lax.dynamic_update_slice_in_dim(whole, piece, home * strip, axis)]
    convert_element_type x20 -> x6, other arithmetic: 52.6 us -> 15.4 us  [split_body(): v.astype(f32)]
    all_gather x1, blocking collectives: 43.4 us -> 8.14 us  [split_body(): vectors = lax.all_gather(vectors, 'fsdp', axis=0, tiled=False)]
    ppermute x16 -> x6, starting transfers between devices: 21.3 us -> 4.29 us  [across_y(): return lax.ppermute(v, 'fsdp', over_y)]
  transfers between devices with their start and end apart: 85 -> 25, of which waited for: 29 -> 10; matrix products, arithmetic and copies ran while one was open for 20% -> 11% of each run, Pallas kernels for 2% -> 28%
where the time goes in v2:
time: 1170 us; the launch traced here: 1160 us
  Pallas kernels  561 us (48%)
  waiting for transfers between devices  242 us (21%)
  matrix products  151 us (13%)
  other arithmetic  61.3 us (5%)
  blocking collectives  54.7 us (5%)
  starting transfers between devices  45.3 us (4%)
  between operations  25.7 us (2%)
  local copies, waits for them, and re-layouts  20.9 us (2%)
    pallas_call x1, Pallas kernels, reduce_all(): pl.pallas_call(kernel, out_shape=(jax.ShapeDtypeStruct((2 * down_rows, st...  306 us
    pallas_call x1, Pallas kernels, gather_all(): pl.pallas_call(gather_kernel, out_shape=(jax.ShapeDtypeStruct((width, 3 *...  228 us
    psum x1, waiting for transfers between devices, split_body(): flat = lax.psum(flat, ('fsdp', 'ctx', 'tp'))  117 us
    ppermute x6, waiting for transfers between devices, across_y(): return lax.ppermute(v, 'fsdp', over_y)  110 us
    dot_general x16, matrix products, weight_product(): jnp.einsum('td,te->de', left, right, preferred_element_type=jnp.float32)  57.5 us
    dot_general x6, matrix products, back_product(): jnp.einsum('te,de->td', left, right, preferred_element_type=jnp.float32)  47.4 us
    dot_general x6, matrix products, matmul(): return jnp.dot(left, right, preferred_element_type=jnp.float32)  46.2 us
    pmax x1, blocking collectives, split_body(): peak_all = lax.pmax(my_peaks, ('fsdp', 'ctx'))  36.9 us
  transfers between devices with their start and end apart: 25, of which 10 were waited for; matrix products, arithmetic and copies ran while one was open for 11% of the time, Pallas kernels for 28%

profile of v2, /device:TPU:0, one launch (start us, length us, event | category | flops | bytes accessed | tf_op | source)
XLA Modules:
  0.0 1161.3 jit_solution(2774592735798392967)
XLA Ops:
  19.3 9.6 all_gather.9
  38.1 8.1 all-gather.1
  50.9 228.3 %shard_map.347 = (bf16[2048,1536]{1,0:T(8,128)(2,1)}, bf16[512,2048]{1,0:T(8,128)(2,1)}, bf16[2048,2048]{1,0:T(8,128)(2,1)}, bf16[2048,2048]{1,0:T(8,128)(2,1)},...) custom-call(bf16[512,1024]{1,0:T(8,128)(2,1)} %q_ref.1, bf16[512,1024]{1,0:T(8,128)(2,1)} %k_ref.1, ...), custom_call_target="tpu_custom_call" | custom-call | bytes 67108864 | tf_op jit(solution)/shard_map/pallas_call | solution.py:786
  279.1 10.0 add_convert_fusion.q_ref.k_ref.v_ref
  289.2 10.6 shard_map.348
  301.2 10.8 collective-permute-start.1
  316.6 24.7 %collective-permute-done.2 = bf16[256,2048]{1,0:T(8,128)(2,1)} collective-permute-done((bf16[256,2048]{1,0:T(8,128)(2,1)}, bf16[256,2048]{1,0:T(8,128)(2,1)}, u32[]{:S(2)}, u32[]{:S(2)}) %collective-permute-start.2) | collective-permute-done | bytes 1048608 | tf_op jit(solution)/shard_map/ppermute | solution.py:1161
  347.6 23.9 %collective-permute-done.4 = bf16[256,2048]{1,0:T(8,128)(2,1)} collective-permute-done((bf16[256,2048]{1,0:T(8,128)(2,1)}, bf16[256,2048]{1,0:T(8,128)(2,1)}, u32[]{:S(2)}, u32[]{:S(2)}) %collective-permute-start.4) | collective-permute-done | bytes 1048608 | tf_op jit(solution)/shard_map/ppermute | solution.py:1161
  371.5 36.9 %pmax.7 = f32[8]{0:T(128)S(1)} all-reduce(f32[8]{0:T(128)S(1)} %reshape.302), channel_id=1, replica_groups=mesh['fsdp'=4,'ctx'=4,'tp'=2] {'fsdp','ctx'}, use_global_device_ids=true, to_apply=%region_18.19 | all-reduce | flops 8 | bytes 64 | tf_op jit(solution)/shard_map/pmax | solution.py:1312
  415.2 17.7 %multiply_convert_fusion = (bf16[1024,2048]{1,0:T(8,128)(2,1)}, f32[1024,2048]{1,0:T(8,128)}) fusion(f32[2048]{0:T(1024)S(1)} %dynamic-slice_convert_fusion.1, bf16[2048,2048]{1,0:T(8,128)(2,1)} %get-tuple-element.90, bf16[256,2048]{1,0:T(8,128)(2,1)} %collective-permute-done.5, bf16[256,2048]{1,0:T(8,128)(2,1)} %collective-permute-done.4, ...), kind=kOutput, calls=%fused_computation.6 | convolution fusion | flops 8619294720 | bytes 25174016 | tf_op jit(solution)/shard_map/dot_general | solution.py:41
  432.9 15.1 %fusion.76 = (f32[2048]{0:T(1024)S(1)}, bf16[1024,2048]{1,0:T(8,128)(2,1)S(1)}) fusion(f32[1024,2048]{1,0:T(8,128)} %get-tuple-element.153, f32[2048]{0:T(1024)S(1)} %dynamic-slice_convert_fusion.1, bf16[1024,2048]{1,0:T(8,128)(2,1)S(1)} %copy-done.26, bf16[2048,2048]{1,0:T(8,128)(2,1)} %get-tuple-element.91), kind=kOutput, calls=%fused_computation.175 | convolution fusion | flops 8615098368 | bytes 25182208 | tf_op jit(solution)/shard_map/te,de->td/dot_general | solution.py:49
  448.0 8.5 fusion.8
  456.5 7.4 fusion.11
  463.9 9.1 fusion.14
  473.0 6.9 fusion.20
  506.2 18.9 %collective-permute-done.13 = bf16[256,2048]{1,0:T(8,128)(2,1)} collective-permute-done((bf16[256,2048]{1,0:T(8,128)(2,1)}, bf16[256,2048]{1,0:T(8,128)(2,1)}, u32[]{:S(2)}, u32[]{:S(2)}) %collective-permute-start.13) | collective-permute-done | bytes 1048608 | tf_op jit(solution)/shard_map/ppermute | solution.py:1161
  528.6 18.1 %collective-permute-done.8 = bf16[256,2048]{1,0:T(8,128)(2,1)} collective-permute-done((bf16[256,2048]{1,0:T(8,128)(2,1)}, bf16[256,2048]{1,0:T(8,128)(2,1)}, u32[]{:S(2)}, u32[]{:S(2)}) %collective-permute-start.8) | collective-permute-done | bytes 1048608 | tf_op jit(solution)/shard_map/ppermute | solution.py:1161
  551.2 5.0 convolution_convert_fusion.2.refs_5_
  560.6 6.4 convolution_convert_fusion.1.refs_6_
  567.0 7.9 collective-permute-done.15
  574.9 5.0 convolution_convert_fusion.4.refs_3_
  580.0 5.1 convolution_convert_fusion.refs_7_
  585.9 9.4 collective-permute-start.9
  599.6 16.3 %shard_map.349 = (bf16[1024,1536]{1,0:T(8,128)(2,1)S(1)}, f32[4,8,128]{2,1,0:T(8,128)S(1)}) custom-call(s32[5]{0:T(128)S(1)} %pad_add_fusion.info, bf16[1024,1536]{1,0:T(8,128)(2,1)} %copy-done, bf16[1024,1536]{1,0:T(8,128)(2,1)} %copy-done, bf16[1024,1536]{1,0:T(8,128)(2,1)} %copy-done, bf16[1024,512]{1,0:T(8,128)(2,1)S(1)} %convolution_convert_fusion.12.g_ref), custom_call_target="tpu_custom_call" | custom-call | flops 5368709120 | bytes 7340032 | tf_op jit(solution)/shard_map/pallas_call | solution.py:516
  615.9 6.7 fusion.26
  622.9 5.6 fusion.28
  638.1 16.5 %collective-permute-done.19 = bf16[256,2048]{1,0:T(8,128)(2,1)S(1)} collective-permute-done((bf16[256,2048]{1,0:T(8,128)(2,1)S(1)}, bf16[256,2048]{1,0:T(8,128)(2,1)S(1)}, u32[]{:S(2)}, u32[]{:S(2)}) %collective-permute-start.19) | collective-permute-done | bytes 1048608 | tf_op jit(solution)/shard_map/ppermute | solution.py:1161
  674.2 13.1 %all-to-all-done.1 = bf16[4,64,2048]{2,1,0:T(8,128)(2,1)} async-done(((bf16[4,64,2048]{2,1,0:T(8,128)(2,1)}), bf16[4,64,2048]{2,1,0:T(8,128)(2,1)}, u32[]{:S(2)}, u32[]{:S(2)}) %all-to-all-start.1) | async-done | bytes 1048608 | tf_op jit(solution)/shard_map/all_to_all | solution.py:1172
  687.3 9.9 collective-permute-start.20
  701.2 305.8 %shard_map.350 = (bf16[4096,512]{1,0:T(8,128)(2,1)}, bf16[512,4096]{1,0:T(8,128)(2,1)}, bf16[1024,512]{1,0:T(8,128)(2,1)S(1)}, bf16[512,1024]{1,0:T(8,128)(2,1)S...) custom-call(bf16[2048,512]{1,0:T(8,128)(2,1)} %convolution_convert_fusion.7.refs_0_, ...), custom_call_target="tpu_custom_call" | custom-call | bytes 67108864 | tf_op jit(solution)/shard_map/pallas_call | solution.py:1076
  1017.8 4.6 convert_element_type.247
  1028.6 116.7 %all-reduce.2.cloned.1.call-done = f32[24576]{0:T(1024)} async-done(((f32[24576]{0:T(1024)}), f32[24576]{0:T(1024)}) %all-reduce.2.cloned.1.call-update) | async-done | bytes 98320 | tf_op jit(solution)/shard_map/psum | solution.py:1298
  (253 shorter events, 137.2 us)
Async XLA Ops:
  29.0 20.4 %copy-start.27 = (f32[1,2048]{1,0:T(1,128)}, f32[1,2048]{1,0:T(1,128)S(1)}, u32[]{:S(2)}) copy-start(f32[1,2048]{1,0:T(1,128)S(1)} %get-tuple-element.136) | copy-start | bytes 24580
  301.2 13.0 %collective-permute-start.1 = (bf16[256,2048]{1,0:T(8,128)(2,1)S(1)}, bf16[256,2048]{1,0:T(8,128)(2,1)S(1)}, u32[]{:S(2)}, u32[]{:S(2)}) collective-permute-start(bf16[256,2048]{1,0:T(8,128)(2,1)S(1)} %slice.371), channel_id=1, source_target_pairs={{0,1},{1,0},{2,3},{3,2},{4,5},{5,4},{6,7},{7,6},{8,9},{9,8},{10,11... | collective-permute-start | bytes 3145736 | tf_op jit(solution)/shard_map/ppermute | solution.py:1164
  313.4 3.2 collective-permute-start
  315.7 25.6 %collective-permute-start.2 = (bf16[256,2048]{1,0:T(8,128)(2,1)}, bf16[256,2048]{1,0:T(8,128)(2,1)}, u32[]{:S(2)}, u32[]{:S(2)}) collective-permute-start(bf16[256,2048]{1,0:T(8,128)(2,1)} %fusion.22), channel_id=1, source_target_pairs={{0,16},{16,0},{8,24},{24,8},{1,17},{17,1},{9,25},{25,9},{2,18},{18... | collective-permute-start | bytes 3145736 | tf_op jit(solution)/shard_map/ppermute | solution.py:1161
  316.6 28.4 %copy-start.30 = (f32[256]{0:T(256)}, f32[256]{0:T(256)S(1)}, u32[]{:S(2)}) copy-start(f32[256]{0:T(256)S(1)} %broadcast_multiply_fusion.3) | copy-start | bytes 3076
  345.0 66.6 %copy-start.20 = (bf16[512,1024]{1,0:T(8,128)(2,1)S(1)}, bf16[512,1024]{1,0:T(8,128)(2,1)}, u32[]{:S(2)}) copy-start(bf16[512,1024]{1,0:T(8,128)(2,1)} %q_ref.1) | copy-start | bytes 3145732
  346.8 24.7 %collective-permute-start.4 = (bf16[256,2048]{1,0:T(8,128)(2,1)}, bf16[256,2048]{1,0:T(8,128)(2,1)}, u32[]{:S(2)}, u32[]{:S(2)}) collective-permute-start(bf16[256,2048]{1,0:T(8,128)(2,1)} %add_convert_fusion.2), channel_id=1, source_target_pairs={{0,16},{16,0},{8,24},{24,8},{1,17},{17,1},{9,25},{25,9},{2,18},{18... | collective-permute-start | bytes 3145736 | tf_op jit(solution)/shard_map/ppermute | solution.py:1161
  347.6 67.6 %collective-permute-start.3 = (bf16[256,2048]{1,0:T(8,128)(2,1)}, bf16[256,2048]{1,0:T(8,128)(2,1)}, u32[]{:S(2)}, u32[]{:S(2)}) collective-permute-start(bf16[256,2048]{1,0:T(8,128)(2,1)} %add_convert_fusion.2), channel_id=1, source_target_pairs={{0,1},{1,0},{2,3},{3,2},{4,5},{5,4},{6,7},{7,6},{8,9},{9,8},{10,11... | collective-permute-start | bytes 3145736 | tf_op jit(solution)/shard_map/ppermute | solution.py:1164
  371.5 43.7 %collective-permute-start.5 = (bf16[256,2048]{1,0:T(8,128)(2,1)}, bf16[256,2048]{1,0:T(8,128)(2,1)}, u32[]{:S(2)}, u32[]{:S(2)}) collective-permute-start(bf16[256,2048]{1,0:T(8,128)(2,1)} %collective-permute-done.4), channel_id=1, source_target_pairs={{0,1},{1,0},{2,3},{3,2},{4,5},{5,4},{6,7},{7,6},{8,9},{9,8},{10,11... | collective-permute-start | bytes 3145736 | tf_op jit(solution)/shard_map/ppermute | solution.py:1164
  408.5 24.4 %copy-start.38 = (f32[8]{0:T(128)}, f32[8]{0:T(128)S(1)}, u32[]{:S(2)}) copy-start(f32[8]{0:T(128)S(1)} %pmax.7) | copy-start | bytes 100
  448.0 54.2 %copy-start.39 = (bf16[1024,2048]{1,0:T(8,128)(2,1)}, bf16[1024,2048]{1,0:T(8,128)(2,1)S(1)}, u32[]{:S(2)}) copy-start(bf16[1024,2048]{1,0:T(8,128)(2,1)S(1)} %get-tuple-element.117) | copy-start | bytes 12582916
  463.8 20.0 %copy-start.25 = (f32[512,2048]{1,0:T(8,128)}, f32[512,2048]{1,0:T(8,128)S(1)}, u32[]{:S(2)}) copy-start(f32[512,2048]{1,0:T(8,128)S(1)} %fusion.11) | copy-start | bytes 12582916
  483.8 13.7 %collective-permute-start.12 = (bf16[256,2048]{1,0:T(8,128)(2,1)S(1)}, bf16[256,2048]{1,0:T(8,128)(2,1)S(1)}, u32[]{:S(2)}, u32[]{:S(2)}) collective-permute-start(bf16[256,2048]{1,0:T(8,128)(2,1)S(1)} %slice.367), channel_id=1, source_target_pairs={{0,1},{1,0},{2,3},{3,2},{4,5},{5,4},{6,7},{7,6},{8,9},{9,8},{10,11... | collective-permute-start | bytes 3145736 | tf_op jit(solution)/shard_map/ppermute | solution.py:1164
  485.0 21.2 %collective-permute-start.11 = (bf16[256,2048]{1,0:T(8,128)(2,1)}, bf16[256,2048]{1,0:T(8,128)(2,1)}, u32[]{:S(2)}, u32[]{:S(2)}) collective-permute-start(bf16[256,2048]{1,0:T(8,128)(2,1)} %slice.368), channel_id=1, source_target_pairs={{0,1},{1,0},{2,3},{3,2},{4,5},{5,4},{6,7},{7,6},{8,9},{9,8},{10,11... | collective-permute-start | bytes 3145736 | tf_op jit(solution)/shard_map/ppermute | solution.py:1164
  485.7 13.7 %collective-permute-start.7 = (bf16[256,2048]{1,0:T(8,128)(2,1)S(1)}, bf16[256,2048]{1,0:T(8,128)(2,1)S(1)}, u32[]{:S(2)}, u32[]{:S(2)}) collective-permute-start(bf16[256,2048]{1,0:T(8,128)(2,1)S(1)} %slice.369), channel_id=1, source_target_pairs={{0,1},{1,0},{2,3},{3,2},{4,5},{5,4},{6,7},{7,6},{8,9},{9,8},{10,11... | collective-permute-start | bytes 3145736 | tf_op jit(solution)/shard_map/ppermute | solution.py:1164
  486.9 41.6 %collective-permute-start.6 = (bf16[256,2048]{1,0:T(8,128)(2,1)}, bf16[256,2048]{1,0:T(8,128)(2,1)S(1)}, u32[]{:S(2)}, u32[]{:S(2)}) collective-permute-start(bf16[256,2048]{1,0:T(8,128)(2,1)} %slice.370), channel_id=1, source_target_pairs={{0,1},{1,0},{2,3},{3,2},{4,5},{5,4},{6,7},{7,6},{8,9},{9,8},{10,11... | collective-permute-start | bytes 3145736 | tf_op jit(solution)/shard_map/ppermute | solution.py:1164
  498.8 26.3 %collective-permute-start.13 = (bf16[256,2048]{1,0:T(8,128)(2,1)}, bf16[256,2048]{1,0:T(8,128)(2,1)}, u32[]{:S(2)}, u32[]{:S(2)}) collective-permute-start(bf16[256,2048]{1,0:T(8,128)(2,1)} %fusion.7), channel_id=1, source_target_pairs={{0,16},{16,0},{8,24},{24,8},{1,17},{17,1},{9,25},{25,9},{2,18},{18... | collective-permute-start | bytes 3145736 | tf_op jit(solution)/shard_map/ppermute | solution.py:1161
  500.8 45.9 %collective-permute-start.8 = (bf16[256,2048]{1,0:T(8,128)(2,1)}, bf16[256,2048]{1,0:T(8,128)(2,1)}, u32[]{:S(2)}, u32[]{:S(2)}) collective-permute-start(bf16[256,2048]{1,0:T(8,128)(2,1)} %fusion.13), channel_id=1, source_target_pairs={{0,16},{16,0},{8,24},{24,8},{1,17},{17,1},{9,25},{25,9},{2,18},{18... | collective-permute-start | bytes 3145736 | tf_op jit(solution)/shard_map/ppermute | solution.py:1161
  506.2 40.5 %copy-start.24 = (f32[512,2048]{1,0:T(8,128)S(1)}, f32[512,2048]{1,0:T(8,128)}, u32[]{:S(2)}) copy-start(f32[512,2048]{1,0:T(8,128)} %copy-done.23) | copy-start | bytes 12582916
  550.5 24.4 %collective-permute-start.15 = (bf16[256,2048]{1,0:T(8,128)(2,1)S(1)}, bf16[256,2048]{1,0:T(8,128)(2,1)}, u32[]{:S(2)}, u32[]{:S(2)}) collective-permute-start(bf16[256,2048]{1,0:T(8,128)(2,1)S(1)} %convert_element_type.217), channel_id=1, source_target_pairs={{0,16},{16,0},{8,24},{24,8},{1,17},{17,1},{9,25},{25,9},{2,18},{18... | collective-permute-start | bytes 3145736 | tf_op jit(solution)/shard_map/ppermute | solution.py:1161
  556.2 29.8 %all-to-all-start = ((bf16[4,64,2048]{2,1,0:T(8,128)(2,1)}), bf16[4,64,2048]{2,1,0:T(8,128)(2,1)}, u32[]{:S(2)}, u32[]{:S(2)}) async-start(bf16[4,64,2048]{2,1,0:T(8,128)(2,1)} %bitcast.18), calls=%async_computation | async-start | bytes 2097152 | tf_op jit(solution)/shard_map/all_to_all | solution.py:1172
  567.0 28.4 %collective-permute-start.14 = (bf16[256,2048]{1,0:T(8,128)(2,1)S(1)}, bf16[256,2048]{1,0:T(8,128)(2,1)}, u32[]{:S(2)}, u32[]{:S(2)}) collective-permute-start(bf16[256,2048]{1,0:T(8,128)(2,1)S(1)} %convert_element_type.217), channel_id=1, source_target_pairs={{0,1},{1,0},{2,3},{3,2},{4,5},{5,4},{6,7},{7,6},{8,9},{9,8},{10,11... | collective-permute-start | bytes 3145736 | tf_op jit(solution)/shard_map/ppermute | solution.py:1164
  574.9 20.4 %collective-permute-start.16 = (bf16[256,2048]{1,0:T(8,128)(2,1)}, bf16[256,2048]{1,0:T(8,128)(2,1)}, u32[]{:S(2)}, u32[]{:S(2)}) collective-permute-start(bf16[256,2048]{1,0:T(8,128)(2,1)} %collective-permute-done.15), channel_id=1, source_target_pairs={{0,1},{1,0},{2,3},{3,2},{4,5},{5,4},{6,7},{7,6},{8,9},{9,8},{10,11... | collective-permute-start | bytes 3145736 | tf_op jit(solution)/shard_map/ppermute | solution.py:1164
  585.9 82.4 %collective-permute-start.9 = (bf16[4,64,2048]{2,1,0:T(8,128)(2,1)}, bf16[4,64,2048]{2,1,0:T(8,128)(2,1)}, u32[]{:S(2)}, u32[]{:S(2)}) collective-permute-start(bf16[4,64,2048]{2,1,0:T(8,128)(2,1)} %all-to-all-done), channel_id=1, source_target_pairs={{0,0},{1,8},{8,1},{9,9},{16,16},{17,24},{24,17},{25,25},{2,2},{3,1... | collective-permute-start | bytes 3145736 | tf_op jit(solution)/shard_map/ppermute | solution.py:1173
  622.8 6.4 collective-permute-start.18
  628.6 9.5 collective-permute-start.17
  629.5 25.2 %collective-permute-start.19 = (bf16[256,2048]{1,0:T(8,128)(2,1)S(1)}, bf16[256,2048]{1,0:T(8,128)(2,1)S(1)}, u32[]{:S(2)}, u32[]{:S(2)}) collective-permute-start(bf16[256,2048]{1,0:T(8,128)(2,1)S(1)} %fusion.5), channel_id=1, source_target_pairs={{0,16},{16,0},{8,24},{24,8},{1,17},{17,1},{9,25},{25,9},{2,18},{18... | collective-permute-start | bytes 3145736 | tf_op jit(solution)/shard_map/ppermute | solution.py:1161
  657.6 29.7 %all-to-all-start.1 = ((bf16[4,64,2048]{2,1,0:T(8,128)(2,1)}), bf16[4,64,2048]{2,1,0:T(8,128)(2,1)}, u32[]{:S(2)}, u32[]{:S(2)}) async-start(bf16[4,64,2048]{2,1,0:T(8,128)(2,1)} %bitcast.22), calls=%async_computation.1 | async-start | bytes 2097152 | tf_op jit(solution)/shard_map/all_to_all | solution.py:1172
  661.8 483.5 %all-reduce.2.cloned.1.call-start = ((), (), s32[]{:S(2)}) async-start(), calls=%async_computation.2 | async-start | bytes 196608 | tf_op jit(solution)/shard_map/psum | solution.py:1298
  668.3 354.1 %collective-permute-start.10 = (bf16[4,64,2048]{2,1,0:T(8,128)(2,1)}, bf16[4,64,2048]{2,1,0:T(8,128)(2,1)}, u32[]{:S(2)}, u32[]{:S(2)}) collective-permute-start(bf16[4,64,2048]{2,1,0:T(8,128)(2,1)} %collective-permute-done.9), channel_id=1, source_target_pairs={{0,1},{1,0},{2,3},{3,2},{4,5},{5,4},{6,7},{7,6},{8,9},{9,8},{10,11... | collective-permute-start | bytes 3145736 | tf_op jit(solution)/shard_map/ppermute | solution.py:1164
  687.3 338.5 %collective-permute-start.20 = (bf16[4,64,2048]{2,1,0:T(8,128)(2,1)}, bf16[4,64,2048]{2,1,0:T(8,128)(2,1)}, u32[]{:S(2)}, u32[]{:S(2)}) collective-permute-start(bf16[4,64,2048]{2,1,0:T(8,128)(2,1)} %all-to-all-done.1), channel_id=1, source_target_pairs={{0,0},{1,8},{8,1},{9,9},{16,16},{17,24},{24,17},{25,25},{2,2},{3,1... | collective-permute-start | bytes 3145736 | tf_op jit(solution)/shard_map/ppermute | solution.py:1173
  1025.8 123.9 %collective-permute-start.21 = (bf16[4,64,2048]{2,1,0:T(8,128)(2,1)}, bf16[4,64,2048]{2,1,0:T(8,128)(2,1)S(1)}, u32[]{:S(2)}, u32[]{:S(2)}) collective-permute-start(bf16[4,64,2048]{2,1,0:T(8,128)(2,1)} %collective-permute-done.20), channel_id=1, source_target_pairs={{0,1},{1,0},{2,3},{3,2},{4,5},{5,4},{6,7},{7,6},{8,9},{9,8},{10,11... | collective-permute-start | bytes 3145736 | tf_op jit(solution)/shard_map/ppermute | solution.py:1164
  (37 other events, 367.6 us)
Sparse Core Ops, SparseCore 0:
  1025.9 119.3 all-reduce.1

commit v3 on v2

--- a/solution.py
+++ b/solution.py
@@ -457,86 +457,6 @@
     return attended, peaks[:, 0, 0]
 
 
-def attention_backward_kernel(
-    ranks, heads, info, q_ref, k_ref, v_ref, g_ref, out_ref, bias_ref, keys, values, key_sum, value_sum
-):
-    tokens, size = keys.shape
-    rows = tokens // ranks
-    scale = 1.0 / math.sqrt(size)
-    head = pl.program_id(0)
-    length = info[ranks]
-
-    def lanes(k):
-        return pl.ds(pl.multiple_of((k * heads + head) * size, size), size)
-
-    for block in range(ranks):
-        at = pl.ds(pl.multiple_of(info[block], rows), rows)
-        keys[pl.ds(block * rows, rows), :] = k_ref[at, :]
-        values[pl.ds(block * rows, rows), :] = v_ref[at, :]
-    key_sum[...] = jnp.zeros_like(key_sum)
-    value_sum[...] = jnp.zeros_like(value_sum)
-    query_bias = jnp.zeros((1, size), jnp.float32)
-    for block in range(ranks):
-        at = pl.ds(pl.multiple_of(info[block], rows), rows)
-        extent = (block + 1) * rows
-        part = pl.ds(0, extent)
-        queries, grads = q_ref[at, :], g_ref[at, :]
-        probs, _ = attention_probs(queries, keys[part, :], block, length)
-        prob_grad = lax.dot_general(
-            grads, values[part, :], (((1,), (1,)), ((), ())), preferred_element_type=jnp.float32
-        )
-        inner = jnp.sum(probs * prob_grad, -1, keepdims=True)
-        score_grad = (probs * (prob_grad - inner)).astype(jnp.bfloat16)
-        query_grad = (
-            jnp.dot(score_grad, keys[part, :], preferred_element_type=jnp.float32) * scale
-        )
-        query_bias += jnp.sum(query_grad, 0, keepdims=True)
-        out_ref[at, lanes(0)] = query_grad.astype(out_ref.dtype)
-        key_sum[part, :] += lax.dot_general(
-            score_grad, queries, (((0,), (0,)), ((), ())), preferred_element_type=jnp.float32
-        )
-        value_sum[part, :] += lax.dot_general(
-            probs.astype(jnp.bfloat16), grads, (((0,), (0,)), ((), ())), preferred_element_type=jnp.float32
-        )
-    for block in range(ranks):
-        at = pl.ds(pl.multiple_of(info[block], rows), rows)
-        out_ref[at, lanes(1)] = (key_sum[pl.ds(block * rows, rows), :] * scale).astype(out_ref.dtype)
-        out_ref[at, lanes(2)] = value_sum[pl.ds(block * rows, rows), :].astype(out_ref.dtype)
-    bias_ref[0, pl.ds(0, 1), :] = query_bias
-    bias_ref[0, pl.ds(1, 1), :] = jnp.sum(value_sum[...], 0, keepdims=True)
-
-
-def attention_backward(info, qkv, grads, head_size):
-    tokens, features = grads.shape
-    heads, ranks = features // head_size, info.shape[0] - 1
-
-    def part(k):
-        return pl.BlockSpec((tokens, head_size), lambda h, info: (0, k * heads + h))
-
-    return pl.pallas_call(
-        functools.partial(attention_backward_kernel, ranks, heads),
-        out_shape=(
-            jax.ShapeDtypeStruct((tokens, 3 * features), jnp.bfloat16),
-            jax.ShapeDtypeStruct((heads, 8, head_size), jnp.float32),
-        ),
-        grid_spec=pltpu.PrefetchScalarGridSpec(
-            num_scalar_prefetch=1,
-            grid=(heads,),
-            in_specs=[part(0), part(1), part(2), part(0)],
-            out_specs=(
-                pl.BlockSpec((tokens, 3 * features), lambda h, info: (0, 0)),
-                pl.BlockSpec((1, 8, head_size), lambda h, info: (h, 0, 0)),
-            ),
-            scratch_shapes=[pltpu.VMEM((tokens, head_size), jnp.bfloat16)] * 2
-            + [pltpu.VMEM((tokens, head_size), jnp.float32)] * 2,
-        ),
-        compiler_params=pltpu.CompilerParams(vmem_limit_bytes=48 << 20),
-        cost_estimate=pl.CostEstimate(
-            flops=10 * tokens * tokens * features, bytes_accessed=14 * tokens * features, transcendentals=0
-        ),
-    )(info, qkv, qkv, qkv, grads)
-
-
 def entry_barrier(targets):
     barrier = pltpu.get_barrier_semaphore()
     for target in targets:
@@ -810,9 +730,53 @@
     )(query_weight, key_weight, value_weight, out_weight, up_weight, down_weight, act, cot, res)
 
 
-def reduce_kernel(
-    down_parts, up_parts, out_parts, qkv_parts, down_sum, up_sum, out_sum, qkv_sums, scratch
-):
+def remote_copy(src, dst, send, recv, target):
+    return pltpu.make_async_remote_copy(
+        src_ref=src,
+        dst_ref=dst,
+        send_sem=send,
+        recv_sem=recv,
+        device_id=target,
+        device_id_type=pl.DeviceIdType.MESH,
+    )
+
+
+def grant(semaphore, target):
+    pl.semaphore_signal(semaphore, inc=1, device_id=target, device_id_type=pl.DeviceIdType.MESH)
+
+
+def aligned(start, size):
+    return pl.ds(pl.multiple_of(start, 128), size)
+
+
+class Place:
+    def __init__(self, depth):
+        self.depth = depth
+        f = lax.axis_index("fsdp")
+        z = lax.axis_index("ctx")
+        t = lax.axis_index("tp")
+        y, x = f // 2, f % 2
+        self.f, self.z, self.t, self.y, self.x = f, z, t, y, x
+        self.over_x = {"fsdp": 2 * y + 1 - x, "ctx": z, "tp": t}
+        self.over_y = {"fsdp": 2 * (1 - y) + x, "ctx": z, "tp": t}
+        self.over_core = {"fsdp": f, "ctx": z, "tp": 1 - t}
+        self.mate = {"fsdp": f, "ctx": z + 1 - 2 * (z % 2), "tp": t}
+        self.middle = {"fsdp": f, "ctx": 3 - z, "tp": t}
+        self.hop = {"fsdp": f, "ctx": lax.rem(z + 2, 4), "tp": t}
+        self.homes = (2 * y + 1 - x, 2 * (1 - y) + 1 - x, f, 2 * (1 - y) + x)
+
+    def row_target(self, k):
+        return {"fsdp": 2 * self.y + self.t, "ctx": k, "tp": self.x}
+
+    def row_targets(self):
+        others = [self.row_target(lax.rem(self.z + k, self.depth)) for k in range(1, self.depth)]
+        return others + [{"fsdp": 2 * self.y + 1 - self.x, "ctx": self.z, "tp": 1 - self.t}]
+
+    def block_place(self, block):
+        return 2 * jnp.where(self.y == block // 2, 0, 1) + jnp.where(self.t == block % 2, 0, 1)
+
+
+def reduce_stages(p, groups, scratch):
     (
         x_slot,
         own_slot,
@@ -837,106 +801,48 @@
         outer_free,
         inner_free,
     ) = scratch
-    f = lax.axis_index("fsdp")
-    z = lax.axis_index("ctx")
-    t = lax.axis_index("tp")
-    y, x = f // 2, f % 2
+    y, z = p.y, p.z
     outer = (z == 0) | (z == 3)
     inner = (z == 1) | (z == 2)
-    over_x = {"fsdp": 2 * y + 1 - x, "ctx": z, "tp": t}
-    over_y = {"fsdp": 2 * (1 - y) + x, "ctx": z, "tp": t}
-    mate = {"fsdp": f, "ctx": z + 1 - 2 * (z % 2), "tp": t}
-    middle = {"fsdp": f, "ctx": 3 - z, "tp": t}
-    entry_barrier([over_x, over_y, mate, middle])
     slots, rows, cols = x_slot.shape
-
-    def remote(src, dst, send, recv, target):
-        return pltpu.make_async_remote_copy(
-            src_ref=src,
-            dst_ref=dst,
-            send_sem=send,
-            recv_sem=recv,
-            device_id=target,
-            device_id_type=pl.DeviceIdType.MESH,
-        )
-
-    def grant(semaphore, target):
-        pl.semaphore_signal(semaphore, inc=1, device_id=target, device_id_type=pl.DeviceIdType.MESH)
-
-    def at(start, size):
-        return pl.ds(pl.multiple_of(start, 128), size)
-
-    near_items, far_items = [], []
-
-    def add_items(parts, row_count, col_count, place):
+    items = []
+    for parts, row_count, col_count, place in groups:
         near_send, far_send, near_own, far_own = parts
         for r in range(row_count):
             for c in range(col_count):
                 cut = (pl.ds(r * rows, rows), pl.ds(c * cols, cols))
-                near_items.append((near_send.at[cut], near_own.at[cut], place(y, r, c)))
-                far_items.append((far_send.at[cut], far_own.at[cut], place(1 - y, r, c)))
-
-    down_rows = down_sum.shape[0] // 2
-    add_items(
-        down_parts,
-        down_rows // rows,
-        1,
-        lambda h, r, c: down_sum.at[at(h * down_rows + r * rows, rows), :],
-    )
-    up_cols = up_sum.shape[1] // 2
-    add_items(
-        up_parts,
-        up_sum.shape[0] // rows,
-        up_cols // cols,
-        lambda h, r, c: up_sum.at[pl.ds(r * rows, rows), at(h * up_cols + c * cols, cols)],
-    )
-    out_rows = out_sum.shape[0] // 2
-    add_items(
-        out_parts,
-        out_rows // rows,
-        1,
-        lambda h, r, c: out_sum.at[at(h * out_rows + r * rows, rows), :],
-    )
-    add_items(
-        qkv_parts,
-        out_sum.shape[1] // rows,
-        3,
-        lambda h, r, c: qkv_sums[c].at[pl.ds(r * rows, rows), at(h * cols, cols)],
-    )
-    items = []
-    for near, far in zip(near_items, far_items):
-        items += [(True, *far), (False, *near)]
+                items.append((True, far_send.at[cut], far_own.at[cut], place(1 - y, r, c)))
+                items.append((False, near_send.at[cut], near_own.at[cut], place(y, r, c)))
     count = len(items)
     far_count = count // 2
     far_slots = y_slot.shape[0]
 
     def x_copy(i):
         k = i % slots
-        return remote(items[i][1], x_slot.at[k], x_send.at[k], x_recv.at[k], over_x)
+        return remote_copy(items[i][1], x_slot.at[k], x_send.at[k], x_recv.at[k], p.over_x)
 
     def own_copy(i):
         k = i % slots
         return pltpu.make_async_copy(items[i][2], own_slot.at[k], own_sem.at[k])
 
     def y_copy(i):
-        k = i % slots
-        g = (i // 2) % far_slots
-        return remote(pair_slot.at[k], y_slot.at[g], y_send.at[g], y_recv.at[g], over_y)
+        k, g = i % slots, (i // 2) % far_slots
+        return remote_copy(pair_slot.at[k], y_slot.at[g], y_send.at[g], y_recv.at[g], p.over_y)
 
     def summed(i):
         return y_slot.at[(i // 2) % far_slots] if items[i][0] else pair_slot.at[i % slots]
 
     def outward(i):
         k = i % slots
-        return remote(summed(i), z_slot.at[k], outer_send.at[k], outer_recv.at[k], mate)
+        return remote_copy(summed(i), z_slot.at[k], outer_send.at[k], outer_recv.at[k], p.mate)
 
     def across(i):
         k = i % slots
-        return remote(z_pair.at[k], inner_slot.at[k], inner_send.at[k], inner_recv.at[k], middle)
+        return remote_copy(z_pair.at[k], inner_slot.at[k], inner_send.at[k], inner_recv.at[k], p.middle)
 
     def backward(i):
         k = i % slots
-        return remote(total_slot.at[k], z_slot.at[k], outer_send.at[k], outer_recv.at[k], mate)
+        return remote_copy(total_slot.at[k], z_slot.at[k], outer_send.at[k], outer_recv.at[k], p.mate)
 
     def result_inner(i):
         k = i % slots
@@ -963,7 +869,7 @@
         k = i % slots
         add(x_slot.at[k], own_slot.at[k], pair_slot.at[k])
         if i + slots < count:
-            grant(x_free, over_x)
+            grant(x_free, p.over_x)
         if items[i][0]:
             if i // 2 >= far_slots:
                 pl.semaphore_wait(y_free, 1)
@@ -991,13 +897,13 @@
             outward(i).wait_recv()
             add(summed(i), z_slot.at[k], z_pair.at[k])
             if i + slots < count:
-                grant(outer_free, mate)
+                grant(outer_free, p.mate)
             if i >= slots:
                 pl.semaphore_wait(inner_free, 1)
             across(i).start()
 
         if items[i][0] and i // 2 + far_slots < far_count:
-            grant(y_free, over_y)
+            grant(y_free, p.over_y)
 
     def stage_total(i):
         k = i % slots
@@ -1007,7 +913,7 @@
             across(i).wait()
             add(z_pair.at[k], inner_slot.at[k], total_slot.at[k])
             if i + slots < count:
-                grant(inner_free, middle)
+                grant(inner_free, p.middle)
             if i >= slots:
                 pl.semaphore_wait(outer_free, 1)
             backward(i).start()
@@ -1029,49 +935,613 @@
         def _():
             result_outer(i).wait()
             if i + slots < count:
-                grant(outer_free, mate)
+                grant(outer_free, p.mate)
 
     stages = (
+        (11, stage_finish),
+        (10, stage_result),
+        (8, stage_total),
+        (6, stage_across),
+        (4, stage_outward),
+        (2, stage_pair),
         (0, stage_send),
-        (2, stage_pair),
-        (4, stage_outward),
-        (6, stage_across),
-        (8, stage_total),
-        (10, stage_result),
-        (11, stage_finish),
-    )
-    for step in range(count + 12):
-        for lag, stage in reversed(stages):
+    )
+
+    def run(step):
+        for lag, stage in stages:
             if 0 <= step - lag < count:
                 stage(step - lag)
 
-
-def reduce_all(down_parts, up_parts, out_parts, qkv_parts):
-    bf16 = jnp.bfloat16
-    parts = (*down_parts, *up_parts, *out_parts, *qkv_parts)
+    return run, count + 12
+
+
+def reduce_scratch(slots, far_slots, rows, cols):
+    dma, regular = pltpu.SemaphoreType.DMA, pltpu.SemaphoreType.REGULAR
+    counts = (slots,) * 3 + (far_slots,) + (slots,) * 4
+    return [pltpu.VMEM((n, rows, cols), jnp.bfloat16) for n in counts] + [
+        dma((n,)) for n in (slots,) * 3 + (far_slots,) * 2 + (slots,) * 5
+    ] + [regular] * 4
+
+
+class RowSum:
+    def __init__(self, p, rows, arrived, sent, loaded, send_sem, recv_sem, load_sem, core_free, y_free, uses):
+        self.p, self.rows, self.uses = p, rows, uses
+        self.arrived, self.sent, self.loaded = arrived, sent, loaded
+        self.send_sem, self.recv_sem, self.load_sem = send_sem, recv_sem, load_sem
+        self.core_free, self.y_free = core_free, y_free
+
+    def block(self, ref, k):
+        return ref.at[pl.ds(k * self.rows, self.rows), :]
+
+    def hop(self, ref, k):
+        source = (self.block(ref, 3), self.block(ref, 1), self.sent)[k]
+        target = self.p.over_y if k == 2 else self.p.over_core
+        return remote_copy(source, self.arrived.at[k], self.send_sem.at[k], self.recv_sem.at[k], target)
+
+    def load(self, ref, k):
+        return pltpu.make_async_copy(self.block(ref, k), self.loaded, self.load_sem)
+
+    def start(self, use, ref, local):
+        if use:
+            pl.semaphore_wait(self.core_free, 1)
+            pl.semaphore_wait(self.y_free, 1)
+        self.hop(ref, 0).start()
+        self.hop(ref, 1).start()
+        if not local:
+            self.load(ref, 2).start()
+
+    def middle(self, ref, local):
+        self.hop(ref, 0).wait()
+        if not local:
+            self.load(ref, 2).wait()
+        base = self.block(ref, 2) if local else self.loaded
+
+        @pl.loop(0, self.rows // 32)
+        def _(k):
+            at = pl.ds(pl.multiple_of(k * 32, 32), 32)
+            self.sent[at, :] = (
+                base[at, :].astype(jnp.float32) + self.arrived[0, at, :].astype(jnp.float32)
+            ).astype(jnp.bfloat16)
+
+        self.hop(ref, 2).start()
+        if not local:
+            self.load(ref, 0).start()
+
+    def finish(self, ref, local):
+        self.hop(ref, 1).wait()
+        self.hop(ref, 2).wait()
+        if not local:
+            self.load(ref, 0).wait()
+
+    def total(self, ref, local, at):
+        base = self.block(ref, 0) if local else self.loaded
+        return (
+            base[at, :].astype(jnp.float32)
+            + self.arrived[1, at, :].astype(jnp.float32)
+            + self.arrived[2, at, :].astype(jnp.float32)
+        )
+
+    def release(self, use):
+        if use + 1 < self.uses:
+            grant(self.core_free, self.p.over_core)
+            grant(self.y_free, self.p.over_y)
+
+
+def unit_rows(values):
+    center = values - jnp.mean(values, -1, keepdims=True)
+    inverse = lax.rsqrt(jnp.mean(center * center, -1, keepdims=True) + EPS)
+    return center * inverse, inverse
+
+
+def unit_back(upstream, unit, inverse, gain):
+    scaled = upstream * gain
+    return inverse * (
+        scaled
+        - jnp.mean(scaled, -1, keepdims=True)
+        - unit * jnp.mean(scaled * unit, -1, keepdims=True)
+    )
+
+
+GAIN_ONE, SHIFT_ONE, OUT_BIAS, GAIN_TWO, SHIFT_TWO, DOWN_BIAS, QUERY_BIAS, VALUE_BIAS, UP_BIAS, PEAKS = (
+    0,
+    1,
+    2,
+    3,
+    4,
+    5,
+    6,
+    7,
+    8,
+    12,
+)
+
+
+def backward_kernel(
+    head_size,
+    info,
+    vector_ref,
+    small_in,
+    down_parts,
+    up_parts,
+    two_part,
+    mlp_part,
+    hidden_hbm,
+    cot_hbm,
+    resid_hbm,
+    out_hbm,
+    qkv_mat_hbm,
+    qkv_hbm,
+    attended_hbm,
+    act_hbm,
+    down_sum,
+    up_sum,
+    out_sum,
+    qkv_sums,
+    rows_out,
+    rows_grad,
+    small,
+    out_products,
+    qkv_products,
+    engine,
+    base,
+    hidden_grad,
+    low,
+    out_mat,
+    attended_grad,
+    qkv,
+    qkv_grad,
+    act,
+    attended,
+    qkv_mat,
+    keys,
+    values,
+    key_sum,
+    value_sum,
+    stage,
+    packed,
+    arrived,
+    sent,
+    loaded,
+    small_arrived,
+    load_sem,
+    sum_send,
+    sum_recv,
+    sum_load,
+    join_send,
+    join_recv,
+    stage_sem,
+    row_send,
+    row_recv,
+    share_send,
+    share_recv,
+    small_send,
+    small_recv,
+    core_free,
+    y_free,
+):
+    f32, bf16 = jnp.float32, jnp.bfloat16
+    own_rows, width = base.shape
+    tokens, features = attended.shape
+    heads = features // head_size
+    depth = rows_out.shape[0] // 2
+    block_rows = rows_out.shape[1]
+    p = Place(depth)
+    x, y, z, t = p.x, p.y, p.z, p.t
+    entry_barrier(
+        [p.over_x, p.over_y, p.over_core, p.mate, p.middle, p.hop] + p.row_targets()
+    )
+    length = info[0]
+    scale = 1.0 / math.sqrt(head_size)
+    column = 2 * t + y
+
+    rows, cols = engine[0].shape[1:]
+    down_rows = down_sum.shape[0] // 2
+    up_cols = up_sum.shape[1] // 2
+    strip = out_sum.shape[1]
+
+    def four(ref):
+        return tuple(ref.at[k] for k in range(4))
+
+    groups = (
+        (
+            down_parts,
+            down_rows // rows,
+            1,
+            lambda h, r, c: down_sum.at[aligned(h * down_rows + r * rows, rows), :],
+        ),
+        (
+            up_parts,
+            strip // rows,
+            up_cols // cols,
+            lambda h, r, c: up_sum.at[pl.ds(r * rows, rows), aligned(h * up_cols + c * cols, cols)],
+        ),
+        (
+            four(out_products),
+            features // rows,
+            1,
+            lambda h, r, c: out_sum.at[aligned(h * features + r * rows, rows), :],
+        ),
+        (
+            four(qkv_products),
+            strip // rows,
+            3,
+            lambda h, r, c: qkv_sums[c].at[pl.ds(r * rows, rows), aligned(h * cols, cols)],
+        ),
+    )
+    run, steps = reduce_stages(p, groups, engine)
+
+    loads = [
+        pltpu.make_async_copy(source, target, load_sem.at[k])
+        for k, (source, target) in enumerate(
+            (
+                (hidden_hbm, base),
+                (cot_hbm.at[pl.ds(0, own_rows), :], packed),
+                (out_hbm, out_mat),
+                (qkv_hbm, qkv),
+                (attended_hbm, attended),
+                (act_hbm, act),
+                (qkv_mat_hbm, qkv_mat),
+                (resid_hbm, base),
+            )
+        )
+    ]
+    sums = RowSum(
+        p, own_rows, arrived, sent, loaded, sum_send, sum_recv, sum_load, core_free, y_free, 3
+    )
+    group_rows = 16
+    quarter = own_rows // 4 // group_rows
+
+    def start():
+        for k in range(7):
+            loads[k].start()
+        small[...] = small_in[...]
+        key_sum[...] = jnp.zeros_like(key_sum)
+        value_sum[...] = jnp.zeros_like(value_sum)
+        sums.start(0, two_part, False)
+
+    def two_middle():
+        sums.middle(two_part, False)
+
+    def two_finish():
+        sums.finish(two_part, False)
+        loads[0].wait()
+        loads[1].wait()
+
+    def accumulate(row, value):
+        small[pl.ds(row, 1), :] += jnp.sum(value, 0, keepdims=True)
+
+    def two_rows(part):
+        gain = vector_ref[pl.ds(GAIN_TWO, 1), :]
+
+        @pl.loop(part * quarter, (part + 1) * quarter)
+        def _(k):
+            at = pl.ds(pl.multiple_of(k * group_rows, group_rows), group_rows)
+            upstream = sums.total(two_part, False, at)
+            unit, inverse = unit_rows(base[at, :])
+            grad = packed[at, :].astype(f32) + unit_back(upstream, unit, inverse, gain)
+            hidden_grad[at, :] = grad
+            low[at, :] = grad.astype(bf16)
+            accumulate(GAIN_TWO, upstream * unit)
+            accumulate(SHIFT_TWO, upstream)
+            accumulate(OUT_BIAS, grad)
+
+    def low_block(k):
+        return low.at[pl.ds(k * own_rows, own_rows), :]
+
+    def join(k):
+        source, place, target = ((0, 1, p.over_core), (0, 2, p.over_y), (2, 3, p.over_core))[k]
+        return remote_copy(low_block(source), low_block(place), join_send.at[k], join_recv.at[k], target)
+
+    def join_start():
+        join(0).start()
+        join(1).start()
+        sums.release(0)
+
+    def join_pass():
+        join(1).wait_recv()
+        join(2).start()
+
+    def attend_block(k):
+        at = pl.ds(k * own_rows, own_rows)
+        attended_grad[at, :] = lax.dot_general(
+            low[at, :], out_mat[...], (((1,), (1,)), ((), ())), preferred_element_type=f32
+        ).astype(bf16)
+
+    def attend_own():
+        loads[2].wait()
+        attend_block(0)
+
+    def attend_peer():
+        join(0).wait()
+        attend_block(1)
+
+    def attend_far():
+        attend_block(2)
+
+    def attend_last():
+        join(1).wait_send()
+        join(2).wait()
+        attend_block(3)
+
+    def mlp_start():
+        sums.start(1, mlp_part, False)
+
+    def mlp_middle():
+        sums.middle(mlp_part, False)
+
+    def mlp_finish():
+        sums.finish(mlp_part, False)
+        bias = vector_ref[pl.ds(DOWN_BIAS, 1), :]
+
+        @pl.loop(0, own_rows // group_rows)
+        def _(k):
+            at = pl.ds(pl.multiple_of(k * group_rows, group_rows), group_rows)
+            packed[at, :] = (base[at, :] + sums.total(mlp_part, False, at) + bias).astype(bf16)
+
+        sums.release(1)
+
+    def row_source(k):
+        return packed.at[pl.ds(k * block_rows, block_rows), :]
+
+    row_ends = (rows_out, rows_grad)
+
+    def row_copy(a, k):
+        end = row_ends[a].at[x * depth + z]
+        return remote_copy(row_source(k), end, row_send.at[a, k], row_recv.at[a, z], p.row_target(k))
+
+    def row_arrival(a, k):
+        end = row_ends[a].at[t * depth + k]
+        return remote_copy(row_source(k), end, row_send.at[a, k], row_recv.at[a, k], p.row_target(k))
+
+    def row_stay(a, k):
+        return pltpu.make_async_copy(row_source(k), row_ends[a].at[x * depth + z], row_send.at[a, k])
+
+    def rows_start(a):
+        for k in range(depth):
+            stays = (z == k) & (x == t)
+            pl.when(stays)(lambda k=k: row_stay(a, k).start())
+            pl.when(jnp.logical_not(stays))(lambda k=k: row_copy(a, k).start())
+
+    def share(a):
+        group = row_ends[a].at[pl.ds(t * depth, depth)]
+        return remote_copy(group, group, share_send.at[a], share_recv.at[a], p.over_core)
+
+    def rows_share(a):
+        for k in range(depth):
+            stays = (z == k) & (x == t)
+            pl.when(stays)(lambda k=k: row_stay(a, k).wait())
+
+            @pl.when(jnp.logical_not(stays))
+            def _(k=k):
+                row_copy(a, k).wait_send()
+                row_arrival(a, k).wait_recv()
+
+        share(a).start()
+
+    def head_rows():
+        loads[3].wait()
+        loads[4].wait()
+        for block in range(4):
+            at = pl.ds(pl.multiple_of(p.block_place(block) * own_rows, own_rows), own_rows)
+            keys[pl.ds(block * own_rows, own_rows), :] = qkv[at, pl.ds(features, features)]
+            values[pl.ds(block * own_rows, own_rows), :] = qkv[at, pl.ds(2 * features, features)]
+
+    def attention_block(block):
+        at = pl.ds(pl.multiple_of(p.block_place(block) * own_rows, own_rows), own_rows)
+        part = pl.ds(0, (block + 1) * own_rows)
+
+        @pl.loop(0, heads)
+        def _(head):
+            lanes = aligned(head * head_size, head_size)
+            queries, grads = qkv[at, lanes], attended_grad[at, lanes]
+            probs, _ = attention_probs(queries, keys[part, lanes], block, length)
+            prob_grad = lax.dot_general(
+                grads, values[part, lanes], (((1,), (1,)), ((), ())), preferred_element_type=f32
+            )
+            inner = jnp.sum(probs * prob_grad, -1, keepdims=True)
+            score_grad = (probs * (prob_grad - inner)).astype(bf16)
+            query_grad = (
+                jnp.dot(score_grad, keys[part, lanes], preferred_element_type=f32) * scale
+            )
+            spot = aligned(column * features + head * head_size, head_size)
+            small[pl.ds(QUERY_BIAS, 1), spot] += jnp.sum(query_grad, 0, keepdims=True)
+            qkv_grad[at, lanes] = query_grad.astype(bf16)
+            key_sum[part, lanes] += lax.dot_general(
+                score_grad, queries, (((0,), (0,)), ((), ())), preferred_element_type=f32
+            )
+            value_sum[part, lanes] += lax.dot_general(
+                probs.astype(bf16), grads, (((0,), (0,)), ((), ())), preferred_element_type=f32
+            )
+
+    def attention_end(block):
+        at = pl.ds(pl.multiple_of(p.block_place(block) * own_rows, own_rows), own_rows)
+        part = pl.ds(block * own_rows, own_rows)
+        qkv_grad[at, pl.ds(features, features)] = (key_sum[part, :] * scale).astype(bf16)
+        value_grad = value_sum[part, :]
+        qkv_grad[at, pl.ds(2 * features, features)] = value_grad.astype(bf16)
+        spot = aligned(column * features, features)
+        small[pl.ds(VALUE_BIAS, 1), spot] += jnp.sum(value_grad, 0, keepdims=True)
+
+    stored = []
+
+    def store(value, target):
+        k = len(stored) % 2
+        if len(stored) >= 2:
+            stored[-2].wait()
+        stage[k] = value.astype(bf16)
+        copy = pltpu.make_async_copy(stage.at[k], target, stage_sem.at[k])
+        copy.start()
+        stored.append(copy)
+
+    def over_tokens(left, right):
+        return lax.dot_general(left, right, (((0,), (0,)), ((), ())), preferred_element_type=f32)
+
+    def out_product(k):
+        store(
+            over_tokens(attended[...], low[:, aligned(p.homes[k] * strip, strip)]),
+            out_products.at[k],
+        )
+
+    def qkv_product(k, c):
+        if k == 0 and c == 0:
+            loads[5].wait()
+        cut = pl.ds(c * features, features)
+        store(
+            over_tokens(act[:, aligned(p.homes[k] * strip, strip)], qkv_grad[:, cut]),
+            qkv_products.at[k, :, cut],
+        )
+
+    def products_end():
+        stored[-2].wait()
+        stored[-1].wait()
+
+    def one_block(k):
+        if k == 3:
+            loads[6].wait()
+        at = pl.ds(k * own_rows, own_rows)
+
+        @pl.loop(0, 4)
+        def _(n):
+            cut = aligned(n * strip, strip)
+            low[at, cut] = lax.dot_general(
+                qkv_grad[at, :], qkv_mat[cut, :], (((1,), (1,)), ((), ())), preferred_element_type=f32
+            ).astype(bf16)
+
+    def one_start():
+        sums.start(2, low, True)
+
+    def one_middle():
+        sums.middle(low, True)
+
+    def one_finish():
+        sums.finish(low, True)
+        loads[7].wait()
+
+    def one_rows(part):
+        gain = vector_ref[pl.ds(GAIN_ONE, 1), :]
+
+        @pl.loop(part * quarter, (part + 1) * quarter)
+        def _(k):
+            at = pl.ds(pl.multiple_of(k * group_rows, group_rows), group_rows)
+            upstream = sums.total(low, True, at)
+            unit, inverse = unit_rows(base[at, :])
+            grad = hidden_grad[at, :] + unit_back(upstream, unit, inverse, gain)
+            packed[at, :] = grad.astype(bf16)
+            accumulate(GAIN_ONE, upstream * unit)
+            accumulate(SHIFT_ONE, upstream)
+
+    def small_copy(k):
+        target = (p.over_core, p.over_x, p.over_y, p.mate, p.hop)[k]
+        return remote_copy(small, small_arrived.at[k], small_send.at[k], small_recv.at[k], target)
+
+    def small_add(k):
+        small_copy(k).wait()
+        mine, other = small[...], small_arrived[k]
+        row = lax.broadcasted_iota(jnp.int32, mine.shape, 0)
+        small[...] = jnp.where(row == PEAKS, jnp.maximum(mine, other), mine + other)
+
+    def call(function, *arguments):
+        return lambda: function(*arguments)
+
+    plan = {}
+
+    def at_step(step, *tasks):
+        plan.setdefault(step, []).extend(tasks)
+
+    at_step(0, start)
+    at_step(2, two_middle)
+    at_step(7, two_finish, call(two_rows, 0))
+    for k in range(1, 4):
+        at_step(7 + k // 2, call(two_rows, k))
+    at_step(8, join_start, mlp_start)
+    at_step(9, attend_own)
+    at_step(10, mlp_middle, attend_peer)
+    at_step(12, head_rows)
+    at_step(13, join_pass)
+    at_step(14, attend_far)
+    at_step(15, attend_last)
+    at_step(16, call(attention_block, 0), call(attention_block, 1))
+    at_step(17, call(attention_block, 2))
+    at_step(18, call(attention_block, 3))
+    at_step(19, *(call(attention_end, k) for k in range(4)))
+    for k in range(4):
+        at_step(19 + k, *(call(qkv_product, k, c) for c in range(3)))
+        at_step(23, call(out_product, k))
+    at_step(24, products_end, call(one_block, 3), call(one_block, 1), one_start)
+    at_step(25, call(one_block, 2), call(one_block, 0))
+    at_step(26, one_middle)
+    at_step(20, mlp_finish, lambda: rows_start(0), loads[7].start)
+    at_step(25, lambda: rows_share(0))
+    at_step(31, one_finish, share(0).wait, call(one_rows, 0))
+    for k in range(1, 4):
+        at_step(31 + k // 2, call(one_rows, k))
+    at_step(32, lambda: rows_start(1))
+    at_step(33, small_copy(0).start)
+    for k in range(4):
+        at_step(35 + 2 * k, call(small_add, k), small_copy(k + 1).start)
+    at_step(43, call(small_add, 4))
+    at_step(38, lambda: rows_share(1))
+    at_step(44, share(1).wait)
+    for step in range(steps):
+        run(step)
+        for task in plan.get(step, ()):
+            task()
+
+
+def backward_all(
+    head_size,
+    length,
+    vectors,
+    small,
+    down_parts,
+    up_parts,
+    two_part,
+    mlp_part,
+    hidden,
+    cot_low,
+    resid,
+    out_mat,
+    qkv_mat,
+    qkv,
+    attended,
+    act_one,
+    slots,
+):
+    bf16, f32 = jnp.bfloat16, jnp.float32
     hbm = pl.BlockSpec(memory_space=pl.ANY)
+    vmem = pl.BlockSpec(memory_space=pltpu.VMEM)
     down_rows, strip = down_parts[0].shape
     up_cols = up_parts[0].shape[1]
-    features = out_parts[0].shape[0]
+    tokens, features = attended.shape
+    own_rows, width = hidden.shape
+    depth = slots // 2
+    engine = reduce_scratch(6, 4, 256, 512)
+    n_engine = len(engine)
 
     def kernel(*refs):
-        reduce_kernel(
-            refs[0:4],
-            refs[4:8],
-            refs[8:12],
-            refs[12:16],
-            refs[16],
-            refs[17],
-            refs[18],
-            refs[19:22],
-            refs[22:],
-        )
-
-    slots, far_slots, rows, cols = 8, 8, 256, 512
+        ins, rest = refs[:21], refs[21:]
+        outs, scratch = rest[:11], rest[11:]
+        backward_kernel(
+            head_size,
+            ins[0],
+            ins[1],
+            ins[2],
+            ins[3:7],
+            ins[7:11],
+            *ins[11:],
+            outs[0],
+            outs[1],
+            outs[2],
+            outs[3:6],
+            *outs[6:],
+            scratch[:n_engine],
+            *scratch[n_engine:],
+        )
+
     dma, regular = pltpu.SemaphoreType.DMA, pltpu.SemaphoreType.REGULAR
 
-    def buffer(n):
-        return pltpu.VMEM((n, rows, cols), bf16)
+    def hold(shape, dtype=bf16):
+        return pltpu.VMEM(shape, dtype)
 
     return pl.pallas_call(
         kernel,
@@ -1079,39 +1549,76 @@
             jax.ShapeDtypeStruct((2 * down_rows, strip), bf16),
             jax.ShapeDtypeStruct((strip, 2 * up_cols), bf16),
             jax.ShapeDtypeStruct((2 * features, strip), bf16),
-        )
-        + (jax.ShapeDtypeStruct((strip, 2 * features), bf16),) * 3,
-        in_specs=[hbm] * 16,
-        out_specs=(hbm,) * 6,
-        scratch_shapes=[
-            buffer(slots),
-            buffer(slots),
-            buffer(slots),
-            buffer(far_slots),
-            buffer(slots),
-            buffer(slots),
-            buffer(slots),
-            buffer(slots),
-            dma((slots,)),
-            dma((slots,)),
-            dma((slots,)),
-            dma((far_slots,)),
-            dma((far_slots,)),
-            dma((slots,)),
-            dma((slots,)),
-            dma((slots,)),
-            dma((slots,)),
-            dma((slots,)),
-            regular,
-            regular,
+            jax.ShapeDtypeStruct((strip, 2 * features), bf16),
+            jax.ShapeDtypeStruct((strip, 2 * features), bf16),
+            jax.ShapeDtypeStruct((strip, 2 * features), bf16),
+            jax.ShapeDtypeStruct((slots, own_rows // depth, width), bf16),
+            jax.ShapeDtypeStruct((slots, own_rows // depth, width), bf16),
+            jax.ShapeDtypeStruct(small.shape, f32),
+            jax.ShapeDtypeStruct((4, features, strip), bf16),
+            jax.ShapeDtypeStruct((4, strip, 3 * features), bf16),
+        ),
+        in_specs=[pl.BlockSpec(memory_space=pltpu.SMEM), vmem, vmem] + [hbm] * 18,
+        out_specs=(hbm,) * 8 + (vmem,) + (hbm,) * 2,
+        scratch_shapes=engine
+        + [
+            hold((own_rows, width), f32),
+            hold((own_rows, width), f32),
+            hold((tokens, width)),
+            hold((features, width)),
+            hold((tokens, features)),
+            hold((tokens, 3 * features)),
+            hold((tokens, 3 * features)),
+            hold((tokens, width)),
+            hold((tokens, features)),
+            hold((width, 3 * features)),
+            hold((tokens, features)),
+            hold((tokens, features)),
+            hold((tokens, features), f32),
+            hold((tokens, features), f32),
+            hold((2, features, strip)),
+            hold((own_rows, width)),
+            hold((3, own_rows, width)),
+            hold((own_rows, width)),
+            hold((own_rows, width)),
+            hold((5,) + small.shape, f32),
+            dma((8,)),
+            dma((3,)),
+            dma((3,)),
+            dma(()),
+            dma((3,)),
+            dma((3,)),
+            dma((2,)),
+            dma((2, depth)),
+            dma((2, depth)),
+            dma((2,)),
+            dma((2,)),
+            dma((5,)),
+            dma((5,)),
             regular,
             regular,
         ],
         compiler_params=pltpu.CompilerParams(
-            collective_id=1, has_side_effects=True, vmem_limit_bytes=40 << 20
+            collective_id=1, has_side_effects=True, vmem_limit_bytes=58 << 20
         ),
         cost_estimate=pl.CostEstimate(flops=0, bytes_accessed=64 << 20, transcendentals=0),
-    )(*parts)
+    )(
+        length,
+        vectors,
+        small,
+        *down_parts,
+        *up_parts,
+        two_part,
+        mlp_part,
+        hidden,
+        cot_low,
+        resid,
+        out_mat,
+        qkv_mat,
+        qkv,
+        attended,
+        act_one,
+    )
 
 
 def split_body(
@@ -1167,14 +1674,6 @@
         size = v.shape[axis] // 2
         return lax.dynamic_slice_in_dim(v, which * size, size, axis)
 
-    def return_rows(rows):
-        part = rows.reshape(depth, block_rows, rows.shape[-1])
-        part = lax.all_to_all(part, "ctx", split_axis=0, concat_axis=0, tiled=True)
-        part = lax.ppermute(part, ("fsdp", "tp"), x_core)
-        other = across_core(part)
-        both = jnp.where(t == 0, jnp.stack([part, other]), jnp.stack([other, part]))
-        return both.reshape(slots, block_rows, rows.shape[-1]).astype(f32)
-
     def gather_rows(own):
         peer = across_core(own)
         far = across_y(own)
@@ -1206,6 +1705,7 @@
 
     small = jnp.stack([attn_gain, attn_shift, out_bias, mlp_gain, mlp_shift, down_bias])
     small = lax.all_gather(small, "fsdp", axis=1, tiled=True).astype(f32)
+    vectors_whole = small
     gain_one, shift_one, out_vec, gain_two, shift_two, down_vec = [small[k] for k in range(6)]
     vectors = jnp.concatenate([query_bias, value_bias, up_bias.reshape(-1, query_bias.shape[1])], 0)
     vectors = lax.all_gather(vectors, "fsdp", axis=0, tiled=False)
@@ -1240,7 +1740,7 @@
     attn_far = matmul(attended[chip_rows:], out_mat)
     attn_near = matmul(attended[:chip_rows], out_mat)
     hidden = resid + scatter_rows(attn_near, attn_far) + out_vec
-    normed_b, unit_two, inverse_two = normalize(hidden, gain_two, shift_two)
+    normed_b = normalize(hidden, gain_two, shift_two)[0]
     act_two = jnp.concatenate(gather_rows(normed_b.astype(bf16)), 0)
 
     pre = matmul(act_two, up_mat) + up_vec
@@ -1250,88 +1750,76 @@
     pre_grad = back_product(cot_low, down_mat) * slope
     pre_low = pre_grad.astype(bf16)
     up_bias_part = jnp.sum(pre_grad, 0)
-    two_far = back_product(pre_low[chip_rows:], up_mat)
-    two_near = back_product(pre_low[:chip_rows], up_mat)
-    normed_two_grad = scatter_rows(two_near, two_far)
-    hidden_in, mlp_gain_part, mlp_shift_part = norm_back(
-        normed_two_grad, unit_two, inverse_two, gain_two
-    )
-    hidden_grad = cot_own.astype(f32) + hidden_in
-    out_bias_part = jnp.sum(hidden_grad, 0)
-    hidden_low = jnp.concatenate(gather_rows(hidden_grad.astype(bf16)), 0)
-    attended_grad = back_product(hidden_low, out_mat).astype(bf16)
-    qkv_low, bias_parts = attention_backward(info, qkv, attended_grad, head_size)
-
     down_parts = products(lambda home: weight_product(gelu_low, strip_of(cot_low, home)))
     up_parts = products(lambda home: weight_product(strip_of(act_two, home), pre_low))
-    out_parts = products(lambda home: weight_product(attended, strip_of(hidden_low, home)))
-    qkv_parts = products(lambda home: weight_product(strip_of(act_one, home), qkv_low))
-    mlp_far = matmul(gelu_low[chip_rows:], down_mat)
-    mlp_near = matmul(gelu_low[:chip_rows], down_mat)
-    layer_output = hidden + scatter_rows(mlp_near, mlp_far) + down_vec
-    final_output = return_rows(layer_output.astype(bf16))
-
-    one_far = back_product(qkv_low[chip_rows:], qkv_mat)
-    one_near = back_product(qkv_low[:chip_rows], qkv_mat)
-    normed_one_grad = scatter_rows(one_near, one_far)
-    _, unit_one, inverse_one = normalize(resid, gain_one, shift_one)
-    input_in, attn_gain_part, attn_shift_part = norm_back(
-        normed_one_grad, unit_one, inverse_one, gain_one
-    )
-    final_grad = return_rows((hidden_grad + input_in).astype(bf16))
-
-    sums = reduce_all(down_parts, up_parts, out_parts, qkv_parts)
-    down_weight_grad, up_weight_grad, out_weight_grad = [v.astype(f32) for v in sums[:3]]
-    query_weight_grad, key_weight_grad, value_weight_grad = [v.astype(f32) for v in sums[3:]]
-
-    def placed(v, which):
-        whole = jnp.zeros((4,) + v.shape, f32)
-        return lax.dynamic_update_slice_in_dim(whole, v[None], which, 0)
-
+    two_part = back_product(pre_low, up_mat).astype(bf16)
+    mlp_part = matmul(gelu_low, down_mat).astype(bf16)
     column = 2 * t + y
-    rows_sum = jnp.stack(
-        [attn_gain_part, attn_shift_part, out_bias_part, mlp_gain_part, mlp_shift_part, down_bias_part]
-    )
-    head_sum = placed(jnp.stack([bias_parts[:, 0].reshape(-1), bias_parts[:, 1].reshape(-1)]), column)
-    unit_sum = placed(up_bias_part, column)
-    flat = jnp.concatenate([rows_sum.reshape(-1), head_sum.reshape(-1), unit_sum.reshape(-1)])
-    flat = lax.psum(flat, ("fsdp", "ctx", "tp"))
-    cut_one, cut_two = rows_sum.size, rows_sum.size + head_sum.size
-    rows_sum = lax.dynamic_slice_in_dim(flat[:cut_one].reshape(6, width), f * strip, strip, 1)
-    head_sum = lax.dynamic_slice_in_dim(flat[cut_one:cut_two].reshape(4, 2, features), 2 * t, 2, 0)
-    head_sum = head_sum.transpose(1, 0, 2).reshape(2, 2 * local_heads, head_size)
+    small = jnp.zeros((16, width), f32).at[DOWN_BIAS].set(down_bias_part)
+    small = lax.dynamic_update_slice(small, up_bias_part[None], (UP_BIAS + column, 0))
+    small = small.at[PEAKS].set(NEG)
+    small = lax.dynamic_update_slice(small, peaks[None], (PEAKS, local_heads * (2 * t + y)))
+    (
+        down_sum,
+        up_sum,
+        out_sum,
+        query_sum,
+        key_sum,
+        value_sum,
+        rows_out,
+        rows_grad,
+        totals,
+        _,
+        _,
+    ) = backward_all(
+        head_size,
+        length[None],
+        vectors_whole,
+        small,
+        down_parts,
+        up_parts,
+        two_part,
+        mlp_part,
+        hidden,
+        cot_low,
+        resid,
+        out_mat,
+        qkv_mat,
+        qkv,
+        attended,
+        act_one,
+        slots,
+    )
+    rows_sum = lax.dynamic_slice(totals, (0, f * strip), (6, strip))
+    head_sum = lax.dynamic_slice(totals, (QUERY_BIAS, 2 * t * features), (2, 2 * features))
+    head_sum = head_sum.reshape(2, 2 * local_heads, head_size)
     head_sum = lax.dynamic_slice_in_dim(head_sum, f * query_bias.shape[1], query_bias.shape[1], 2)
-    unit_sum = lax.dynamic_slice_in_dim(
-        flat[cut_two:].reshape(2, up_bias.shape[0], width), t, 1, 0
-    )[0]
-    unit_sum = lax.dynamic_slice_in_dim(unit_sum, f * strip, strip, 1)
-
-    my_peaks = lax.dynamic_update_slice_in_dim(
-        jnp.full((2, local_heads), NEG, f32), peaks[None], y, 0
-    ).reshape(-1)
-    peak_all = lax.pmax(my_peaks, ("fsdp", "ctx"))
+    unit_sum = lax.dynamic_slice(
+        totals, (UP_BIAS + up_bias.shape[0] * t, f * strip), (up_bias.shape[0], strip)
+    )
+    peak_all = lax.dynamic_slice(totals, (PEAKS, 2 * local_heads * t), (1, 2 * local_heads))[0]
     level = clip_level[0]
     factor = jnp.repeat(jnp.sqrt(level / jnp.maximum(peak_all, level)), head_size)
     query_clipped = (query_weight.astype(f32) * factor[None, :]).astype(bf16)
     key_clipped = (key_weight.astype(f32) * factor[None, :]).astype(bf16)
     return (
-        final_output,
-        final_grad,
-        rows_sum[0],
-        rows_sum[1],
-        query_weight_grad,
+        rows_out.astype(f32),
+        rows_grad.astype(f32),
+        rows_sum[GAIN_ONE],
+        rows_sum[SHIFT_ONE],
+        query_sum.astype(f32),
         head_sum[0],
-        key_weight_grad,
-        value_weight_grad,
+        key_sum.astype(f32),
+        value_sum.astype(f32),
         head_sum[1],
-        out_weight_grad,
-        rows_sum[2],
-        rows_sum[3],
-        rows_sum[4],
-        up_weight_grad,
+        out_sum.astype(f32),
+        rows_sum[OUT_BIAS],
+        rows_sum[GAIN_TWO],
+        rows_sum[SHIFT_TWO],
+        up_sum.astype(f32),
         unit_sum,
-        down_weight_grad,
-        rows_sum[5],
+        down_sum.astype(f32),
+        rows_sum[DOWN_BIAS],
         peak_all,
         query_clipped,
         key_clipped,

time: 1170 us -> 886 us (0.76)
  waiting for transfers between devices: 242 us -> 50.6 us
  Pallas kernels: 561 us -> 636 us
  matrix products: 151 us -> 104 us
  blocking collectives: 54.7 us -> 17.8 us
  starting transfers between devices: 45.3 us -> 11.3 us
  other arithmetic: 61.3 us -> 37.4 us
  between operations: 25.7 us -> 11.9 us
    psum x1 -> x0, waiting for transfers between devices: 117 us -> none  [split_body(): flat = lax.psum(flat, ('fsdp', 'ctx', 'tp'))]
    pallas_call x2 -> x1, Pallas kernels: 322 us -> 397 us  [backward_all(): pl.pallas_call(kernel, out_shape=(jax.ShapeDtypeStruct((2 * down_rows, st...]
    ppermute x6 -> x2, waiting for transfers between devices: 110 us -> 48.4 us  [across_y(): return lax.ppermute(v, 'fsdp', over_y)]
    pmax x1 -> x0, blocking collectives: 36.9 us -> none  [split_body(): peak_all = lax.pmax(my_peaks, ('fsdp', 'ctx'))]
    dot_general x16 -> x8, matrix products: 57.5 us -> 30.3 us  [weight_product(): jnp.einsum('td,te->de', left, right, preferred_element_type=jnp.float32)]
    ppermute x2 -> x0, starting transfers between devices: 19.3 us -> none  [return_rows(): part = lax.ppermute(part, ('fsdp', 'tp'), x_core)]
    dot_general x6 -> x2, matrix products: 47.4 us -> 29.8 us  [back_product(): jnp.einsum('te,de->td', left, right, preferred_element_type=jnp.float32)]
    all_to_all x2 -> x0, waiting for transfers between devices: 13.9 us -> none  [return_rows(): part = lax.all_to_all(part, 'ctx', split_axis=0, concat_axis=0, tiled=True)]
  transfers between devices with their start and end apart: 25 -> 6, of which waited for: 10 -> 4; matrix products, arithmetic and copies ran while one was open for 11% -> 1% of each run, Pallas kernels for 28% -> 0%
where the time goes in v3:
time: 886 us; the launch traced here: 883 us
  Pallas kernels  636 us (72%)
  matrix products  104 us (12%)
  waiting for transfers between devices  50.6 us (6%)
  other arithmetic  37.4 us (4%)
  blocking collectives  17.8 us (2%)
  local copies, waits for them, and re-layouts  14.6 us (2%)
  between operations  11.9 us (1%)
  starting transfers between devices  11.3 us (1%)
    pallas_call x1, Pallas kernels, backward_all(): pl.pallas_call(kernel, out_shape=(jax.ShapeDtypeStruct((2 * down_rows, st...  397 us
    pallas_call x1, Pallas kernels, gather_all(): pl.pallas_call(gather_kernel, out_shape=(jax.ShapeDtypeStruct((width, 3 *...  228 us
    ppermute x2, waiting for transfers between devices, across_y(): return lax.ppermute(v, 'fsdp', over_y)  48.4 us
    dot_general x5, matrix products, matmul(): return jnp.dot(left, right, preferred_element_type=jnp.float32)  43.6 us
    dot_general x8, matrix products, weight_product(): jnp.einsum('td,te->de', left, right, preferred_element_type=jnp.float32)  30.3 us
    dot_general x2, matrix products, back_product(): jnp.einsum('te,de->td', left, right, preferred_element_type=jnp.float32)  29.8 us
  transfers between devices with their start and end apart: 6, of which 4 were waited for; matrix products, arithmetic and copies ran while one was open for 1% of the time, Pallas kernels for 0%

profile of v3, /device:TPU:0, one launch (start us, length us, event | category | flops | bytes accessed | tf_op | source)
XLA Modules:
  0.0 883.2 jit_solution(9572264469287422567)
XLA Ops:
  11.3 1.7 constant_dynamic-slice_fusion.4
  15.0 9.6 %all_gather.9 = bf16[6,2048]{1,0:T(8,128)(2,1)S(1)} all-gather(bf16[6,512]{1,0:T(8,128)(2,1)S(1)} %stack.27), channel_id=1, replica_groups=mesh['fsdp'=4,'ctx'=4,'tp'=2] {'fsdp'}, dimensions={1}, use_global_device_ids=true | all-gather | bytes 30720 | tf_op jit(solution)/shard_map/all_gather | solution.py:1707
  24.7 2.7 dynamic-slice_convert_fusion.cot_ref
  27.6 8.1 all-gather.1
  40.5 228.3 %shard_map.347 = (bf16[2048,1536]{1,0:T(8,128)(2,1)}, bf16[512,2048]{1,0:T(8,128)(2,1)}, bf16[2048,2048]{1,0:T(8,128)(2,1)}, bf16[2048,2048]{1,0:T(8,128)(2,1)},...) custom-call(bf16[512,1024]{1,0:T(8,128)(2,1)} %q_ref.1, bf16[512,1024]{1,0:T(8,128)(2,1)} %k_ref.1, ...), custom_call_target="tpu_custom_call" | custom-call | bytes 67108864 | tf_op jit(solution)/shard_map/pallas_call | solution.py:706
  268.8 10.0 %add_convert_fusion.q_ref.k_ref.v_ref.refs_18_ = bf16[1024,1536]{1,0:T(8,128)(2,1)S(1)} fusion(bf16[1024,2048]{1,0:T(8,128)(2,1)} %get-tuple-element.113.refs_20_, bf16[2048,1536]{1,0:T(8,128)(2,1)} %get-tuple-element.114.refs_17_, f32[1536]{0:T(1024)S(1)} %pad_maximum_fusion.3), kind=kOutput, calls=%fused_computation.8 | convolution fusion | flops 6445596672 | bytes 13637632 | tf_op jit(solution)/shard_map/dot_general | solution.py:41
  278.8 10.6 %shard_map.348 = (bf16[1024,512]{1,0:T(8,128)(2,1)S(1)}, f32[4,8,128]{2,1,0:T(8,128)S(1)}) custom-call(s32[5]{0:T(128)S(1)} %pad_add_fusion.info, bf16[1024,1536]{1,0:T(8,128)(2,1)S(1)} %add_convert_fusion.q_ref.k_ref.v_ref.refs_18_, bf16[1024,1536]{1,0:T(8,128)(2,1)S(1)} %add_convert_fusion.q_ref.k_ref.v_ref.refs_18_, ...), custom_call_target="tpu_custom_call" | custom-call | flops 2147483648 | bytes 4194304 | tf_op jit(solution)/shard_map/pallas_call | solution.py:436
  290.9 10.8 %collective-permute-start.1 = (bf16[256,2048]{1,0:T(8,128)(2,1)S(1)}, bf16[256,2048]{1,0:T(8,128)(2,1)S(1)}, u32[]{:S(2)}, u32[]{:S(2)}) collective-permute-start(bf16[256,2048]{1,0:T(8,128)(2,1)S(1)} %slice.190), channel_id=1, source_target_pairs={{0,1},{1,0},{2,3},{3,2},{4,5},{5,4},{6,7},{7,6},{8,9},{9,8},{10,11... | collective-permute-start | bytes 3145736 | tf_op jit(solution)/shard_map/ppermute | solution.py:1671
  305.8 24.0 %collective-permute-done.2 = bf16[256,2048]{1,0:T(8,128)(2,1)S(1)} collective-permute-done((bf16[256,2048]{1,0:T(8,128)(2,1)S(1)}, bf16[256,2048]{1,0:T(8,128)(2,1)S(1)}, u32[]{:S(2)}, u32[]{:S(2)}) %collective-permute-start.2) | collective-permute-done | bytes 1048608 | tf_op jit(solution)/shard_map/ppermute | solution.py:1668
  331.6 24.4 %collective-permute-done.4 = bf16[256,2048]{1,0:T(8,128)(2,1)} collective-permute-done((bf16[256,2048]{1,0:T(8,128)(2,1)S(1)}, bf16[256,2048]{1,0:T(8,128)(2,1)}, u32[]{:S(2)}, u32[]{:S(2)}) %collective-permute-start.4) | collective-permute-done | bytes 1048608 | tf_op jit(solution)/shard_map/ppermute | solution.py:1668
  357.0 1.7 dynamic-slice_reduce_fusion
  359.5 17.0 %multiply_convert_fusion = (bf16[1024,2048]{1,0:T(8,128)(2,1)S(1)}, f32[1024,2048]{1,0:T(8,128)}) fusion(f32[2048]{0:T(1024)S(1)} %dynamic-slice_convert_fusion.1, bf16[2048,2048]{1,0:T(8,128)(2,1)} %get-tuple-element.117, bf16[256,2048]{1,0:T(8,128)(2,1)} %collective-permute-done.5, bf16[256,2048]{1,0:T(8,128)(2,1)} %collective-permute-done.4, ...), kind=kOutput, calls=%fused_computation.6 | convolution fusion | flops 8619294720 | bytes 25174016 | tf_op jit(solution)/shard_map/dot_general | solution.py:41
  376.5 14.1 %convolution_convert_fusion.refs_12_ = bf16[1024,2048]{1,0:T(8,128)(2,1)} fusion(bf16[1024,2048]{1,0:T(8,128)(2,1)S(1)} %get-tuple-element.163, bf16[2048,2048]{1,0:T(8,128)(2,1)} %get-tuple-element.111), kind=kOutput, calls=%fused_computation.10 | convolution fusion | flops 8592031744 | bytes 16777216 | tf_op jit(solution)/shard_map/dot_general | solution.py:41
  390.7 17.4 %fusion.33 = (bf16[1024,2048]{1,0:T(8,128)(2,1)}, f32[2048]{0:T(1024)S(1)}) fusion(f32[1024,2048]{1,0:T(8,128)} %get-tuple-element.164, f32[2048]{0:T(1024)S(1)} %dynamic-slice_convert_fusion.1, bf16[1024,2048]{1,0:T(8,128)(2,1)S(1)} %copy-done.5, bf16[2048,2048]{1,0:T(8,128)(2,1)} %get-tuple-element.111), kind=kOutput, calls=%fused_computation.89 | convolution fusion | flops 8615098368 | bytes 25182208 | tf_op jit(solution)/shard_map/te,de->td/dot_general | solution.py:49
  408.1 12.4 %convolution_convert_fusion.1.refs_11_ = bf16[1024,2048]{1,0:T(8,128)(2,1)} fusion(bf16[1024,2048]{1,0:T(8,128)(2,1)} %get-tuple-element.132, bf16[2048,2048]{1,0:T(8,128)(2,1)S(1)} %bitcast.87), kind=kOutput, calls=%fused_computation.11 | convolution fusion | flops 8592031744 | bytes 16777216 | tf_op jit(solution)/shard_map/te,de->td/dot_general | solution.py:49
  420.5 3.7 convolution_convert_fusion.6.refs_6_
  424.2 2.4 pad_maximum_fusion
  427.3 3.8 convolution_convert_fusion.2.refs_10_
  431.1 3.8 convolution_convert_fusion.3.refs_9_
  434.9 3.7 convolution_convert_fusion.7.refs_5_
  438.6 3.8 convolution_convert_fusion.4.refs_8_
  442.4 3.7 convolution_convert_fusion.8.refs_4_
  446.1 4.0 convolution_convert_fusion.5.refs_7_
  450.2 3.7 convolution_convert_fusion.9.refs_3_
  455.2 397.1 %shard_map.349 = (bf16[4096,512]{1,0:T(8,128)(2,1)}, bf16[512,4096]{1,0:T(8,128)(2,1)}, bf16[1024,512]{1,0:T(8,128)(2,1)}, bf16[512,1024]{1,0:T(8,128)(2,1)}, bf...) custom-call(s32[1]{0:T(128)} %dynamic_slice.82.refs_0_, ...), custom_call_target="tpu_custom_call" | custom-call | bytes 67108864 | tf_op jit(solution)/shard_map/pallas_call | solution.py:1546
  852.3 6.8 convert_element_type.140
  859.1 4.6 convert_element_type.141
  863.7 2.5 convert_element_type.134
  866.3 2.5 convert_element_type.135
  870.2 1.9 multiply_convert_fusion.1
  876.8 1.6 convert_element_type.139
  881.3 1.6 fusion.34
  (136 shorter events, 27.2 us)
Async XLA Ops:
  13.0 2.0 copy-start.23
  13.0 2.0 copy-start.24
  13.0 14.4 %copy-start.16 = (bf16[2,512]{1,0:T(2,128)(2,1)S(1)}, bf16[2,512]{1,0:T(2,128)(2,1)}, u32[]{:S(2)}) copy-start(bf16[2,512]{1,0:T(2,128)(2,1)} %param.48) | copy-start | bytes 6148
  13.0 14.5 %copy-start.17 = (bf16[8,32]{1,0:T(8,128)(2,1)S(1)}, bf16[8,32]{1,0:T(8,128)(2,1)}, u32[]{:S(2)}) copy-start(bf16[8,32]{1,0:T(8,128)(2,1)} %param.42) | copy-start | bytes 1540
  13.0 14.5 %copy-start.18 = (bf16[8,32]{1,0:T(8,128)(2,1)S(1)}, bf16[8,32]{1,0:T(8,128)(2,1)}, u32[]{:S(2)}) copy-start(bf16[8,32]{1,0:T(8,128)(2,1)} %param.39) | copy-start | bytes 1540
  13.0 24.7 %copy-start.25 = (s32[8]{0:T(128)S(1)}, s32[8]{0:T(128)}, u32[]{:S(2)}) copy-start(s32[8]{0:T(128)} %param.34) | copy-start | bytes 100
  278.8 10.6 %copy-start = (bf16[1024,1536]{1,0:T(8,128)(2,1)}, bf16[1024,1536]{1,0:T(8,128)(2,1)S(1)}, u32[]{:S(2)}) copy-start(bf16[1024,1536]{1,0:T(8,128)(2,1)S(1)} %add_convert_fusion.q_ref.k_ref.v_ref.refs_18_) | copy-start | bytes 9437188
  278.8 10.6 %copy-start.3 = (bf16[512,2048]{1,0:T(8,128)(2,1)S(1)}, bf16[512,2048]{1,0:T(8,128)(2,1)}, u32[]{:S(2)}) copy-start(bf16[512,2048]{1,0:T(8,128)(2,1)} %get-tuple-element.116.refs_16_) | copy-start | bytes 6291460
  289.4 12.2 %copy-start.1 = (bf16[1024,512]{1,0:T(8,128)(2,1)}, bf16[1024,512]{1,0:T(8,128)(2,1)S(1)}, u32[]{:S(2)}) copy-start(bf16[1024,512]{1,0:T(8,128)(2,1)S(1)} %get-tuple-element.115.refs_19_) | copy-start | bytes 3145732
  290.9 13.0 %collective-permute-start.1 = (bf16[256,2048]{1,0:T(8,128)(2,1)S(1)}, bf16[256,2048]{1,0:T(8,128)(2,1)S(1)}, u32[]{:S(2)}, u32[]{:S(2)}) collective-permute-start(bf16[256,2048]{1,0:T(8,128)(2,1)S(1)} %slice.190), channel_id=1, source_target_pairs={{0,1},{1,0},{2,3},{3,2},{4,5},{5,4},{6,7},{7,6},{8,9},{9,8},{10,11... | collective-permute-start | bytes 3145736 | tf_op jit(solution)/shard_map/ppermute | solution.py:1671
  302.9 26.9 %copy-start.4 = (f32[256,2048]{1,0:T(8,128)S(1)}, f32[256,2048]{1,0:T(8,128)}, u32[]{:S(2)}) copy-start(f32[256,2048]{1,0:T(8,128)} %get-tuple-element.112.refs_15_) | copy-start | bytes 6291460
  303.0 2.7 collective-permute-start
  304.2 25.5 %collective-permute-start.2 = (bf16[256,2048]{1,0:T(8,128)(2,1)S(1)}, bf16[256,2048]{1,0:T(8,128)(2,1)S(1)}, u32[]{:S(2)}, u32[]{:S(2)}) collective-permute-start(bf16[256,2048]{1,0:T(8,128)(2,1)S(1)} %fusion.5), channel_id=1, source_target_pairs={{0,16},{16,0},{8,24},{24,8},{1,17},{17,1},{9,25},{25,9},{2,18},{18... | collective-permute-start | bytes 3145736 | tf_op jit(solution)/shard_map/ppermute | solution.py:1668
  330.4 46.1 %copy-start.2 = (f32[256,2048]{1,0:T(8,128)}, f32[256,2048]{1,0:T(8,128)S(1)}, u32[]{:S(2)}) copy-start(f32[256,2048]{1,0:T(8,128)S(1)} %get-tuple-element.131.refs_13_) | copy-start | bytes 6291460
  331.2 24.8 %collective-permute-start.4 = (bf16[256,2048]{1,0:T(8,128)(2,1)S(1)}, bf16[256,2048]{1,0:T(8,128)(2,1)}, u32[]{:S(2)}, u32[]{:S(2)}) collective-permute-start(bf16[256,2048]{1,0:T(8,128)(2,1)S(1)} %add_convert_fusion.1), channel_id=1, source_target_pairs={{0,16},{16,0},{8,24},{24,8},{1,17},{17,1},{9,25},{25,9},{2,18},{18... | collective-permute-start | bytes 3145736 | tf_op jit(solution)/shard_map/ppermute | solution.py:1668
  331.6 27.9 %collective-permute-start.3 = (bf16[256,2048]{1,0:T(8,128)(2,1)S(1)}, bf16[256,2048]{1,0:T(8,128)(2,1)}, u32[]{:S(2)}, u32[]{:S(2)}) collective-permute-start(bf16[256,2048]{1,0:T(8,128)(2,1)S(1)} %add_convert_fusion.1), channel_id=1, source_target_pairs={{0,1},{1,0},{2,3},{3,2},{4,5},{5,4},{6,7},{7,6},{8,9},{9,8},{10,11... | collective-permute-start | bytes 3145736 | tf_op jit(solution)/shard_map/ppermute | solution.py:1671
  356.0 3.5 collective-permute-start.5
  376.5 14.2 %copy-start.27 = (bf16[1024,2048]{1,0:T(8,128)(2,1)}, bf16[1024,2048]{1,0:T(8,128)(2,1)S(1)}, u32[]{:S(2)}) copy-start(bf16[1024,2048]{1,0:T(8,128)(2,1)S(1)} %get-tuple-element.163) | copy-start | bytes 12582916
  376.5 14.2 %copy-start.5 = (bf16[1024,2048]{1,0:T(8,128)(2,1)S(1)}, bf16[1024,2048]{1,0:T(8,128)(2,1)}, u32[]{:S(2)}) copy-start(bf16[1024,2048]{1,0:T(8,128)(2,1)} %get-tuple-element.110.refs_14_) | copy-start | bytes 12582916
  376.5 31.5 %slice-start = ((s8[8388608]{0:T(1024)(128)(4,1)}), s8[4194304]{0:T(1024)(128)(4,1)S(1)}, s32[]{:S(2)}) async-start(s8[8388608]{0:T(1024)(128)(4,1)} %bitcast.86), calls=%async_computation | async-start | bytes 8388608
  390.7 17.4 %slice-start.1 = ((s8[8388608]{0:T(1024)(128)(4,1)}), s8[4194304]{0:T(1024)(128)(4,1)S(1)}, s32[]{:S(2)}) async-start(s8[8388608]{0:T(1024)(128)(4,1)} %bitcast.86), calls=%async_computation.1 | async-start | bytes 8388608
  408.1 12.4 %copy-start.28 = (bf16[1024,2048]{1,0:T(8,128)(2,1)S(1)}, bf16[1024,2048]{1,0:T(8,128)(2,1)}, u32[]{:S(2)}) copy-start(bf16[1024,2048]{1,0:T(8,128)(2,1)} %copy-done.27) | copy-start | bytes 12582916
  424.2 3.1 copy-start.26
  852.3 6.8 copy-start.6
  859.1 4.6 copy-start.10
  863.7 2.6 copy-start.9
  866.2 4.0 copy-start.7
  866.3 4.0 copy-start.8
  866.3 5.9 copy-start.14
  868.8 4.9 copy-start.13
  872.1 3.1 copy-start.12
  872.1 4.7 copy-start.11
  (5 other events, 8.5 us)

commit v4 on v3

--- a/solution.py
+++ b/solution.py
@@ -404,330 +404,11 @@
     return terms / jnp.sum(terms, -1, keepdims=True), top
 
 
-def attention_forward_kernel(ranks, info, q_ref, k_ref, v_ref, out_ref, peak_ref, keys, values):
-    rows = keys.shape[0] // ranks
-    length = info[ranks]
-    for block in range(ranks):
-        at = pl.ds(pl.multiple_of(info[block], rows), rows)
-        keys[pl.ds(block * rows, rows), :] = k_ref[at, :]
-        values[pl.ds(block * rows, rows), :] = v_ref[at, :]
-    peak = jnp.full((1, 1), NEG, jnp.float32)
-    for block in range(ranks):
-        at = pl.ds(pl.multiple_of(info[block], rows), rows)
-        extent = (block + 1) * rows
-        probs, top = attention_probs(q_ref[at, :], keys[pl.ds(0, extent), :], block, length)
-        out_ref[at, :] = jnp.dot(
-            probs.astype(jnp.bfloat16),
-            values[pl.ds(0, extent), :],
-            preferred_element_type=jnp.float32,
-        ).astype(out_ref.dtype)
-        live = block * rows + lax.broadcasted_iota(jnp.int32, top.shape, 0) < length
-        peak = jnp.maximum(peak, jnp.max(jnp.where(live, top, NEG), 0, keepdims=True))
-    peak_ref[...] = jnp.broadcast_to(peak[None], peak_ref.shape)
-
-
-def attention_forward(info, qkv, head_size):
-    tokens, features = qkv.shape[0], qkv.shape[1] // 3
-    heads, ranks = features // head_size, info.shape[0] - 1
-
-    def part(k):
-        return pl.BlockSpec((tokens, head_size), lambda h, info: (0, k * heads + h))
-
-    attended, peaks = pl.pallas_call(
-        functools.partial(attention_forward_kernel, ranks),
-        out_shape=(
-            jax.ShapeDtypeStruct((tokens, features), jnp.bfloat16),
-            jax.ShapeDtypeStruct((heads, 8, 128), jnp.float32),
-        ),
-        grid_spec=pltpu.PrefetchScalarGridSpec(
-            num_scalar_prefetch=1,
-            grid=(heads,),
-            in_specs=[part(0), part(1), part(2)],
-            out_specs=(
-                pl.BlockSpec((tokens, head_size), lambda h, info: (0, h)),
-                pl.BlockSpec((1, 8, 128), lambda h, info: (h, 0, 0)),
-            ),
-            scratch_shapes=[pltpu.VMEM((tokens, head_size), jnp.bfloat16)] * 2,
-        ),
-        compiler_params=pltpu.CompilerParams(vmem_limit_bytes=40 << 20),
-        cost_estimate=pl.CostEstimate(
-            flops=4 * tokens * tokens * features, bytes_accessed=8 * tokens * features, transcendentals=0
-        ),
-    )(info, qkv, qkv, qkv)
-    return attended, peaks[:, 0, 0]
-
-
 def entry_barrier(targets):
     barrier = pltpu.get_barrier_semaphore()
     for target in targets:
         pl.semaphore_signal(barrier, inc=1, device_id=target, device_id_type=pl.DeviceIdType.MESH)
     pl.semaphore_wait(barrier, len(targets))
-
-
-def gather_kernel(
-    q_ref,
-    k_ref,
-    v_ref,
-    o_ref,
-    u_ref,
-    d_ref,
-    act_ref,
-    cot_ref,
-    res_ref,
-    qkv_all,
-    out_all,
-    up_all,
-    down_all,
-    act_all,
-    cot_all,
-    res_own,
-    local_sem,
-    send_sem,
-    recv_sem,
-    row_send,
-    row_recv,
-    join_send,
-    join_recv,
-):
-    f = lax.axis_index("fsdp")
-    z = lax.axis_index("ctx")
-    t = lax.axis_index("tp")
-    y, x = f // 2, f % 2
-    depth = act_ref.shape[0]
-    block_rows = act_ref.shape[1]
-    own_rows = depth * block_rows
-    strip = q_ref.shape[0]
-    features = q_ref.shape[1] // 2
-    hidden = u_ref.shape[1] // 2
-    even = z % 2 == 0
-    mate_z = z + 1 - 2 * (z % 2)
-    over_x = {"fsdp": 2 * y + 1 - x, "ctx": z, "tp": t}
-    over_y = {"fsdp": 2 * (1 - y) + x, "ctx": z, "tp": t}
-    over_z = {"fsdp": f, "ctx": mate_z, "tp": t}
-    over_core = {"fsdp": f, "ctx": z, "tp": 1 - t}
-    turned = x != t
-
-    def row_target(k):
-        return {"fsdp": 2 * y + t, "ctx": k, "tp": x}
-
-    targets = [over_x, over_y, over_z, over_core]
-    targets += [row_target(lax.rem(z + k, depth)) for k in range(1, depth)]
-    targets.append({"fsdp": 2 * y + 1 - x, "ctx": z, "tp": 1 - t})
-    entry_barrier(targets)
-
-    def at(start, size):
-        return pl.ds(pl.multiple_of(start, 128), size)
-
-    chunks = []
-    for k, ref in enumerate((q_ref, k_ref, v_ref)):
-        chunks.append(
-            (
-                lambda w, ref=ref: ref.at[:, at(w * features, features)],
-                lambda home, k=k: qkv_all.at[at(home * strip, strip), pl.ds(k * features, features)],
-            )
-        )
-    chunks.append(
-        (
-            lambda w: o_ref.at[at(w * features, features), :],
-            lambda home: out_all.at[:, at(home * strip, strip)],
-        )
-    )
-    pieces = 4
-    for k in range(pieces):
-        size = strip // pieces
-        chunks.append(
-            (
-                lambda w, k=k, size=size: u_ref.at[pl.ds(k * size, size), at(w * hidden, hidden)],
-                lambda home, k=k, size=size: up_all.at[at(home * strip + k * size, size), :],
-            )
-        )
-    for k in range(pieces):
-        size = hidden // pieces
-        chunks.append(
-            (
-                lambda w, k=k, size=size: d_ref.at[at(w * hidden + k * size, size), :],
-                lambda home, k=k, size=size: down_all.at[pl.ds(k * size, size), at(home * strip, strip)],
-            )
-        )
-    count = len(chunks)
-
-    def remote(src, dst, send, recv, target):
-        return pltpu.make_async_remote_copy(
-            src_ref=src,
-            dst_ref=dst,
-            send_sem=send,
-            recv_sem=recv,
-            device_id=target,
-            device_id_type=pl.DeviceIdType.MESH,
-        )
-
-    far_home = 2 * (1 - y) + x
-
-    def own_copy(i):
-        source, place = chunks[i]
-        return pltpu.make_async_copy(source(y), place(f), local_sem.at[i])
-
-    def y_copy(i):
-        source, place = chunks[i]
-        return remote(source(1 - y), place(f), send_sem.at[0, i], recv_sem.at[0, i], over_y)
-
-    def x_copy(i, is_even):
-        source, place = chunks[i]
-        if is_even:
-            return remote(source(y), place(f), send_sem.at[1, i], recv_sem.at[1, i], over_x)
-        return remote(
-            place(far_home), place(far_home), send_sem.at[1, i], recv_sem.at[1, i], over_x
-        )
-
-    def z_copy(i, is_even):
-        source, place = chunks[i]
-        home = 2 * y + 1 - x if is_even else 2 * (1 - y) + 1 - x
-        return remote(place(home), place(home), send_sem.at[2, i], recv_sem.at[2, i], over_z)
-
-    rows_of = ((act_ref, act_all), (cot_ref, cot_all), (res_ref, res_own))
-
-    def row_copy(a, k):
-        source, place = rows_of[a]
-        return remote(
-            source.at[k],
-            place.at[pl.ds(pl.multiple_of(z * block_rows, block_rows), block_rows), :],
-            row_send.at[a, k],
-            row_recv.at[a, z],
-            row_target(k),
-        )
-
-    def row_arrival(a, k):
-        source, place = rows_of[a]
-        return remote(
-            source.at[k],
-            place.at[pl.ds(k * block_rows, block_rows), :],
-            row_send.at[a, k],
-            row_recv.at[a, k],
-            row_target(k),
-        )
-
-    def row_stay(a, k):
-        source, place = rows_of[a]
-        return pltpu.make_async_copy(
-            source.at[k], place.at[pl.ds(k * block_rows, block_rows), :], row_send.at[a, k]
-        )
-
-    def rows_start(a):
-        for k in range(depth):
-            stays = (z == k) & (x == t)
-            pl.when(stays)(lambda k=k: row_stay(a, k).start())
-            pl.when(jnp.logical_not(stays))(lambda k=k: row_copy(a, k).start())
-
-    def rows_wait(a):
-        for k in range(depth):
-            stays = (z == k) & (x == t)
-            pl.when(stays)(lambda k=k: row_stay(a, k).wait())
-
-            @pl.when(jnp.logical_not(stays))
-            def _(k=k):
-                row_copy(a, k).wait_send()
-                row_arrival(a, k).wait_recv()
-
-    def block(a, k):
-        return rows_of[a][1].at[pl.ds(k * own_rows, own_rows), :]
-
-    def join_copy(a, step):
-        source, place, target = (
-            (0, 1, over_core),
-            (0, 2, over_y),
-            (2, 3, over_core),
-        )[step]
-        return remote(
-            block(a, source), block(a, place), join_send.at[a, step], join_recv.at[a, step], target
-        )
-
-    def join_start(a):
-        rows_wait(a)
-        join_copy(a, 0).start()
-        join_copy(a, 1).start()
-
-    def join_pass(a):
-        join_copy(a, 1).wait_recv()
-        join_copy(a, 2).start()
-
-    events = {
-        0: [lambda: rows_start(0)],
-        2: [lambda: rows_start(1), lambda: join_start(0)],
-        4: [lambda: rows_start(2), lambda: join_pass(0)],
-        6: [lambda: join_start(1)],
-        9: [lambda: join_pass(1)],
-    }
-    lag = 2
-    for i in range(count + 2 * lag):
-        for event in events.get(i, ()):
-            event()
-        if i < count:
-            y_copy(i).start()
-            pl.when(even)(lambda i=i: x_copy(i, True).start())
-            own_copy(i).start()
-        j = i - lag
-        if 0 <= j < count:
-            y_copy(j).wait_recv()
-
-            @pl.when(even)
-            def _(j=j):
-                x_copy(j, True).wait_recv()
-                z_copy(j, True).start()
-
-            pl.when(jnp.logical_not(even))(lambda j=j: x_copy(j, False).start())
-        j = i - 2 * lag
-        if 0 <= j < count:
-
-            @pl.when(jnp.logical_not(even))
-            def _(j=j):
-                x_copy(j, False).wait_recv()
-                z_copy(j, False).start()
-
-    for i in range(count):
-        own_copy(i).wait()
-        y_copy(i).wait_send()
-        x_copy(i, True).wait_send()
-        z_copy(i, True).wait()
-    for a in range(2):
-        join_copy(a, 0).wait()
-        join_copy(a, 1).wait_send()
-        join_copy(a, 2).wait()
-    rows_wait(2)
-
-
-def gather_all(query_weight, key_weight, value_weight, out_weight, up_weight, down_weight, act, cot, res):
-    strip, features, hidden = query_weight.shape[0], query_weight.shape[1] // 2, up_weight.shape[1] // 2
-    width = 4 * strip
-    own_rows = act.shape[0] * act.shape[1]
-    bf16 = jnp.bfloat16
-    hbm = pl.BlockSpec(memory_space=pl.ANY)
-    count = 12
-    dma = pltpu.SemaphoreType.DMA
-    return pl.pallas_call(
-        gather_kernel,
-        out_shape=(
-            jax.ShapeDtypeStruct((width, 3 * features), bf16),
-            jax.ShapeDtypeStruct((features, width), bf16),
-            jax.ShapeDtypeStruct((width, hidden), bf16),
-            jax.ShapeDtypeStruct((hidden, width), bf16),
-            jax.ShapeDtypeStruct((4 * own_rows, width), bf16),
-            jax.ShapeDtypeStruct((4 * own_rows, width), bf16),
-            jax.ShapeDtypeStruct((own_rows, width), jnp.float32),
-        ),
-        in_specs=[hbm] * 9,
-        out_specs=(hbm,) * 7,
-        scratch_shapes=[
-            dma((count,)),
-            dma((3, count)),
-            dma((3, count)),
-            dma((3, act.shape[0])),
-            dma((3, act.shape[0])),
-            dma((2, 3)),
-            dma((2, 3)),
-        ],
-        compiler_params=pltpu.CompilerParams(collective_id=0, has_side_effects=True),
-        cost_estimate=pl.CostEstimate(flops=0, bytes_accessed=64 << 20, transcendentals=0),
-    )(query_weight, key_weight, value_weight, out_weight, up_weight, down_weight, act, cot, res)
 
 
 def remote_copy(src, dst, send, recv, target):
@@ -1054,6 +735,508 @@
     8,
     12,
 )
+
+
+def forward_kernel(
+    head_size,
+    info,
+    vec_hbm,
+    head_hbm,
+    q_ref,
+    k_ref,
+    v_ref,
+    o_ref,
+    u_ref,
+    d_ref,
+    arrived_hbm,
+    cot_hbm,
+    qkv_mat_out,
+    out_mat_out,
+    up_all,
+    down_all,
+    act_out,
+    cot_all,
+    qkv_out,
+    attended_out,
+    hidden_out,
+    resid_out,
+    two_out,
+    vec_all,
+    peaks,
+    qkv_mat,
+    out_mat,
+    fresh,
+    part,
+    act,
+    hidden,
+    qkv,
+    keys,
+    values,
+    attended,
+    partial,
+    arrived,
+    sent,
+    two,
+    vec_own,
+    head_own,
+    head_got,
+    qkv_bias,
+    local_sem,
+    send_sem,
+    recv_sem,
+    row_send,
+    row_recv,
+    join_send,
+    join_recv,
+    vec_send,
+    vec_recv,
+    load_sem,
+    sum_send,
+    sum_recv,
+    out_sem,
+):
+    f32, bf16 = jnp.float32, jnp.bfloat16
+    depth, block_rows, width = arrived_hbm.shape
+    own_rows = depth * block_rows
+    strip = q_ref.shape[0]
+    features = q_ref.shape[1] // 2
+    units = u_ref.shape[1] // 2
+    heads = features // head_size
+    p = Place(depth)
+    f, x, y, z, t = p.f, p.x, p.y, p.z, p.t
+    even = z % 2 == 0
+    odd = jnp.logical_not(even)
+    diagonal = {"fsdp": 3 - f, "ctx": z, "tp": t}
+    entry_barrier([p.over_x, p.over_y, p.mate, p.over_core, diagonal] + p.row_targets())
+    length = info[0]
+
+    chunks = []
+    rows = strip // 2
+    for k, ref in enumerate((q_ref, k_ref, v_ref)):
+        for r in range(2):
+            chunks.append(
+                (
+                    lambda w, ref=ref, r=r: ref.at[pl.ds(r * rows, rows), aligned(w * features, features)],
+                    lambda home, k=k, r=r: qkv_mat.at[
+                        aligned(home * strip + r * rows, rows), pl.ds(k * features, features)
+                    ],
+                )
+            )
+    for r in range(2):
+        chunks.append(
+            (
+                lambda w, r=r: o_ref.at[aligned(w * features + r * rows, rows), :],
+                lambda home, r=r: out_mat.at[pl.ds(r * rows, rows), aligned(home * strip, strip)],
+            )
+        )
+    pieces = 8
+    for r in range(pieces):
+        size = strip // pieces
+        chunks.append(
+            (
+                lambda w, r=r, size=size: u_ref.at[pl.ds(r * size, size), aligned(w * units, units)],
+                lambda home, r=r, size=size: up_all.at[
+                    pl.ds(pl.multiple_of(home * strip + r * size, size), size), :
+                ],
+            )
+        )
+    for r in range(pieces):
+        size = units // pieces
+        chunks.append(
+            (
+                lambda w, r=r, size=size: d_ref.at[aligned(w * units + r * size, size), :],
+                lambda home, r=r, size=size: down_all.at[pl.ds(r * size, size), aligned(home * strip, strip)],
+            )
+        )
+    count = len(chunks)
+    far_home = 2 * (1 - y) + x
+
+    def own_copy(i):
+        source, place = chunks[i]
+        return pltpu.make_async_copy(source(y), place(f), local_sem.at[i])
+
+    def y_copy(i):
+        source, place = chunks[i]
+        return remote_copy(source(1 - y), place(f), send_sem.at[0, i], recv_sem.at[0, i], p.over_y)
+
+    def x_copy(i, is_even):
+        source, place = chunks[i]
+        start = source(y) if is_even else place(far_home)
+        home = f if is_even else far_home
+        return remote_copy(start, place(home), send_sem.at[1, i], recv_sem.at[1, i], p.over_x)
+
+    def z_copy(i, is_even):
+        place = chunks[i][1]
+        home = 2 * y + 1 - x if is_even else 2 * (1 - y) + 1 - x
+        return remote_copy(place(home), place(home), send_sem.at[2, i], recv_sem.at[2, i], p.mate)
+
+    rows_of = ((part, act), (cot_hbm, cot_all), (arrived_hbm, hidden))
+
+    def row_copy(a, k):
+        source, place = rows_of[a]
+        return remote_copy(
+            source.at[k],
+            place.at[pl.ds(pl.multiple_of(z * block_rows, block_rows), block_rows), :],
+            row_send.at[a, k],
+            row_recv.at[a, z],
+            p.row_target(k),
+        )
+
+    def row_arrival(a, k):
+        source, place = rows_of[a]
+        return remote_copy(
+            source.at[k],
+            place.at[pl.ds(k * block_rows, block_rows), :],
+            row_send.at[a, k],
+            row_recv.at[a, k],
+            p.row_target(k),
+        )
+
+    def row_stay(a, k):
+        source, place = rows_of[a]
+        return pltpu.make_async_copy(
+            source.at[k], place.at[pl.ds(k * block_rows, block_rows), :], row_send.at[a, k]
+        )
+
+    def rows_start(a):
+        for k in range(depth):
+            stays = (z == k) & (x == t)
+            pl.when(stays)(lambda k=k: row_stay(a, k).start())
+            pl.when(jnp.logical_not(stays))(lambda k=k: row_copy(a, k).start())
+
+    def rows_wait(a):
+        for k in range(depth):
+            stays = (z == k) & (x == t)
+            pl.when(stays)(lambda k=k: row_stay(a, k).wait())
+
+            @pl.when(jnp.logical_not(stays))
+            def _(k=k):
+                row_copy(a, k).wait_send()
+                row_arrival(a, k).wait_recv()
+
+    joined = (act, cot_all, two)
+
+    def block(ref, k):
+        return ref.at[pl.ds(k * own_rows, own_rows), :]
+
+    def join(a, step):
+        source, place, target = ((0, 1, p.over_core), (0, 2, p.over_y), (2, 3, p.over_core))[step]
+        ref = joined[a]
+        return remote_copy(
+            block(ref, source), block(ref, place), join_send.at[a, step], join_recv.at[a, step], target
+        )
+
+    def join_start(a):
+        join(a, 0).start()
+        join(a, 1).start()
+
+    def join_pass(a):
+        join(a, 1).wait_recv()
+        join(a, 2).start()
+
+    def join_end(a):
+        join(a, 0).wait()
+        join(a, 1).wait_send()
+        join(a, 2).wait()
+
+    def vec_place(ref):
+        return ref.at[:, aligned(f * strip, strip)]
+
+    vec_targets = (p.over_x, p.over_y, diagonal)
+
+    def vec_copy(k):
+        return remote_copy(vec_own, vec_place(vec_all), vec_send.at[0, k], vec_recv.at[0, k], vec_targets[k])
+
+    def head_copy(k):
+        return remote_copy(head_own, head_got.at[k], vec_send.at[1, k], vec_recv.at[1, k], vec_targets[k])
+
+    loads = [
+        pltpu.make_async_copy(source, target, load_sem.at[k])
+        for k, (source, target) in enumerate(
+            ((vec_hbm, vec_own), (head_hbm, head_own), (arrived_hbm, fresh))
+        )
+    ]
+
+    def begin():
+        for load in loads:
+            load.start()
+        loads[0].wait()
+        loads[1].wait()
+        for k in range(3):
+            vec_copy(k).start()
+            head_copy(k).start()
+        vec_place(vec_all)[...] = vec_own[...]
+        peaks[...] = jnp.full_like(peaks, NEG)
+
+    def vector_row(k):
+        return vec_all[pl.ds(k, 1), :]
+
+    group_rows = 16
+
+    def first_norm():
+        for k in range(3):
+            vec_copy(k).wait()
+            head_copy(k).wait()
+        loads[2].wait()
+        for k in range(3):
+            head_own[...] += head_got[k]
+        qkv_bias[...] = jnp.zeros_like(qkv_bias)
+        for h in range(heads):
+            lanes = pl.ds(h * head_size, head_size)
+            qkv_bias[pl.ds(0, 1), lanes] = head_own[pl.ds(heads * y + h, 1), :]
+            lanes = pl.ds(2 * features + h * head_size, head_size)
+            qkv_bias[pl.ds(0, 1), lanes] = head_own[pl.ds(2 * heads + heads * y + h, 1), :]
+        gain, shift = vector_row(GAIN_ONE), vector_row(SHIFT_ONE)
+        for s in range(depth):
+
+            @pl.loop(0, block_rows // group_rows)
+            def _(k, s=s):
+                at = pl.ds(pl.multiple_of(k * group_rows, group_rows), group_rows)
+                unit, _ = unit_rows(fresh[s, at, :])
+                part[s, at, :] = (unit * gain + shift).astype(bf16)
+
+        rows_start(0)
+
+    def weights_wait(start, stop):
+        for i in range(start, stop):
+            own_copy(i).wait()
+            z_copy(i, True).wait_recv()
+
+    kept, used = [], [0]
+
+    def keep(source, target):
+        copy = pltpu.make_async_copy(source, target, out_sem.at[used[0]])
+        used[0] += 1
+        copy.start()
+        kept.append(copy)
+
+    def project(k):
+        at = pl.ds(k * own_rows, own_rows)
+
+        @pl.loop(0, 3)
+        def _(c):
+            cut = aligned(c * features, features)
+            qkv[at, cut] = (
+                jnp.dot(act[at, :], qkv_mat[:, cut], preferred_element_type=f32)
+                + qkv_bias[pl.ds(0, 1), cut]
+            ).astype(bf16)
+
+    def head_rows():
+        for b in range(4):
+            at = pl.ds(pl.multiple_of(p.block_place(b) * own_rows, own_rows), own_rows)
+            keys[pl.ds(b * own_rows, own_rows), :] = qkv[at, pl.ds(features, features)]
+            values[pl.ds(b * own_rows, own_rows), :] = qkv[at, pl.ds(2 * features, features)]
+
+    def attention_block(b):
+        at = pl.ds(pl.multiple_of(p.block_place(b) * own_rows, own_rows), own_rows)
+        past = pl.ds(0, (b + 1) * own_rows)
+
+        @pl.loop(0, heads)
+        def _(head):
+            lanes = aligned(head * head_size, head_size)
+            probs, top = attention_probs(qkv[at, lanes], keys[past, lanes], b, length)
+            attended[at, lanes] = jnp.dot(
+                probs.astype(bf16), values[past, lanes], preferred_element_type=f32
+            ).astype(bf16)
+            live = b * own_rows + lax.broadcasted_iota(jnp.int32, top.shape, 0) < length
+            peak = jnp.max(jnp.where(live, top, NEG), 0, keepdims=True)
+            row = pl.ds(head, 1)
+            peaks[row, :] = jnp.maximum(peaks[row, :], jnp.broadcast_to(peak, (1, peaks.shape[1])))
+
+    sums = RowSum(p, own_rows, arrived, sent, None, sum_send, sum_recv, None, None, None, 1)
+
+    def out_block(k):
+        at = pl.ds(k * own_rows, own_rows)
+
+        @pl.loop(0, 4)
+        def _(n):
+            cut = aligned(n * strip, strip)
+            partial[at, cut] = jnp.dot(
+                attended[at, :], out_mat[:, cut], preferred_element_type=f32
+            ).astype(bf16)
+
+    def second_norm():
+        sums.finish(partial, True)
+        kept[-1].wait()
+        kept.pop()
+        bias, gain, shift = vector_row(OUT_BIAS), vector_row(GAIN_TWO), vector_row(SHIFT_TWO)
+
+        @pl.loop(0, own_rows // group_rows)
+        def _(k):
+            at = pl.ds(pl.multiple_of(k * group_rows, group_rows), group_rows)
+            value = hidden[at, :] + sums.total(partial, True, at) + bias
+            hidden[at, :] = value
+            unit, _ = unit_rows(value)
+            two[at, :] = (unit * gain + shift).astype(bf16)
+
+        join_start(2)
+        keep(hidden, hidden_out)
+
+    def call(function, *arguments):
+        return lambda: function(*arguments)
+
+    plan = {}
+
+    def at_step(step, *tasks):
+        plan.setdefault(step, []).extend(tasks)
+
+    at_step(0, begin)
+    at_step(1, first_norm)
+    at_step(2, call(rows_start, 1))
+    at_step(3, call(rows_wait, 0), call(join_start, 0))
+    at_step(4, call(rows_start, 2))
+    at_step(7, call(join_pass, 0))
+    at_step(9, call(join_end, 0), lambda: keep(act, act_out))
+    at_step(10, call(weights_wait, 0, 6), call(project, 0), lambda: keep(qkv_mat, qkv_mat_out))
+    at_step(10, call(project, 1))
+    at_step(11, call(project, 2), call(project, 3), head_rows, lambda: keep(qkv, qkv_out))
+    at_step(12, *(call(attention_block, b) for b in range(4)))
+    at_step(13, lambda: keep(attended, attended_out), call(weights_wait, 6, 8), call(out_block, 3))
+    at_step(13, call(out_block, 1), call(sums.start, 0, partial, True), call(out_block, 2))
+    at_step(13, call(sums.middle, partial, True), call(out_block, 0))
+    at_step(14, lambda: keep(out_mat, out_mat_out), call(rows_wait, 2), lambda: keep(hidden, resid_out))
+    at_step(17, second_norm)
+    at_step(18, call(rows_wait, 1), call(join_start, 1))
+    at_step(21, call(join_pass, 2))
+    at_step(22, call(join_end, 2), lambda: keep(two, two_out))
+    at_step(24, call(join_pass, 1))
+    lag = 2
+    for i in range(count + 2 * lag):
+        if i < count:
+            y_copy(i).start()
+            pl.when(even)(lambda i=i: x_copy(i, True).start())
+            own_copy(i).start()
+        j = i - lag
+        if 0 <= j < count:
+            y_copy(j).wait_recv()
+
+            @pl.when(even)
+            def _(j=j):
+                x_copy(j, True).wait_recv()
+                z_copy(j, True).start()
+
+            pl.when(odd)(lambda j=j: x_copy(j, False).start())
+        j = i - 2 * lag
+        if 0 <= j < count:
+
+            @pl.when(odd)
+            def _(j=j):
+                x_copy(j, False).wait_recv()
+                z_copy(j, False).start()
+
+        for task in plan.get(i, ()):
+            task()
+
+    weights_wait(8, count)
+    for i in range(count):
+        y_copy(i).wait_send()
+        x_copy(i, True).wait_send()
+        z_copy(i, True).wait_send()
+    join_end(1)
+    for copy in kept:
+        copy.wait()
+
+
+def forward_all(
+    head_size,
+    length,
+    vectors,
+    head_vectors,
+    query_weight,
+    key_weight,
+    value_weight,
+    out_weight,
+    up_weight,
+    down_weight,
+    arrived,
+    cot,
+):
+    strip, features, units = query_weight.shape[0], query_weight.shape[1] // 2, up_weight.shape[1] // 2
+    width = 4 * strip
+    depth, block_rows = arrived.shape[:2]
+    own_rows = depth * block_rows
+    tokens = 4 * own_rows
+    bf16, f32 = jnp.bfloat16, jnp.float32
+    hbm = pl.BlockSpec(memory_space=pl.ANY)
+    vmem = pl.BlockSpec(memory_space=pltpu.VMEM)
+    count = 24
+    dma = pltpu.SemaphoreType.DMA
+
+    def made(shape, dtype=bf16):
+        return jax.ShapeDtypeStruct(shape, dtype)
+
+    def hold(shape, dtype=bf16):
+        return pltpu.VMEM(shape, dtype)
+
+    return pl.pallas_call(
+        functools.partial(forward_kernel, head_size),
+        out_shape=(
+            made((width, 3 * features)),
+            made((features, width)),
+            made((width, units)),
+            made((units, width)),
+            made((tokens, width)),
+            made((tokens, width)),
+            made((tokens, 3 * features)),
+            made((tokens, features)),
+            made((own_rows, width), f32),
+            made((own_rows, width), f32),
+            made((tokens, width)),
+            made((8, width), f32),
+            made((8, 128), f32),
+        ),
+        in_specs=[pl.BlockSpec(memory_space=pltpu.SMEM)] + [hbm] * 10,
+        out_specs=(hbm,) * 11 + (vmem,) * 2,
+        scratch_shapes=[
+            hold((width, 3 * features)),
+            hold((features, width)),
+            hold((depth, block_rows, width), f32),
+            hold((depth, block_rows, width)),
+            hold((tokens, width)),
+            hold((own_rows, width), f32),
+            hold((tokens, 3 * features)),
+            hold((tokens, features)),
+            hold((tokens, features)),
+            hold((tokens, features)),
+            hold((tokens, width)),
+            hold((3, own_rows, width)),
+            hold((own_rows, width)),
+            hold((tokens, width)),
+            hold((8, strip), f32),
+            hold(head_vectors.shape, f32),
+            hold((3,) + head_vectors.shape, f32),
+            hold((8, 3 * features), f32),
+            dma((count,)),
+            dma((3, count)),
+            dma((3, count)),
+            dma((3, depth)),
+            dma((3, depth)),
+            dma((3, 3)),
+            dma((3, 3)),
+            dma((2, 3)),
+            dma((2, 3)),
+            dma((3,)),
+            dma((3,)),
+            dma((3,)),
+            dma((8,)),
+        ],
+        compiler_params=pltpu.CompilerParams(
+            collective_id=0, has_side_effects=True, vmem_limit_bytes=56 << 20
+        ),
+        cost_estimate=pl.CostEstimate(flops=0, bytes_accessed=64 << 20, transcendentals=0),
+    )(
+        length,
+        vectors,
+        head_vectors,
+        query_weight,
+        key_weight,
+        value_weight,
+        out_weight,
+        up_weight,
+        down_weight,
+        arrived,
+        cot,
+    )
 
 
 def backward_kernel(
@@ -1657,34 +1840,6 @@
     strip = query_weight.shape[0]
     own_rows = depth * block_rows
 
-    over_x = [(0, 1), (1, 0), (2, 3), (3, 2)]
-    over_y = [(0, 2), (2, 0), (1, 3), (3, 1)]
-    x_core = [(0, 0), (1, 2), (2, 1), (3, 3), (4, 4), (5, 6), (6, 5), (7, 7)]
-
-    def across_x(v):
-        return lax.ppermute(v, "fsdp", over_x)
-
-    def across_y(v):
-        return lax.ppermute(v, "fsdp", over_y)
-
-    def across_core(v):
-        return lax.ppermute(v, "tp", [(0, 1), (1, 0)])
-
-    def half(v, which, axis):
-        size = v.shape[axis] // 2
-        return lax.dynamic_slice_in_dim(v, which * size, size, axis)
-
-    def gather_rows(own):
-        peer = across_core(own)
-        far = across_y(own)
-        far_peer = across_core(far)
-        return jnp.concatenate([own, peer], 0), jnp.concatenate([far, far_peer], 0)
-
-    def scatter_rows(near, far):
-        far_mine = far[:own_rows] + across_core(far[own_rows:].astype(bf16)).astype(f32)
-        arrived = across_y(far_mine.astype(bf16)).astype(f32)
-        return near[:own_rows] + across_core(near[own_rows:].astype(bf16)).astype(f32) + arrived
-
     def strip_of(v, home):
         return lax.dynamic_slice_in_dim(v, home * strip, strip, 1)
 
@@ -1695,53 +1850,46 @@
 
     slot = x * depth + z
     length = seq_lengths[dealing[slot]]
-    own_rank = 2 * y + t
-    near_rank = 2 * y + 1 - t
-    far_rank = 2 * (1 - y) + t
-    places = jnp.zeros((4,), jnp.int32)
-    for k, rank in enumerate((own_rank, near_rank, far_rank, 2 * (1 - y) + 1 - t)):
-        places = places.at[rank].set(k * own_rows)
-    info = jnp.concatenate([places, length[None]])
-
-    small = jnp.stack([attn_gain, attn_shift, out_bias, mlp_gain, mlp_shift, down_bias])
-    small = lax.all_gather(small, "fsdp", axis=1, tiled=True).astype(f32)
-    vectors_whole = small
-    gain_one, shift_one, out_vec, gain_two, shift_two, down_vec = [small[k] for k in range(6)]
-    vectors = jnp.concatenate([query_bias, value_bias, up_bias.reshape(-1, query_bias.shape[1])], 0)
-    vectors = lax.all_gather(vectors, "fsdp", axis=0, tiled=False)
-    nb = query_bias.shape[0]
-    query_vec = half(vectors[:, :nb].transpose(1, 0, 2).reshape(-1), y, 0).astype(f32)
-    value_vec = half(vectors[:, nb : 2 * nb].transpose(1, 0, 2).reshape(-1), y, 0).astype(f32)
-    up_vec = half(
-        vectors[:, 2 * nb :].reshape(4, up_bias.shape[0], -1).transpose(1, 0, 2).reshape(-1), y, 0
-    ).astype(f32)
-
     arrived = pick_slots(layer_input, dealing, t * depth, depth)
     cot_part = lax.dynamic_slice_in_dim(cotangent, t * depth, depth, 0)
     down_bias_part = jnp.sum(cot_part, (0, 1))
-    act_part = normalize(arrived, gain_one, shift_one)[0].astype(bf16)
-    qkv_mat, out_mat, up_mat, down_mat, act_one, cot_low, resid = gather_all(
+    vectors = jnp.concatenate(
+        [jnp.stack([attn_gain, attn_shift, out_bias, mlp_gain, mlp_shift, down_bias]), up_bias], 0
+    ).astype(f32)
+    head_vectors = jnp.concatenate([query_bias, value_bias], 0).astype(f32)
+    head_vectors = lax.dynamic_update_slice(
+        jnp.zeros((head_vectors.shape[0], head_size), f32), head_vectors, (0, f * query_bias.shape[1])
+    )
+    (
+        qkv_mat,
+        out_mat,
+        up_mat,
+        down_mat,
+        act_one,
+        cot_low,
+        qkv,
+        attended,
+        hidden,
+        resid,
+        act_two,
+        vectors_whole,
+        peaks,
+    ) = forward_all(
+        head_size,
+        length[None],
+        vectors,
+        head_vectors,
         query_weight,
         key_weight,
         value_weight,
         out_weight,
         up_weight,
         down_weight,
-        act_part,
+        arrived,
         cot_part.astype(bf16),
-        arrived,
-    )
-    cot_own = cot_low[:own_rows]
-
-    qkv_vec = jnp.concatenate([query_vec, jnp.zeros_like(query_vec), value_vec])
-    qkv = (matmul(act_one, qkv_mat) + qkv_vec).astype(bf16)
-    attended, peaks = attention_forward(info, qkv, head_size)
-    chip_rows = 2 * own_rows
-    attn_far = matmul(attended[chip_rows:], out_mat)
-    attn_near = matmul(attended[:chip_rows], out_mat)
-    hidden = resid + scatter_rows(attn_near, attn_far) + out_vec
-    normed_b = normalize(hidden, gain_two, shift_two)[0]
-    act_two = jnp.concatenate(gather_rows(normed_b.astype(bf16)), 0)
+    )
+    peaks = peaks[:local_heads, 0]
+    up_vec = lax.dynamic_slice_in_dim(vectors_whole, 6 + y, 1, 0)
 
     pre = matmul(act_two, up_mat) + up_vec
     cdf = 0.5 * (1.0 + lax.erf(pre * INV_ROOT_TWO))

time: 886 us -> 852 us (0.962)
  Pallas kernels: 636 us -> 693 us
  waiting for transfers between devices: 50.6 us -> 0 us
  blocking collectives: 17.8 us -> 0 us
  starting transfers between devices: 11.3 us -> 0 us
    pallas_call x2 -> x1, Pallas kernels: 239 us -> 295 us  [forward_all(): pl.pallas_call(functools.partial(forward_kernel, head_size), out_shape=(m...]
    ppermute x6 -> x0, waiting for transfers between devices: 50.6 us -> none  [the longest x2 48.4 us: across_y(): return lax.ppermute(v, 'fsdp', over_y)]
    dot_general x5 -> x2, matrix products: 43.6 us -> 25.7 us  [matmul(): return jnp.dot(left, right, preferred_element_type=jnp.float32)]
    all_gather x2 -> x0, blocking collectives: 17.8 us -> none  [the longest x1 9.62 us: split_body(): small = lax.all_gather(small, 'fsdp', axis=1, tiled=True).astype(f32)]
    ppermute x6 -> x0, starting transfers between devices: 11.3 us -> none  [the longest x4 10.8 us: across_core(): return lax.ppermute(v, 'tp', [(0, 1), (1, 0)])]
    dot_general x8, matrix products: 30.3 us -> 40.6 us  [weight_product(): jnp.einsum('td,te->de', left, right, preferred_element_type=jnp.float32)]
  transfers between devices with their start and end apart: 6 -> 0, of which waited for: 4 -> 0; matrix products, arithmetic and copies ran while one was open for 1% -> 0% of each run, Pallas kernels for 0% -> 0%
where the time goes in v4:
time: 852 us; the launch traced here: 844 us
  Pallas kernels  693 us (81%)
  matrix products  95.2 us (11%)
  other arithmetic  29.8 us (3%)
  local copies, waits for them, and re-layouts  13.7 us (2%)
  between operations  12 us (1%)
    pallas_call x1, Pallas kernels, backward_all(): pl.pallas_call(kernel, out_shape=(jax.ShapeDtypeStruct((2 * down_rows, st...  398 us
    pallas_call x1, Pallas kernels, forward_all(): pl.pallas_call(functools.partial(forward_kernel, head_size), out_shape=(m...  295 us
    dot_general x8, matrix products, weight_product(): jnp.einsum('td,te->de', left, right, preferred_element_type=jnp.float32)  40.6 us
    dot_general x2, matrix products, back_product(): jnp.einsum('te,de->td', left, right, preferred_element_type=jnp.float32)  28.9 us
    dot_general x2, matrix products, matmul(): return jnp.dot(left, right, preferred_element_type=jnp.float32)  25.7 us

profile of v4, /device:TPU:0, one launch (start us, length us, event | category | flops | bytes accessed | tf_op | source)
XLA Modules:
  0.0 843.8 jit_solution(4069824322361604646)
XLA Ops:
  0.7 1.4 fusion.25
  9.9 1.7 constant_dynamic-slice_fusion.7
  11.7 1.5 pad_maximum_fusion.arrived_hbm
  15.7 2.7 dynamic-slice_convert_fusion.cot_hbm
  19.5 295.1 %shard_map.347 = (bf16[2048,1536]{1,0:T(8,128)(2,1)}, bf16[512,2048]{1,0:T(8,128)(2,1)}, bf16[2048,2048]{1,0:T(8,128)(2,1)}, bf16[2048,2048]{1,0:T(8,128)(2,1)},...) custom-call(s32[1]{0:T(128)} %dynamic_slice.76.info.refs_0_, ...), custom_call_target="tpu_custom_call" | custom-call | bytes 67108864 | tf_op jit(solution)/shard_map/pallas_call | solution.py:1171
  314.5 0.9 constant_dynamic-slice_fusion.3
  315.4 15.2 %multiply_convert_fusion = (bf16[1024,2048]{1,0:T(8,128)(2,1)S(1)}, f32[1024,2048]{1,0:T(8,128)}) fusion(f32[2048]{0:T(1024)S(1)} %bitcast.50, bf16[1024,2048]{1,0:T(8,128)(2,1)} %get-tuple-element.69, bf16[2048,2048]{1,0:T(8,128)(2,1)} %get-tuple-element.70), kind=kOutput, calls=%fused_computation.6 | convolution fusion | flops 8602517504 | bytes 25174016 | tf_op jit(solution)/shard_map/dot_general | solution.py:41
  330.6 10.6 %convolution_convert_fusion.refs_12_ = bf16[1024,2048]{1,0:T(8,128)(2,1)} fusion(bf16[1024,2048]{1,0:T(8,128)(2,1)S(1)} %get-tuple-element.112, bf16[2048,2048]{1,0:T(8,128)(2,1)S(1)} %copy-done.23), kind=kOutput, calls=%fused_computation.8 | convolution fusion | flops 8592031744 | bytes 16777216 | tf_op jit(solution)/shard_map/dot_general | solution.py:41
  341.2 16.5 %fusion.23 = (bf16[1024,2048]{1,0:T(8,128)(2,1)}, f32[2048]{0:T(1024)S(1)}) fusion(f32[1024,2048]{1,0:T(8,128)} %get-tuple-element.113, f32[2048]{0:T(1024)S(1)} %bitcast.51, bf16[1024,2048]{1,0:T(8,128)(2,1)S(1)} %copy-done, bf16[2048,2048]{1,0:T(8,128)(2,1)} %get-tuple-element.68), kind=kOutput, calls=%fused_computation.56 | convolution fusion | flops 8615098368 | bytes 25182208 | tf_op jit(solution)/shard_map/te,de->td/dot_general | solution.py:49
  357.7 12.4 %convolution_convert_fusion.1.refs_11_ = bf16[1024,2048]{1,0:T(8,128)(2,1)} fusion(bf16[1024,2048]{1,0:T(8,128)(2,1)} %get-tuple-element.90, bf16[2048,2048]{1,0:T(8,128)(2,1)S(1)} %bitcast.60), kind=kOutput, calls=%fused_computation.9 | convolution fusion | flops 8592031744 | bytes 16777216 | tf_op jit(solution)/shard_map/te,de->td/dot_general | solution.py:49
  370.1 6.2 convolution_convert_fusion.2.refs_10_
  376.3 6.2 convolution_convert_fusion.3.refs_9_
  382.5 6.3 convolution_convert_fusion.4.refs_8_
  388.8 6.3 convolution_convert_fusion.5.refs_7_
  395.1 3.8 convolution_convert_fusion.6.refs_6_
  398.9 4.2 convolution_convert_fusion.7.refs_5_
  403.1 3.8 convolution_convert_fusion.8.refs_4_
  406.9 3.8 convolution_convert_fusion.9.refs_3_
  410.7 1.7 dynamic-slice_reduce_fusion
  413.9 398.1 %shard_map.348 = (bf16[4096,512]{1,0:T(8,128)(2,1)}, bf16[512,4096]{1,0:T(8,128)(2,1)}, bf16[1024,512]{1,0:T(8,128)(2,1)}, bf16[512,1024]{1,0:T(8,128)(2,1)}, bf...) custom-call(s32[1]{0:T(128)} %dynamic_slice.76.info.refs_0_, ...), custom_call_target="tpu_custom_call" | custom-call | bytes 67108864 | tf_op jit(solution)/shard_map/pallas_call | solution.py:1729
  812.0 6.8 convert_element_type.102
  818.8 4.6 convert_element_type.103
  823.4 2.5 convert_element_type.96
  826.0 2.5 convert_element_type.97
  829.3 1.3 divide_sqrt_fusion
  830.6 1.9 multiply_convert_fusion.1
  832.5 1.6 convert_element_type.100
  834.1 1.6 convert_element_type.101
  835.7 1.6 convert_element_type.98
  837.3 1.6 convert_element_type.99
  840.4 1.6 fusion.24
  842.0 1.4 dynamic_slice.98
  (81 shorter events, 4.6 us)
Async XLA Ops:
  9.9 5.2 copy-start.24
  11.6 6.8 copy-start.13
  11.6 6.8 copy-start.14
  11.6 7.1 copy-start.16
  11.6 7.1 copy-start.17
  11.6 7.1 copy-start.18
  11.6 7.1 copy-start.19
  11.7 7.1 copy-start.20
  11.7 7.1 copy-start.21
  11.7 7.1 copy-start.15
  18.7 0.8 copy-start.12
  315.4 15.2 %copy-start.23 = (bf16[2048,2048]{1,0:T(8,128)(2,1)S(1)}, bf16[2048,2048]{1,0:T(8,128)(2,1)}, u32[]{:S(2)}) copy-start(bf16[2048,2048]{1,0:T(8,128)(2,1)} %get-tuple-element.68) | copy-start | bytes 25165828
  330.6 10.6 %copy-start.25 = (bf16[1024,2048]{1,0:T(8,128)(2,1)}, bf16[1024,2048]{1,0:T(8,128)(2,1)S(1)}, u32[]{:S(2)}) copy-start(bf16[1024,2048]{1,0:T(8,128)(2,1)S(1)} %get-tuple-element.112) | copy-start | bytes 12582916
  330.6 10.6 %copy-start = (bf16[1024,2048]{1,0:T(8,128)(2,1)S(1)}, bf16[1024,2048]{1,0:T(8,128)(2,1)}, u32[]{:S(2)}) copy-start(bf16[1024,2048]{1,0:T(8,128)(2,1)} %get-tuple-element.67.refs_14_) | copy-start | bytes 12582916
  330.6 27.1 %slice-start = ((s8[8388608]{0:T(1024)(128)(4,1)}), s8[4194304]{0:T(1024)(128)(4,1)S(1)}, s32[]{:S(2)}) async-start(s8[8388608]{0:T(1024)(128)(4,1)} %bitcast.59), calls=%async_computation | async-start | bytes 8388608
  341.2 16.5 %slice-start.1 = ((s8[8388608]{0:T(1024)(128)(4,1)}), s8[4194304]{0:T(1024)(128)(4,1)S(1)}, s32[]{:S(2)}) async-start(s8[8388608]{0:T(1024)(128)(4,1)} %bitcast.59), calls=%async_computation.1 | async-start | bytes 8388608
  388.8 6.4 copy-start.1
  388.8 6.4 copy-start.26
  406.9 6.0 copy-start.22
  413.2 0.7 copy-start.11
  812.0 6.8 copy-start.2
  818.8 4.6 copy-start.6
  823.4 2.6 copy-start.5
  825.9 4.7 copy-start.3
  825.9 4.7 copy-start.4
  828.5 5.6 copy-start.9
  828.5 4.0 copy-start.10
  832.5 3.2 copy-start.8
  832.5 4.8 copy-start.7

commit v5 on v4

--- a/solution.py
+++ b/solution.py
@@ -457,9 +457,10 @@
         return 2 * jnp.where(self.y == block // 2, 0, 1) + jnp.where(self.t == block % 2, 0, 1)
 
 
-def reduce_stages(p, groups, scratch):
+def reduce_stages(p, items, scratch):
     (
         x_slot,
+        made_slot,
         own_slot,
         pair_slot,
         y_slot,
@@ -469,7 +470,6 @@
         total_slot,
         x_send,
         x_recv,
-        own_sem,
         y_send,
         y_recv,
         outer_send,
@@ -485,26 +485,14 @@
     y, z = p.y, p.z
     outer = (z == 0) | (z == 3)
     inner = (z == 1) | (z == 2)
-    slots, rows, cols = x_slot.shape
-    items = []
-    for parts, row_count, col_count, place in groups:
-        near_send, far_send, near_own, far_own = parts
-        for r in range(row_count):
-            for c in range(col_count):
-                cut = (pl.ds(r * rows, rows), pl.ds(c * cols, cols))
-                items.append((True, far_send.at[cut], far_own.at[cut], place(1 - y, r, c)))
-                items.append((False, near_send.at[cut], near_own.at[cut], place(y, r, c)))
+    slots = x_slot.shape[0]
     count = len(items)
     far_count = count // 2
     far_slots = y_slot.shape[0]
 
     def x_copy(i):
         k = i % slots
-        return remote_copy(items[i][1], x_slot.at[k], x_send.at[k], x_recv.at[k], p.over_x)
-
-    def own_copy(i):
-        k = i % slots
-        return pltpu.make_async_copy(items[i][2], own_slot.at[k], own_sem.at[k])
+        return remote_copy(made_slot.at[k], x_slot.at[k], x_send.at[k], x_recv.at[k], p.over_x)
 
     def y_copy(i):
         k, g = i % slots, (i // 2) % far_slots
@@ -527,11 +515,11 @@
 
     def result_inner(i):
         k = i % slots
-        return pltpu.make_async_copy(total_slot.at[k], items[i][3], out_sem.at[k])
+        return pltpu.make_async_copy(total_slot.at[k], items[i][1], out_sem.at[k])
 
     def result_outer(i):
         k = i % slots
-        return pltpu.make_async_copy(z_slot.at[k], items[i][3], out_sem.at[k])
+        return pltpu.make_async_copy(z_slot.at[k], items[i][1], out_sem.at[k])
 
     def add(left, right, target):
         target[...] = (left[...].astype(jnp.float32) + right[...].astype(jnp.float32)).astype(
@@ -539,14 +527,14 @@
         )
 
     def stage_send(i):
+        k = i % slots
+        items[i][2](made_slot.at[k], own_slot.at[k])
         if i >= slots:
             pl.semaphore_wait(x_free, 1)
         x_copy(i).start()
-        own_copy(i).start()
 
     def stage_pair(i):
         x_copy(i).wait()
-        own_copy(i).wait()
         k = i % slots
         add(x_slot.at[k], own_slot.at[k], pair_slot.at[k])
         if i + slots < count:
@@ -638,10 +626,13 @@
 
 def reduce_scratch(slots, far_slots, rows, cols):
     dma, regular = pltpu.SemaphoreType.DMA, pltpu.SemaphoreType.REGULAR
-    counts = (slots,) * 3 + (far_slots,) + (slots,) * 4
+    counts = (slots,) * 4 + (far_slots,) + (slots,) * 4
     return [pltpu.VMEM((n, rows, cols), jnp.bfloat16) for n in counts] + [
-        dma((n,)) for n in (slots,) * 3 + (far_slots,) * 2 + (slots,) * 5
+        dma((n,)) for n in (slots,) * 2 + (far_slots,) * 2 + (slots,) * 5
     ] + [regular] * 4
+
+
+PARTS = 4
 
 
 class RowSum:
@@ -655,9 +646,24 @@
         return ref.at[pl.ds(k * self.rows, self.rows), :]
 
     def hop(self, ref, k):
-        source = (self.block(ref, 3), self.block(ref, 1), self.sent)[k]
-        target = self.p.over_y if k == 2 else self.p.over_core
-        return remote_copy(source, self.arrived.at[k], self.send_sem.at[k], self.recv_sem.at[k], target)
+        return remote_copy(
+            self.block(ref, 3 - 2 * k),
+            self.arrived.at[k],
+            self.send_sem.at[k],
+            self.recv_sem.at[k],
+            self.p.over_core,
+        )
+
+    def hop_y(self, part):
+        size = self.rows // PARTS
+        cut = pl.ds(part * size, size)
+        return remote_copy(
+            self.sent.at[cut, :],
+            self.arrived.at[2, cut, :],
+            self.send_sem.at[2 + part],
+            self.recv_sem.at[2 + part],
+            self.p.over_y,
+        )
 
     def load(self, ref, k):
         return pltpu.make_async_copy(self.block(ref, k), self.loaded, self.load_sem)
@@ -671,26 +677,29 @@
         if not local:
             self.load(ref, 2).start()
 
-    def middle(self, ref, local):
-        self.hop(ref, 0).wait()
-        if not local:
-            self.load(ref, 2).wait()
+    def middle(self, ref, local, part):
+        if part == 0:
+            self.hop(ref, 0).wait()
+            if not local:
+                self.load(ref, 2).wait()
         base = self.block(ref, 2) if local else self.loaded
-
-        @pl.loop(0, self.rows // 32)
+        size = self.rows // PARTS
+
+        @pl.loop(part * size // 32, (part + 1) * size // 32)
         def _(k):
             at = pl.ds(pl.multiple_of(k * 32, 32), 32)
             self.sent[at, :] = (
                 base[at, :].astype(jnp.float32) + self.arrived[0, at, :].astype(jnp.float32)
             ).astype(jnp.bfloat16)
 
-        self.hop(ref, 2).start()
-        if not local:
+        self.hop_y(part).start()
+        if part == PARTS - 1 and not local:
             self.load(ref, 0).start()
 
     def finish(self, ref, local):
         self.hop(ref, 1).wait()
-        self.hop(ref, 2).wait()
+        for part in range(PARTS):
+            self.hop_y(part).wait()
         if not local:
             self.load(ref, 0).wait()
 
@@ -1082,24 +1091,24 @@
 
     at_step(0, begin)
     at_step(1, first_norm)
-    at_step(2, call(rows_start, 1))
-    at_step(3, call(rows_wait, 0), call(join_start, 0))
-    at_step(4, call(rows_start, 2))
-    at_step(7, call(join_pass, 0))
-    at_step(9, call(join_end, 0), lambda: keep(act, act_out))
-    at_step(10, call(weights_wait, 0, 6), call(project, 0), lambda: keep(qkv_mat, qkv_mat_out))
-    at_step(10, call(project, 1))
-    at_step(11, call(project, 2), call(project, 3), head_rows, lambda: keep(qkv, qkv_out))
-    at_step(12, *(call(attention_block, b) for b in range(4)))
-    at_step(13, lambda: keep(attended, attended_out), call(weights_wait, 6, 8), call(out_block, 3))
-    at_step(13, call(out_block, 1), call(sums.start, 0, partial, True), call(out_block, 2))
-    at_step(13, call(sums.middle, partial, True), call(out_block, 0))
-    at_step(14, lambda: keep(out_mat, out_mat_out), call(rows_wait, 2), lambda: keep(hidden, resid_out))
-    at_step(17, second_norm)
-    at_step(18, call(rows_wait, 1), call(join_start, 1))
-    at_step(21, call(join_pass, 2))
-    at_step(22, call(join_end, 2), lambda: keep(two, two_out))
-    at_step(24, call(join_pass, 1))
+    at_step(5, call(rows_wait, 0), call(join_start, 0), call(rows_start, 1))
+    at_step(7, call(rows_start, 2))
+    at_step(10, call(rows_wait, 1), call(join_start, 1), call(join_pass, 0))
+    at_step(16, call(join_pass, 1))
+    at_step(11, call(weights_wait, 0, 6), call(project, 0))
+    at_step(12, join(0, 0).wait, call(project, 1), lambda: keep(qkv_mat, qkv_mat_out))
+    at_step(13, join(0, 1).wait_send, join(0, 2).wait, call(project, 2), lambda: keep(act, act_out))
+    at_step(14, call(project, 3), head_rows, lambda: keep(qkv, qkv_out))
+    at_step(15, call(attention_block, 0), call(attention_block, 1))
+    at_step(16, call(attention_block, 2))
+    at_step(17, call(attention_block, 3), lambda: keep(attended, attended_out))
+    at_step(18, call(weights_wait, 6, 8), call(out_block, 3), call(out_block, 1))
+    at_step(18, call(sums.start, 0, partial, True))
+    at_step(19, call(out_block, 2), *(call(sums.middle, partial, True, part) for part in range(PARTS)))
+    at_step(19, call(out_block, 0), lambda: keep(out_mat, out_mat_out))
+    at_step(19, call(rows_wait, 2), lambda: keep(hidden, resid_out))
+    at_step(24, second_norm)
+    at_step(27, call(join_pass, 2), call(join_end, 2), lambda: keep(two, two_out))
     lag = 2
     for i in range(count + 2 * lag):
         if i < count:
@@ -1216,8 +1225,8 @@
             dma((2, 3)),
             dma((2, 3)),
             dma((3,)),
-            dma((3,)),
-            dma((3,)),
+            dma((2 + PARTS,)),
+            dma((2 + PARTS,)),
             dma((8,)),
         ],
         compiler_params=pltpu.CompilerParams(
@@ -1244,8 +1253,9 @@
     info,
     vector_ref,
     small_in,
-    down_parts,
-    up_parts,
+    gelu_hbm,
+    pre_hbm,
+    act_two_hbm,
     two_part,
     mlp_part,
     hidden_hbm,
@@ -1263,8 +1273,6 @@
     rows_out,
     rows_grad,
     small,
-    out_products,
-    qkv_products,
     engine,
     base,
     hidden_grad,
@@ -1280,7 +1288,7 @@
     values,
     key_sum,
     value_sum,
-    stage,
+    strips,
     packed,
     arrived,
     sent,
@@ -1292,7 +1300,7 @@
     sum_load,
     join_send,
     join_recv,
-    stage_sem,
+    strip_sem,
     row_send,
     row_recv,
     share_send,
@@ -1322,36 +1330,91 @@
     up_cols = up_sum.shape[1] // 2
     strip = out_sum.shape[1]
 
-    def four(ref):
-        return tuple(ref.at[k] for k in range(4))
-
-    groups = (
-        (
-            down_parts,
-            down_rows // rows,
-            1,
-            lambda h, r, c: down_sum.at[aligned(h * down_rows + r * rows, rows), :],
-        ),
-        (
-            up_parts,
-            strip // rows,
-            up_cols // cols,
-            lambda h, r, c: up_sum.at[pl.ds(r * rows, rows), aligned(h * up_cols + c * cols, cols)],
-        ),
-        (
-            four(out_products),
-            features // rows,
-            1,
-            lambda h, r, c: out_sum.at[aligned(h * features + r * rows, rows), :],
-        ),
-        (
-            four(qkv_products),
-            strip // rows,
-            3,
-            lambda h, r, c: qkv_sums[c].at[pl.ds(r * rows, rows), aligned(h * cols, cols)],
-        ),
-    )
-    run, steps = reduce_stages(p, groups, engine)
+    def over_tokens(left, right, target):
+        target[...] = lax.dot_general(
+            left, right, (((0,), (0,)), ((), ())), preferred_element_type=f32
+        ).astype(target.dtype)
+
+    per_down, per_up = down_rows // strip, up_cols // cols
+    strip_count = per_down + per_up
+
+    def strip_load(n):
+        source = gelu_hbm if n < per_down else pre_hbm
+        cut = pl.ds((n % per_down) * strip, strip)
+        return pltpu.make_async_copy(source.at[:, cut], strips.at[n % 2], strip_sem.at[n % 2])
+
+    def resident_load(k):
+        source = (cot_hbm, act_two_hbm, act_hbm)[k]
+        return pltpu.make_async_copy(source, act, load_sem.at[5])
+
+    def strip_ready(n):
+        strip_load(n).wait()
+        if n + 1 < strip_count:
+            strip_load(n + 1).start()
+
+    def homes_of(far):
+        return (p.homes[1], p.homes[3]) if far else (p.homes[0], p.homes[2])
+
+    def down_item(r, far):
+        def make(send, own):
+            if far and r % 2 == 0:
+                if r == 0:
+                    resident_load(0).wait()
+                strip_ready(r // 2)
+            left = strips.at[(r // 2) % 2, :, pl.ds((r % 2) * rows, rows)]
+            for home, target in zip(homes_of(far), (send, own)):
+                over_tokens(left[...], act[:, aligned(home * strip, strip)], target)
+
+        side = 1 - y if far else y
+        return far, down_sum.at[aligned(side * down_rows + r * rows, rows), :], make
+
+    def up_item(c, r, far):
+        def make(send, own):
+            if far and r == 0:
+                if c == 0:
+                    resident_load(1).start()
+                    resident_load(1).wait()
+                strip_ready(per_down + c)
+            for home, target in zip(homes_of(far), (send, own)):
+                over_tokens(
+                    act[:, aligned(home * strip + r * rows, rows)], strips[c % 2], target
+                )
+
+        side = 1 - y if far else y
+        place = up_sum.at[pl.ds(r * rows, rows), aligned(side * up_cols + c * cols, cols)]
+        return far, place, make
+
+    def out_item(r, far):
+        def make(send, own):
+            for home, target in zip(homes_of(far), (send, own)):
+                over_tokens(
+                    attended[:, pl.ds(r * rows, rows)], low[:, aligned(home * strip, strip)], target
+                )
+
+        side = 1 - y if far else y
+        return far, out_sum.at[aligned(side * features + r * rows, rows), :], make
+
+    def qkv_item(r, c, far):
+        def make(send, own):
+            if far and r == 0 and c == 0:
+                resident_load(2).start()
+                resident_load(2).wait()
+            for home, target in zip(homes_of(far), (send, own)):
+                over_tokens(
+                    act[:, aligned(home * strip + r * rows, rows)],
+                    qkv_grad[:, pl.ds(c * cols, cols)],
+                    target,
+                )
+
+        side = 1 - y if far else y
+        return far, qkv_sums[c].at[pl.ds(r * rows, rows), aligned(side * cols, cols)], make
+
+    sides = (True, False)
+    items = [down_item(r, far) for r in range(down_rows // rows) for far in sides]
+    items += [up_item(c, r, far) for c in range(per_up) for r in range(strip // rows) for far in sides]
+    items += [out_item(r, far) for r in range(features // rows) for far in sides]
+    items += [qkv_item(r, c, far) for r in range(strip // rows) for c in range(3) for far in sides]
+    run, steps = reduce_stages(p, items, engine)
 
     loads = [
         pltpu.make_async_copy(source, target, load_sem.at[k])
@@ -1362,7 +1425,7 @@
                 (out_hbm, out_mat),
                 (qkv_hbm, qkv),
                 (attended_hbm, attended),
-                (act_hbm, act),
+                (cot_hbm, act),
                 (qkv_mat_hbm, qkv_mat),
                 (resid_hbm, base),
             )
@@ -1375,15 +1438,17 @@
     quarter = own_rows // 4 // group_rows
 
     def start():
-        for k in range(7):
+        loads[5].start()
+        strip_load(0).start()
+        sums.start(0, two_part, False)
+        for k in (0, 1, 2, 3, 4, 6):
             loads[k].start()
         small[...] = small_in[...]
         key_sum[...] = jnp.zeros_like(key_sum)
         value_sum[...] = jnp.zeros_like(value_sum)
-        sums.start(0, two_part, False)
-
-    def two_middle():
-        sums.middle(two_part, False)
+
+    def two_middle(part):
+        sums.middle(two_part, False, part)
 
     def two_finish():
         sums.finish(two_part, False)
@@ -1412,16 +1477,29 @@
         return low.at[pl.ds(k * own_rows, own_rows), :]
 
     def join(k):
-        source, place, target = ((0, 1, p.over_core), (0, 2, p.over_y), (2, 3, p.over_core))[k]
-        return remote_copy(low_block(source), low_block(place), join_send.at[k], join_recv.at[k], target)
+        source, place = ((0, 1), (None, None), (2, 3))[k]
+        return remote_copy(
+            low_block(source), low_block(place), join_send.at[k], join_recv.at[k], p.over_core
+        )
+
+    def join_y(part):
+        size = own_rows // PARTS
+        return remote_copy(
+            low.at[pl.ds(part * size, size), :],
+            low.at[pl.ds(2 * own_rows + part * size, size), :],
+            join_send.at[3 + part],
+            join_recv.at[3 + part],
+            p.over_y,
+        )
 
     def join_start():
         join(0).start()
-        join(1).start()
+        join_y(0).start()
         sums.release(0)
 
     def join_pass():
-        join(1).wait_recv()
+        for part in range(PARTS):
+            join_y(part).wait_recv()
         join(2).start()
 
     def attend_block(k):
@@ -1442,15 +1520,16 @@
         attend_block(2)
 
     def attend_last():
-        join(1).wait_send()
+        for part in range(PARTS):
+            join_y(part).wait_send()
         join(2).wait()
         attend_block(3)
 
     def mlp_start():
         sums.start(1, mlp_part, False)
 
-    def mlp_middle():
-        sums.middle(mlp_part, False)
+    def mlp_middle(part):
+        sums.middle(mlp_part, False, part)
 
     def mlp_finish():
         sums.finish(mlp_part, False)
@@ -1545,39 +1624,6 @@
         spot = aligned(column * features, features)
         small[pl.ds(VALUE_BIAS, 1), spot] += jnp.sum(value_grad, 0, keepdims=True)
 
-    stored = []
-
-    def store(value, target):
-        k = len(stored) % 2
-        if len(stored) >= 2:
-            stored[-2].wait()
-        stage[k] = value.astype(bf16)
-        copy = pltpu.make_async_copy(stage.at[k], target, stage_sem.at[k])
-        copy.start()
-        stored.append(copy)
-
-    def over_tokens(left, right):
-        return lax.dot_general(left, right, (((0,), (0,)), ((), ())), preferred_element_type=f32)
-
-    def out_product(k):
-        store(
-            over_tokens(attended[...], low[:, aligned(p.homes[k] * strip, strip)]),
-            out_products.at[k],
-        )
-
-    def qkv_product(k, c):
-        if k == 0 and c == 0:
-            loads[5].wait()
-        cut = pl.ds(c * features, features)
-        store(
-            over_tokens(act[:, aligned(p.homes[k] * strip, strip)], qkv_grad[:, cut]),
-            qkv_products.at[k, :, cut],
-        )
-
-    def products_end():
-        stored[-2].wait()
-        stored[-1].wait()
-
     def one_block(k):
         if k == 3:
             loads[6].wait()
@@ -1593,8 +1639,8 @@
     def one_start():
         sums.start(2, low, True)
 
-    def one_middle():
-        sums.middle(low, True)
+    def one_middle(part):
+        sums.middle(low, True, part)
 
     def one_finish():
         sums.finish(low, True)
@@ -1631,40 +1677,46 @@
     def at_step(step, *tasks):
         plan.setdefault(step, []).extend(tasks)
 
-    at_step(0, start)
-    at_step(2, two_middle)
-    at_step(7, two_finish, call(two_rows, 0))
+    at_step(2, call(two_middle, 0))
+    at_step(3, call(two_middle, 1))
+    at_step(4, call(two_middle, 2))
+    at_step(5, call(two_middle, 3))
+    at_step(9, two_finish, call(two_rows, 0))
     for k in range(1, 4):
-        at_step(7 + k // 2, call(two_rows, k))
-    at_step(8, join_start, mlp_start)
-    at_step(9, attend_own)
-    at_step(10, mlp_middle, attend_peer)
-    at_step(12, head_rows)
-    at_step(13, join_pass)
-    at_step(14, attend_far)
-    at_step(15, attend_last)
-    at_step(16, call(attention_block, 0), call(attention_block, 1))
-    at_step(17, call(attention_block, 2))
-    at_step(18, call(attention_block, 3))
-    at_step(19, *(call(attention_end, k) for k in range(4)))
+        at_step(9 + k // 2, call(two_rows, k))
+    at_step(10, join_start)
+    for k in range(1, 4):
+        at_step(10 + k, join_y(k).start)
+    at_step(11, attend_own)
+    at_step(12, attend_peer)
+    at_step(14, head_rows)
+    at_step(17, join_pass)
+    at_step(18, attend_far)
+    at_step(19, attend_last)
+    at_step(20, call(attention_block, 0), call(attention_block, 1))
+    at_step(21, call(attention_block, 2))
+    at_step(22, call(attention_block, 3))
+    at_step(23, *(call(attention_end, k) for k in range(4)))
+    at_step(14, mlp_start)
     for k in range(4):
-        at_step(19 + k, *(call(qkv_product, k, c) for c in range(3)))
-        at_step(23, call(out_product, k))
-    at_step(24, products_end, call(one_block, 3), call(one_block, 1), one_start)
-    at_step(25, call(one_block, 2), call(one_block, 0))
-    at_step(26, one_middle)
-    at_step(20, mlp_finish, lambda: rows_start(0), loads[7].start)
-    at_step(25, lambda: rows_share(0))
-    at_step(31, one_finish, share(0).wait, call(one_rows, 0))
+        at_step(16 + k, call(mlp_middle, k))
+    at_step(25, mlp_finish, loads[7].start, lambda: rows_start(0))
+    at_step(33, lambda: rows_share(0))
+    at_step(36, call(one_block, 3), call(one_block, 1), one_start)
+    at_step(37, call(one_block, 2), call(one_block, 0))
+    for k in range(4):
+        at_step(38 + k, call(one_middle, k))
+    at_step(45, one_finish, share(0).wait, call(one_rows, 0))
     for k in range(1, 4):
-        at_step(31 + k // 2, call(one_rows, k))
-    at_step(32, lambda: rows_start(1))
-    at_step(33, small_copy(0).start)
+        at_step(45 + k // 2, call(one_rows, k))
+    at_step(46, lambda: rows_start(1))
+    at_step(47, small_copy(0).start)
     for k in range(4):
-        at_step(35 + 2 * k, call(small_add, k), small_copy(k + 1).start)
-    at_step(43, call(small_add, 4))
-    at_step(38, lambda: rows_share(1))
-    at_step(44, share(1).wait)
+        at_step(49 + 2 * k, call(small_add, k), small_copy(k + 1).start)
+    at_step(57, call(small_add, 4))
+    at_step(55, lambda: rows_share(1))
+    at_step(58, share(1).wait)
+    start()
     for step in range(steps):
         run(step)
         for task in plan.get(step, ()):
@@ -1676,8 +1728,9 @@
     length,
     vectors,
     small,
-    down_parts,
-    up_parts,
+    gelu_low,
+    pre_low,
+    act_two,
     two_part,
     mlp_part,
     hidden,
@@ -1693,25 +1746,20 @@
     bf16, f32 = jnp.bfloat16, jnp.float32
     hbm = pl.BlockSpec(memory_space=pl.ANY)
     vmem = pl.BlockSpec(memory_space=pltpu.VMEM)
-    down_rows, strip = down_parts[0].shape
-    up_cols = up_parts[0].shape[1]
+    down_rows, up_cols = gelu_low.shape[1], pre_low.shape[1]
     tokens, features = attended.shape
     own_rows, width = hidden.shape
+    strip = width // 4
     depth = slots // 2
     engine = reduce_scratch(6, 4, 256, 512)
     n_engine = len(engine)
 
     def kernel(*refs):
-        ins, rest = refs[:21], refs[21:]
-        outs, scratch = rest[:11], rest[11:]
+        ins, rest = refs[:16], refs[16:]
+        outs, scratch = rest[:9], rest[9:]
         backward_kernel(
             head_size,
-            ins[0],
-            ins[1],
-            ins[2],
-            ins[3:7],
-            ins[7:11],
-            *ins[11:],
+            *ins,
             outs[0],
             outs[1],
             outs[2],
@@ -1738,11 +1786,9 @@
             jax.ShapeDtypeStruct((slots, own_rows // depth, width), bf16),
             jax.ShapeDtypeStruct((slots, own_rows // depth, width), bf16),
             jax.ShapeDtypeStruct(small.shape, f32),
-            jax.ShapeDtypeStruct((4, features, strip), bf16),
-            jax.ShapeDtypeStruct((4, strip, 3 * features), bf16),
         ),
-        in_specs=[pl.BlockSpec(memory_space=pltpu.SMEM), vmem, vmem] + [hbm] * 18,
-        out_specs=(hbm,) * 8 + (vmem,) + (hbm,) * 2,
+        in_specs=[pl.BlockSpec(memory_space=pltpu.SMEM), vmem, vmem] + [hbm] * 13,
+        out_specs=(hbm,) * 8 + (vmem,),
         scratch_shapes=engine
         + [
             hold((own_rows, width), f32),
@@ -1759,18 +1805,18 @@
             hold((tokens, features)),
             hold((tokens, features), f32),
             hold((tokens, features), f32),
-            hold((2, features, strip)),
+            hold((2, tokens, strip)),
             hold((own_rows, width)),
             hold((3, own_rows, width)),
             hold((own_rows, width)),
             hold((own_rows, width)),
             hold((5,) + small.shape, f32),
             dma((8,)),
-            dma((3,)),
-            dma((3,)),
+            dma((2 + PARTS,)),
+            dma((2 + PARTS,)),
             dma(()),
-            dma((3,)),
-            dma((3,)),
+            dma((3 + PARTS,)),
+            dma((3 + PARTS,)),
             dma((2,)),
             dma((2, depth)),
             dma((2, depth)),
@@ -1782,15 +1828,16 @@
             regular,
         ],
         compiler_params=pltpu.CompilerParams(
-            collective_id=1, has_side_effects=True, vmem_limit_bytes=58 << 20
+            collective_id=1, has_side_effects=True, vmem_limit_bytes=60 << 20
         ),
         cost_estimate=pl.CostEstimate(flops=0, bytes_accessed=64 << 20, transcendentals=0),
     )(
         length,
         vectors,
         small,
-        *down_parts,
-        *up_parts,
+        gelu_low,
+        pre_low,
+        act_two,
         two_part,
         mlp_part,
         hidden,
@@ -1840,14 +1887,6 @@
     strip = query_weight.shape[0]
     own_rows = depth * block_rows
 
-    def strip_of(v, home):
-        return lax.dynamic_slice_in_dim(v, home * strip, strip, 1)
-
-    homes = (2 * y + 1 - x, 2 * (1 - y) + 1 - x, f, 2 * (1 - y) + x)
-
-    def products(product):
-        return tuple(product(home).astype(bf16) for home in homes)
-
     slot = x * depth + z
     length = seq_lengths[dealing[slot]]
     arrived = pick_slots(layer_input, dealing, t * depth, depth)
@@ -1898,8 +1937,6 @@
     pre_grad = back_product(cot_low, down_mat) * slope
     pre_low = pre_grad.astype(bf16)
     up_bias_part = jnp.sum(pre_grad, 0)
-    down_parts = products(lambda home: weight_product(gelu_low, strip_of(cot_low, home)))
-    up_parts = products(lambda home: weight_product(strip_of(act_two, home), pre_low))
     two_part = back_product(pre_low, up_mat).astype(bf16)
     mlp_part = matmul(gelu_low, down_mat).astype(bf16)
     column = 2 * t + y
@@ -1917,15 +1954,14 @@
         rows_out,
         rows_grad,
         totals,
-        _,
-        _,
     ) = backward_all(
         head_size,
         length[None],
         vectors_whole,
         small,
-        down_parts,
-        up_parts,
+        gelu_low,
+        pre_low,
+        act_two,
         two_part,
         mlp_part,
         hidden,

time: 852 us -> 766 us (0.90)
  Pallas kernels: 693 us -> 635 us
  matrix products: 95.2 us -> 57.4 us
    pallas_call x1, Pallas kernels: 295 us -> 247 us  [forward_all(): pl.pallas_call(functools.partial(forward_kernel, head_size), out_shape=(m...]
    dot_general x8 -> x0, matrix products: 40.6 us -> none  [weight_product(): jnp.einsum('td,te->de', left, right, preferred_element_type=jnp.float32)]
    pallas_call x1, Pallas kernels: 398 us -> 388 us  [backward_all(): pl.pallas_call(kernel, out_shape=(jax.ShapeDtypeStruct((2 * down_rows, st...]
where the time goes in v5:
time: 766 us; the launch traced here: 753 us
  Pallas kernels  635 us (83%)
  matrix products  57.4 us (7%)
  other arithmetic  31.9 us (4%)
  local copies, waits for them, and re-layouts  16.9 us (2%)
  between operations  11.4 us (1%)
    pallas_call x1, Pallas kernels, backward_all(): pl.pallas_call(kernel, out_shape=(jax.ShapeDtypeStruct((2 * down_rows, st...  388 us
    pallas_call x1, Pallas kernels, forward_all(): pl.pallas_call(functools.partial(forward_kernel, head_size), out_shape=(m...  247 us
    dot_general x2, matrix products, back_product(): jnp.einsum('te,de->td', left, right, preferred_element_type=jnp.float32)  29 us
    dot_general x2, matrix products, matmul(): return jnp.dot(left, right, preferred_element_type=jnp.float32)  28.4 us

profile of v5, /device:TPU:0, one launch (start us, length us, event | category | flops | bytes accessed | tf_op | source)
XLA Modules:
  0.0 752.7 jit_solution(17296401397114943789)
XLA Ops:
  0.7 1.5 fusion.7
  4.1 1.2 dynamic_slice.52.info.refs_0_
  6.0 0.7 stack.19
  6.7 0.7 stack.20
  7.4 0.7 stack.21
  8.0 0.7 stack.22
  8.7 0.7 stack.23
  9.4 0.7 concatenate.13
  10.7 0.7 maximum_convert_fusion
  19.4 1.8 constant_dynamic-slice_fusion.5
  21.2 1.5 pad_maximum_fusion.arrived_hbm
  22.7 1.1 dynamic-slice_convert_fusion.cot_hbm
  23.8 247.5 %shard_map.347 = (bf16[2048,1536]{1,0:T(8,128)(2,1)}, bf16[512,2048]{1,0:T(8,128)(2,1)}, bf16[2048,2048]{1,0:T(8,128)(2,1)}, bf16[2048,2048]{1,0:T(8,128)(2,1)},...) custom-call(s32[1]{0:T(128)} %dynamic_slice.52.info.refs_0_, ...), custom_call_target="tpu_custom_call" | custom-call | bytes 67108864 | tf_op jit(solution)/shard_map/pallas_call | solution.py:1180
  271.5 0.9 constant_dynamic-slice_fusion.1
  272.4 15.9 %multiply_convert_fusion = (bf16[1024,2048]{1,0:T(8,128)(2,1)}, f32[1024,2048]{1,0:T(8,128)}) fusion(f32[2048]{0:T(1024)S(1)} %bitcast.42, bf16[1024,2048]{1,0:T(8,128)(2,1)} %get-tuple-element.69.refs_5_, bf16[2048,2048]{1,0:T(8,128)(2,1)} %get-tuple-element.70), kind=kOutput, calls=%fused_computation.6 | convolution fusion | flops 8602517504 | bytes 25174016 | tf_op jit(solution)/shard_map/dot_general | solution.py:41
  288.3 15.0 %fusion.5 = (bf16[1024,2048]{1,0:T(8,128)(2,1)}, f32[2048]{0:T(1024)S(1)}) fusion(f32[1024,2048]{1,0:T(8,128)} %get-tuple-element.113, f32[2048]{0:T(1024)S(1)} %bitcast.43, bf16[1024,2048]{1,0:T(8,128)(2,1)S(1)} %copy-done, bf16[2048,2048]{1,0:T(8,128)(2,1)S(1)} %copy-done.13), kind=kOutput, calls=%fused_computation.30 | convolution fusion | flops 8615098368 | bytes 25182208 | tf_op jit(solution)/shard_map/te,de->td/dot_general | solution.py:49
  304.1 14.0 %convolution_convert_fusion.1.refs_6_ = bf16[1024,2048]{1,0:T(8,128)(2,1)} fusion(bf16[1024,2048]{1,0:T(8,128)(2,1)} %get-tuple-element.90.refs_4_, bf16[2048,2048]{1,0:T(8,128)(2,1)} %get-tuple-element.70), kind=kOutput, calls=%fused_computation.9 | convolution fusion | flops 8592031744 | bytes 16777216 | tf_op jit(solution)/shard_map/te,de->td/dot_general | solution.py:49
  318.1 12.5 %convolution_convert_fusion.refs_7_ = bf16[1024,2048]{1,0:T(8,128)(2,1)} fusion(bf16[1024,2048]{1,0:T(8,128)(2,1)S(1)} %copy-done.2, bf16[2048,2048]{1,0:T(8,128)(2,1)} %get-tuple-element.68), kind=kOutput, calls=%fused_computation.8 | convolution fusion | flops 8592031744 | bytes 16777216 | tf_op jit(solution)/shard_map/dot_general | solution.py:41
  330.6 387.6 %shard_map.348 = (bf16[4096,512]{1,0:T(8,128)(2,1)}, bf16[512,4096]{1,0:T(8,128)(2,1)}, bf16[1024,512]{1,0:T(8,128)(2,1)}, bf16[512,1024]{1,0:T(8,128)(2,1)}, bf...) custom-call(s32[1]{0:T(128)} %dynamic_slice.52.info.refs_0_, ...), custom_call_target="tpu_custom_call" | custom-call | bytes 67108864 | tf_op jit(solution)/shard_map/pallas_call | solution.py:1777
  718.2 4.3 convert_element_type.64
  722.5 2.5 convert_element_type.65
  725.0 1.6 fusion.6
  726.6 2.9 convert_element_type.66
  729.5 0.8 dynamic-slice_bitcast_fusion
  731.0 1.6 convert_element_type.67
  732.6 1.6 convert_element_type.68
  734.2 1.6 convert_element_type.69
  735.8 4.5 convert_element_type.70
  740.3 1.4 dynamic_slice.66
  741.7 6.9 convert_element_type.71
  749.2 1.3 divide_sqrt_fusion
  750.6 1.9 multiply_convert_fusion.1
  (42 shorter events, 3.2 us)
Async XLA Ops:
  11.6 11.1 %copy-start.11 = (f32[16,128]{1,0:T(8,128)}, f32[16,128]{1,0:T(8,128)S(1)}, u32[]{:S(2)}) copy-start(f32[16,128]{1,0:T(8,128)S(1)} %dynamic_update_slice.9.head_hbm) | copy-start | bytes 24580
  19.4 3.3 copy-start.5
  272.4 15.9 %copy-start = (bf16[1024,2048]{1,0:T(8,128)(2,1)S(1)}, bf16[1024,2048]{1,0:T(8,128)(2,1)}, u32[]{:S(2)}) copy-start(bf16[1024,2048]{1,0:T(8,128)(2,1)} %get-tuple-element.67.refs_9_) | copy-start | bytes 12582916
  272.4 15.9 %copy-start.13 = (bf16[2048,2048]{1,0:T(8,128)(2,1)S(1)}, bf16[2048,2048]{1,0:T(8,128)(2,1)}, u32[]{:S(2)}) copy-start(bf16[2048,2048]{1,0:T(8,128)(2,1)} %get-tuple-element.68) | copy-start | bytes 25165828
  288.2 15.4 %copy-start.12 = (f32[8,128]{1,0:T(8,128)S(1)}, f32[8,128]{1,0:T(8,128)}, u32[]{:S(2)}) copy-start(f32[8,128]{1,0:T(8,128)} %get-tuple-element.71) | copy-start | bytes 12292
  304.0 14.0 %copy-start.10 = (f32[16,2048]{1,0:T(8,128)}, f32[16,2048]{1,0:T(8,128)S(1)}, u32[]{:S(2)}) copy-start(f32[16,2048]{1,0:T(8,128)S(1)} %dynamic_update_slice.11.refs_2_) | copy-start | bytes 393220
  304.1 14.0 %copy-start.2 = (bf16[1024,2048]{1,0:T(8,128)(2,1)S(1)}, bf16[1024,2048]{1,0:T(8,128)(2,1)}, u32[]{:S(2)}) copy-start(bf16[1024,2048]{1,0:T(8,128)(2,1)} %get-tuple-element.112.refs_3_) | copy-start | bytes 12582916
  718.2 4.3 copy-start.6
  722.5 8.6 %copy-start.9 = (bf16[512,1024]{1,0:T(8,128)(2,1)S(1)}, bf16[512,1024]{1,0:T(8,128)(2,1)}, u32[]{:S(2)}) copy-start(bf16[512,1024]{1,0:T(8,128)(2,1)} %get-tuple-element.83) | copy-start | bytes 3145732
  725.0 7.6 %copy-start.8 = (bf16[512,1024]{1,0:T(8,128)(2,1)S(1)}, bf16[512,1024]{1,0:T(8,128)(2,1)}, u32[]{:S(2)}) copy-start(bf16[512,1024]{1,0:T(8,128)(2,1)} %get-tuple-element.84) | copy-start | bytes 3145732
  726.6 7.5 %copy-start.7 = (bf16[1024,512]{1,0:T(8,128)(2,1)S(1)}, bf16[1024,512]{1,0:T(8,128)(2,1)}, u32[]{:S(2)}) copy-start(bf16[1024,512]{1,0:T(8,128)(2,1)} %get-tuple-element.85) | copy-start | bytes 3145732
  731.0 4.8 copy-start.1
  741.7 8.9 %copy-start.3 = (bf16[512,1024]{1,0:T(8,128)(2,1)S(1)}, bf16[512,1024]{1,0:T(8,128)(2,1)}, u32[]{:S(2)}) copy-start(bf16[512,1024]{1,0:T(8,128)(2,1)} %q_ref.1) | copy-start | bytes 3145732
  741.7 8.9 %copy-start.4 = (bf16[512,1024]{1,0:T(8,128)(2,1)S(1)}, bf16[512,1024]{1,0:T(8,128)(2,1)}, u32[]{:S(2)}) copy-start(bf16[512,1024]{1,0:T(8,128)(2,1)} %k_ref.1) | copy-start | bytes 3145732

commit v6 on v5

--- a/solution.py
+++ b/solution.py
@@ -746,6 +746,91 @@
 )
 
 
+def prepare_kernel(dealing, lengths, place, rows_ref, cot_ref, rows_out, cot_out, bias_ref):
+    step = pl.program_id(0)
+    rows_out[...] = rows_ref[...]
+    cot = cot_ref[...]
+    cot_out[...] = cot.astype(cot_out.dtype)
+
+    @pl.when(step == 0)
+    def _():
+        bias_ref[...] = jnp.zeros_like(bias_ref)
+
+    bias_ref[pl.ds(0, 1), :] += jnp.sum(cot[0], 0, keepdims=True)
+
+
+def prepare(dealing, seq_lengths, place, layer_input, cotangent, count):
+    block = (1,) + layer_input.shape[1:]
+    width = layer_input.shape[2]
+    return pl.pallas_call(
+        prepare_kernel,
+        out_shape=(
+            jax.ShapeDtypeStruct((count,) + block[1:], jnp.float32),
+            jax.ShapeDtypeStruct((count,) + block[1:], jnp.bfloat16),
+            jax.ShapeDtypeStruct((8, width), jnp.float32),
+        ),
+        grid_spec=pltpu.PrefetchScalarGridSpec(
+            num_scalar_prefetch=3,
+            grid=(count,),
+            in_specs=[
+                pl.BlockSpec(block, lambda j, dealing, lengths, place: (dealing[place[0] * count + j], 0, 0)),
+                pl.BlockSpec(block, lambda j, dealing, lengths, place: (place[0] * count + j, 0, 0)),
+            ],
+            out_specs=(
+                pl.BlockSpec(block, lambda j, *_: (j, 0, 0)),
+                pl.BlockSpec(block, lambda j, *_: (j, 0, 0)),
+                pl.BlockSpec((8, width), lambda j, *_: (0, 0)),
+            ),
+        ),
+    )(dealing, seq_lengths, place, layer_input, cotangent)
+
+
+def finish_kernel(head_size, place, level_ref, totals_ref, query_ref, key_ref, *refs):
+    count = (len(refs) - 3) // 2
+    for source, target in zip(refs[:count], refs[count : 2 * count]):
+        target[...] = source[...].astype(target.dtype)
+    query_out, key_out, factor = refs[2 * count :]
+    level = level_ref[0]
+    heads = factor.shape[1] // head_size
+
+    @pl.when(pl.program_id(0) == 0)
+    def _():
+        peaks = totals_ref[pl.ds(PEAKS, 1), :]
+        lane = lax.broadcasted_iota(jnp.int32, peaks.shape, 1)
+        for h in range(heads):
+            mine = jnp.where(lane == place[0] * heads + h, peaks, NEG)
+            peak = jnp.max(mine, -1, keepdims=True)
+            value = jnp.sqrt(level / jnp.maximum(peak, level))
+            factor[:, pl.ds(h * head_size, head_size)] = jnp.broadcast_to(value, (8, head_size))
+
+    scale = factor[pl.ds(0, 1), :]
+    query_out[...] = (query_ref[...].astype(jnp.float32) * scale).astype(query_out.dtype)
+    key_out[...] = (key_ref[...].astype(jnp.float32) * scale).astype(key_out.dtype)
+
+
+def finish_all(head_size, place, level, totals, query_weight, key_weight, arrays):
+    steps = 8
+
+    def spec(v):
+        block = (v.shape[0] // steps,) + v.shape[1:]
+        return pl.BlockSpec(block, lambda i: (i,) + (0,) * (v.ndim - 1))
+
+    smem = pl.BlockSpec(memory_space=pltpu.SMEM)
+    weights = (query_weight, key_weight)
+    return pl.pallas_call(
+        functools.partial(finish_kernel, head_size),
+        out_shape=tuple(jax.ShapeDtypeStruct(v.shape, jnp.float32) for v in arrays)
+        + tuple(jax.ShapeDtypeStruct(v.shape, v.dtype) for v in weights),
+        grid=(steps,),
+        in_specs=[smem, smem, pl.BlockSpec(totals.shape, lambda i: (0, 0))]
+        + [spec(v) for v in weights]
+        + [spec(v) for v in arrays],
+        out_specs=tuple(spec(v) for v in arrays) + tuple(spec(v) for v in weights),
+        scratch_shapes=[pltpu.VMEM((8, query_weight.shape[1]), jnp.float32)],
+        compiler_params=pltpu.CompilerParams(vmem_limit_bytes=48 << 20),
+    )(place, level, totals, *weights, *arrays)
+
+
 def forward_kernel(
     head_size,
     info,
@@ -762,16 +847,20 @@
     qkv_mat_out,
     out_mat_out,
     up_all,
-    down_all,
+    down_out,
     act_out,
-    cot_all,
+    cot_out,
     qkv_out,
     attended_out,
     hidden_out,
     resid_out,
     two_out,
+    back_out,
     vec_all,
     peaks,
+    cot_all,
+    down_all,
+    back_stage,
     qkv_mat,
     out_mat,
     fresh,
@@ -1064,10 +1153,39 @@
                 attended[at, :], out_mat[:, cut], preferred_element_type=f32
             ).astype(bf16)
 
+    spot = []
+
+    def keep_resid():
+        spot.append(len(kept))
+        keep(hidden, resid_out)
+
+    back_sem = [out_sem.at[10], out_sem.at[11]]
+    unit_rows_per_chunk = units // pieces
+
+    def back_store(r):
+        cut = pl.ds(r * unit_rows_per_chunk, unit_rows_per_chunk)
+        return pltpu.make_async_copy(back_stage.at[r % 2], back_out.at[:, cut], back_sem[r % 2])
+
+    def back_chunk(r):
+        weights_wait(8 + pieces + r, 9 + pieces + r)
+        if r >= 2:
+            back_store(r - 2).wait()
+
+        @pl.loop(0, 4)
+        def _(b):
+            at = pl.ds(pl.multiple_of(b * own_rows, own_rows), own_rows)
+            back_stage[r % 2, at, :] = lax.dot_general(
+                cot_all[at, :],
+                down_all[pl.ds(r * unit_rows_per_chunk, unit_rows_per_chunk), :],
+                (((1,), (1,)), ((), ())),
+                preferred_element_type=f32,
+            ).astype(bf16)
+
+        back_store(r).start()
+
     def second_norm():
         sums.finish(partial, True)
-        kept[-1].wait()
-        kept.pop()
+        kept.pop(spot[0]).wait()
         bias, gain, shift = vector_row(OUT_BIAS), vector_row(GAIN_TWO), vector_row(SHIFT_TWO)
 
         @pl.loop(0, own_rows // group_rows)
@@ -1106,9 +1224,14 @@
     at_step(18, call(sums.start, 0, partial, True))
     at_step(19, call(out_block, 2), *(call(sums.middle, partial, True, part) for part in range(PARTS)))
     at_step(19, call(out_block, 0), lambda: keep(out_mat, out_mat_out))
-    at_step(19, call(rows_wait, 2), lambda: keep(hidden, resid_out))
+    at_step(19, call(rows_wait, 2), keep_resid)
+    at_step(21, call(join_end, 1), lambda: keep(cot_all, cot_out))
+    at_step(23, call(back_chunk, 0))
     at_step(24, second_norm)
-    at_step(27, call(join_pass, 2), call(join_end, 2), lambda: keep(two, two_out))
+    at_step(24, call(back_chunk, 1))
+    at_step(25, call(back_chunk, 2))
+    at_step(26, call(back_chunk, 3))
+    at_step(27, call(join_pass, 2), call(back_chunk, 4))
     lag = 2
     for i in range(count + 2 * lag):
         if i < count:
@@ -1136,12 +1259,18 @@
         for task in plan.get(i, ()):
             task()
 
-    weights_wait(8, count)
+    for r in range(5, pieces):
+        back_chunk(r)
+    keep(down_all, down_out)
+    join_end(2)
+    keep(two, two_out)
+    weights_wait(8, 8 + pieces)
+    back_store(pieces - 2).wait()
+    back_store(pieces - 1).wait()
     for i in range(count):
         y_copy(i).wait_send()
         x_copy(i, True).wait_send()
         z_copy(i, True).wait_send()
-    join_end(1)
     for copy in kept:
         copy.wait()
 
@@ -1191,12 +1320,16 @@
             made((own_rows, width), f32),
             made((own_rows, width), f32),
             made((tokens, width)),
+            made((tokens, units)),
             made((8, width), f32),
             made((8, 128), f32),
         ),
         in_specs=[pl.BlockSpec(memory_space=pltpu.SMEM)] + [hbm] * 10,
-        out_specs=(hbm,) * 11 + (vmem,) * 2,
+        out_specs=(hbm,) * 12 + (vmem,) * 2,
         scratch_shapes=[
+            hold((tokens, width)),
+            hold((units, width)),
+            hold((2, tokens, units // 8)),
             hold((width, 3 * features)),
             hold((features, width)),
             hold((depth, block_rows, width), f32),
@@ -1227,7 +1360,7 @@
             dma((3,)),
             dma((2 + PARTS,)),
             dma((2 + PARTS,)),
-            dma((8,)),
+            dma((12,)),
         ],
         compiler_params=pltpu.CompilerParams(
             collective_id=0, has_side_effects=True, vmem_limit_bytes=56 << 20
@@ -1677,45 +1810,43 @@
     def at_step(step, *tasks):
         plan.setdefault(step, []).extend(tasks)
 
-    at_step(2, call(two_middle, 0))
-    at_step(3, call(two_middle, 1))
-    at_step(4, call(two_middle, 2))
-    at_step(5, call(two_middle, 3))
-    at_step(9, two_finish, call(two_rows, 0))
+    for k in range(4):
+        at_step(3 + k, call(two_middle, k))
+    at_step(11, two_finish, call(two_rows, 0))
     for k in range(1, 4):
-        at_step(9 + k // 2, call(two_rows, k))
-    at_step(10, join_start)
+        at_step(11 + k // 2, call(two_rows, k))
+    at_step(12, join_start)
     for k in range(1, 4):
-        at_step(10 + k, join_y(k).start)
-    at_step(11, attend_own)
-    at_step(12, attend_peer)
+        at_step(12 + k, join_y(k).start)
+    at_step(13, attend_own)
+    at_step(14, attend_peer)
     at_step(14, head_rows)
-    at_step(17, join_pass)
-    at_step(18, attend_far)
-    at_step(19, attend_last)
-    at_step(20, call(attention_block, 0), call(attention_block, 1))
-    at_step(21, call(attention_block, 2))
-    at_step(22, call(attention_block, 3))
-    at_step(23, *(call(attention_end, k) for k in range(4)))
-    at_step(14, mlp_start)
+    at_step(19, join_pass)
+    at_step(20, attend_far)
+    at_step(21, attend_last)
+    at_step(22, call(attention_block, 0), call(attention_block, 1))
+    at_step(22 + 1, call(attention_block, 2))
+    at_step(22 + 2, call(attention_block, 3))
+    at_step(22 + 3, *(call(attention_end, k) for k in range(4)))
+    at_step(16, mlp_start)
     for k in range(4):
-        at_step(16 + k, call(mlp_middle, k))
-    at_step(25, mlp_finish, loads[7].start, lambda: rows_start(0))
-    at_step(33, lambda: rows_share(0))
+        at_step(19 + 1 * k, call(mlp_middle, k))
+    at_step(29, mlp_finish, loads[7].start, lambda: rows_start(0))
+    at_step(38, lambda: rows_share(0))
     at_step(36, call(one_block, 3), call(one_block, 1), one_start)
-    at_step(37, call(one_block, 2), call(one_block, 0))
+    at_step(36 + 1, call(one_block, 2), call(one_block, 0))
     for k in range(4):
         at_step(38 + k, call(one_middle, k))
-    at_step(45, one_finish, share(0).wait, call(one_rows, 0))
+    at_step(47, one_finish, share(0).wait, call(one_rows, 0))
     for k in range(1, 4):
-        at_step(45 + k // 2, call(one_rows, k))
-    at_step(46, lambda: rows_start(1))
-    at_step(47, small_copy(0).start)
+        at_step(47 + k // 2, call(one_rows, k))
+    at_step(48, lambda: rows_start(1))
+    at_step(49, small_copy(0).start)
     for k in range(4):
-        at_step(49 + 2 * k, call(small_add, k), small_copy(k + 1).start)
-    at_step(57, call(small_add, 4))
-    at_step(55, lambda: rows_share(1))
-    at_step(58, share(1).wait)
+        at_step(49 + 2 + 2 * k, call(small_add, k), small_copy(k + 1).start)
+    at_step(49 + 5 * 2, call(small_add, 4))
+    at_step(57, lambda: rows_share(1))
+    at_step(59, share(1).wait)
     start()
     for step in range(steps):
         run(step)
@@ -1887,14 +2018,15 @@
     strip = query_weight.shape[0]
     own_rows = depth * block_rows
 
-    slot = x * depth + z
-    length = seq_lengths[dealing[slot]]
-    arrived = pick_slots(layer_input, dealing, t * depth, depth)
-    cot_part = lax.dynamic_slice_in_dim(cotangent, t * depth, depth, 0)
-    down_bias_part = jnp.sum(cot_part, (0, 1))
+    place = t[None]
+    length = seq_lengths[dealing[x * depth + z]]
+    arrived, cot_part, down_bias_part = prepare(
+        dealing, seq_lengths, place, layer_input, cotangent, depth
+    )
     vectors = jnp.concatenate(
-        [jnp.stack([attn_gain, attn_shift, out_bias, mlp_gain, mlp_shift, down_bias]), up_bias], 0
-    ).astype(f32)
+        [attn_gain, attn_shift, out_bias, mlp_gain, mlp_shift, down_bias, up_bias.reshape(-1)]
+    )
+    vectors = vectors.reshape(8, strip).astype(f32)
     head_vectors = jnp.concatenate([query_bias, value_bias], 0).astype(f32)
     head_vectors = lax.dynamic_update_slice(
         jnp.zeros((head_vectors.shape[0], head_size), f32), head_vectors, (0, f * query_bias.shape[1])
@@ -1911,6 +2043,7 @@
         hidden,
         resid,
         act_two,
+        back,
         vectors_whole,
         peaks,
     ) = forward_all(
@@ -1925,7 +2058,7 @@
         up_weight,
         down_weight,
         arrived,
-        cot_part.astype(bf16),
+        cot_part,
     )
     peaks = peaks[:local_heads, 0]
     up_vec = lax.dynamic_slice_in_dim(vectors_whole, 6 + y, 1, 0)
@@ -1934,13 +2067,13 @@
     cdf = 0.5 * (1.0 + lax.erf(pre * INV_ROOT_TWO))
     gelu_low = (pre * cdf).astype(bf16)
     slope = cdf + pre * (jnp.exp(-0.5 * pre * pre) * INV_ROOT_TWO_PI)
-    pre_grad = back_product(cot_low, down_mat) * slope
+    pre_grad = back.astype(f32) * slope
     pre_low = pre_grad.astype(bf16)
     up_bias_part = jnp.sum(pre_grad, 0)
     two_part = back_product(pre_low, up_mat).astype(bf16)
     mlp_part = matmul(gelu_low, down_mat).astype(bf16)
     column = 2 * t + y
-    small = jnp.zeros((16, width), f32).at[DOWN_BIAS].set(down_bias_part)
+    small = jnp.zeros((16, width), f32).at[DOWN_BIAS].set(down_bias_part[0])
     small = lax.dynamic_update_slice(small, up_bias_part[None], (UP_BIAS + column, 0))
     small = small.at[PEAKS].set(NEG)
     small = lax.dynamic_update_slice(small, peaks[None], (PEAKS, local_heads * (2 * t + y)))
@@ -1982,27 +2115,43 @@
         totals, (UP_BIAS + up_bias.shape[0] * t, f * strip), (up_bias.shape[0], strip)
     )
     peak_all = lax.dynamic_slice(totals, (PEAKS, 2 * local_heads * t), (1, 2 * local_heads))[0]
-    level = clip_level[0]
-    factor = jnp.repeat(jnp.sqrt(level / jnp.maximum(peak_all, level)), head_size)
-    query_clipped = (query_weight.astype(f32) * factor[None, :]).astype(bf16)
-    key_clipped = (key_weight.astype(f32) * factor[None, :]).astype(bf16)
+    (
+        final_output,
+        final_grad,
+        query_weight_grad,
+        key_weight_grad,
+        value_weight_grad,
+        out_weight_grad,
+        up_weight_grad,
+        down_weight_grad,
+        query_clipped,
+        key_clipped,
+    ) = finish_all(
+        head_size,
+        place,
+        clip_level,
+        totals,
+        query_weight,
+        key_weight,
+        (rows_out, rows_grad, query_sum, key_sum, value_sum, out_sum, up_sum, down_sum),
+    )
     return (
-        rows_out.astype(f32),
-        rows_grad.astype(f32),
+        final_output,
+        final_grad,
         rows_sum[GAIN_ONE],
         rows_sum[SHIFT_ONE],
-        query_sum.astype(f32),
+        query_weight_grad,
         head_sum[0],
-        key_sum.astype(f32),
-        value_sum.astype(f32),
+        key_weight_grad,
+        value_weight_grad,
         head_sum[1],
-        out_sum.astype(f32),
+        out_weight_grad,
         rows_sum[OUT_BIAS],
         rows_sum[GAIN_TWO],
         rows_sum[SHIFT_TWO],
-        up_sum.astype(f32),
+        up_weight_grad,
         unit_sum,
-        down_sum.astype(f32),
+        down_weight_grad,
         rows_sum[DOWN_BIAS],
         peak_all,
         query_clipped,

time: 766 us -> 729 us (0.952)
  other arithmetic: 31.9 us -> 0.7 us
  Pallas kernels: 635 us -> 654 us
  matrix products: 57.4 us -> 43.1 us
    convert_element_type x10 -> x0, other arithmetic: 28.4 us -> none  [the longest x1 6.93 us: split_body(): down_sum.astype(f32)]
    pallas_call x0 -> x2, Pallas kernels: none -> 21.9 us  [the longest x1 16.7 us: finish_all(): pl.pallas_call(functools.partial(finish_kernel, head_size), out_shape=tup...]
    dot_general x2 -> x1, matrix products: 29 us -> 10.8 us  [back_product(): jnp.einsum('te,de->td', left, right, preferred_element_type=jnp.float32)]
    pallas_call x1, Pallas kernels: 388 us -> 377 us  [backward_all(): pl.pallas_call(kernel, out_shape=(jax.ShapeDtypeStruct((2 * down_rows, st...]
    pallas_call x1, Pallas kernels: 247 us -> 255 us  [forward_all(): pl.pallas_call(functools.partial(forward_kernel, head_size), out_shape=(m...]
where the time goes in v6:
time: 729 us; the launch traced here: 720 us
  Pallas kernels  654 us (90%)
  matrix products  43.1 us (6%)
  local copies, waits for them, and re-layouts  18.2 us (2%)
    pallas_call x1, Pallas kernels, backward_all(): pl.pallas_call(kernel, out_shape=(jax.ShapeDtypeStruct((2 * down_rows, st...  377 us
    pallas_call x1, Pallas kernels, forward_all(): pl.pallas_call(functools.partial(forward_kernel, head_size), out_shape=(m...  255 us
    dot_general x2, matrix products, matmul(): return jnp.dot(left, right, preferred_element_type=jnp.float32)  32.3 us
    pallas_call x1, Pallas kernels, finish_all(): pl.pallas_call(functools.partial(finish_kernel, head_size), out_shape=tup...  16.7 us

profile of v6, /device:TPU:0, one launch (start us, length us, event | category | flops | bytes accessed | tf_op | source)
XLA Modules:
  0.0 719.9 jit_solution(16549296141993225108)
XLA Ops:
  0.7 1.2 dynamic_slice.24
  3.9 1.2 dynamic_slice.25.info.refs_0_
  5.1 0.7 maximum_convert_fusion
  6.1 5.2 shard_map.347
  11.4 0.3 dynamic-update-slice.6
  11.6 0.2 dynamic-update-slice.7
  11.8 0.2 dynamic-update-slice.8
  12.1 0.2 dynamic-update-slice.9
  12.3 0.2 dynamic-update-slice.10
  12.5 0.2 dynamic-update-slice.11
  12.7 0.6 reshape.97.vec_hbm
  13.4 255.4 %shard_map.348 = (bf16[2048,1536]{1,0:T(8,128)(2,1)}, bf16[512,2048]{1,0:T(8,128)(2,1)}, bf16[2048,2048]{1,0:T(8,128)(2,1)}, bf16[2048,2048]{1,0:T(8,128)(2,1)},...) custom-call(s32[1]{0:T(128)} %dynamic_slice.25.info.refs_0_, ...), custom_call_target="tpu_custom_call" | custom-call | bytes 67108864 | tf_op jit(solution)/shard_map/pallas_call | solution.py:1309
  268.8 0.9 constant_dynamic-slice_fusion.1
  269.6 16.8 %fusion.5 = (bf16[1024,2048]{1,0:T(8,128)(2,1)S(1)}, f32[2048]{0:T(1024)S(1)}, bf16[1024,2048]{1,0:T(8,128)(2,1)S(1)}) fusion(f32[2048]{0:T(1024)S(1)} %bitcast.32, bf16[1024,2048]{1,0:T(8,128)(2,1)} %get-tuple-element.84, bf16[1024,2048]{1,0:T(8,128)(2,1)} %get-tuple-element.85.refs_5_, bf16[2048,2048]{1,0:T(8,128)(2,1)} %get-tuple-element.86), kind=kOutput, calls=%fused_computation.20 | convolution fusion | flops 8621389824 | bytes 25182208 | tf_op jit(solution)/shard_map/dot_general | solution.py:41
  286.4 15.5 %convolution_convert_fusion.refs_7_ = bf16[1024,2048]{1,0:T(8,128)(2,1)} fusion(bf16[1024,2048]{1,0:T(8,128)(2,1)S(1)} %get-tuple-element.118.refs_3_, bf16[2048,2048]{1,0:T(8,128)(2,1)} %get-tuple-element.88), kind=kOutput, calls=%fused_computation.8 | convolution fusion | flops 8592031744 | bytes 16777216 | tf_op jit(solution)/shard_map/dot_general | solution.py:41
  301.9 10.8 %convolution_convert_fusion.1.refs_6_ = bf16[1024,2048]{1,0:T(8,128)(2,1)} fusion(bf16[1024,2048]{1,0:T(8,128)(2,1)S(1)} %get-tuple-element.116.refs_4_, bf16[2048,2048]{1,0:T(8,128)(2,1)S(1)} %copy-done.18), kind=kOutput, calls=%fused_computation.9 | convolution fusion | flops 8592031744 | bytes 16777216 | tf_op jit(solution)/shard_map/te,de->td/dot_general | solution.py:49
  312.8 0.8 slice.59
  313.6 0.2 dynamic_update_slice.10
  313.9 0.2 scatter.9
  314.2 0.2 dynamic_update_slice.11.refs_2_
  314.5 0.6 copy-done.8
  315.1 376.9 %shard_map.349 = (bf16[4096,512]{1,0:T(8,128)(2,1)}, bf16[512,4096]{1,0:T(8,128)(2,1)}, bf16[1024,512]{1,0:T(8,128)(2,1)}, bf16[512,1024]{1,0:T(8,128)(2,1)}, bf...) custom-call(s32[1]{0:T(128)} %dynamic_slice.25.info.refs_0_, ...), custom_call_target="tpu_custom_call" | custom-call | bytes 67108864 | tf_op jit(solution)/shard_map/pallas_call | solution.py:1908
  692.7 1.2 copy-done.2
  693.9 1.2 copy-done.3
  695.1 1.2 copy-done.4
  696.3 0.9 copy-done.5
  697.2 16.7 %shard_map.350 = (f32[8,64,2048]{2,1,0:T(8,128)}, f32[8,64,2048]{2,1,0:T(8,128)}, f32[512,1024]{1,0:T(8,128)}, f32[512,1024]{1,0:T(8,128)}, f32[512,1024]{1,0:T(...) custom-call(s32[1]{0:T(128)} %bitcast.place, ...), custom_call_target="tpu_custom_call" | custom-call | tf_op jit(solution)/shard_map/pallas_call | solution.py:820
  713.9 0.8 dynamic-slice_bitcast_fusion
  714.7 0.7 dynamic-slice_bitcast_fusion.1
  715.4 1.6 fusion.7
  717.0 1.4 dynamic_slice.30
  718.4 1.3 dynamic-slice_bitcast_fusion.3
  (42 shorter events, 0.4 us)
Async XLA Ops:
  6.0 5.3 copy-start.9
  6.0 5.3 copy-start.12
  6.0 5.6 copy-start.13
  6.0 5.8 copy-start.14
  6.1 6.0 copy-start.15
  6.1 6.2 copy-start.16
  6.1 6.4 copy-start.17
  6.1 6.6 copy-start.10
  286.4 15.5 %copy-start.7 = (bf16[1024,2048]{1,0:T(8,128)(2,1)}, bf16[1024,2048]{1,0:T(8,128)(2,1)S(1)}, u32[]{:S(2)}) copy-start(bf16[1024,2048]{1,0:T(8,128)(2,1)S(1)} %get-tuple-element.118.refs_3_) | copy-start | bytes 12582916
  286.4 15.5 %copy-start.6 = (bf16[1024,2048]{1,0:T(8,128)(2,1)}, bf16[1024,2048]{1,0:T(8,128)(2,1)S(1)}, u32[]{:S(2)}) copy-start(bf16[1024,2048]{1,0:T(8,128)(2,1)S(1)} %get-tuple-element.116.refs_4_) | copy-start | bytes 12582916
  286.4 15.5 %copy-start.18 = (bf16[2048,2048]{1,0:T(8,128)(2,1)S(1)}, bf16[2048,2048]{1,0:T(8,128)(2,1)}, u32[]{:S(2)}) copy-start(bf16[2048,2048]{1,0:T(8,128)(2,1)} %get-tuple-element.86) | copy-start | bytes 25165828
  301.9 12.1 %copy-start.11 = (f32[8,128]{1,0:T(8,128)S(1)}, f32[8,128]{1,0:T(8,128)}, u32[]{:S(2)}) copy-start(f32[8,128]{1,0:T(8,128)} %get-tuple-element.87) | copy-start | bytes 12292
  314.4 0.7 copy-start.8
  315.1 377.5 %copy-start = (bf16[512,1024]{1,0:T(8,128)(2,1)S(1)}, bf16[512,1024]{1,0:T(8,128)(2,1)}, u32[]{:S(2)}) copy-start(bf16[512,1024]{1,0:T(8,128)(2,1)} %query_ref.1) | copy-start | bytes 3145732
  315.1 377.5 %copy-start.1 = (bf16[512,1024]{1,0:T(8,128)(2,1)S(1)}, bf16[512,1024]{1,0:T(8,128)(2,1)}, u32[]{:S(2)}) copy-start(bf16[512,1024]{1,0:T(8,128)(2,1)} %key_ref.1) | copy-start | bytes 3145732
  692.6 1.2 copy-start.2
  693.9 1.2 copy-start.3
  695.1 1.2 copy-start.4
  696.3 0.9 copy-start.5

commit v7 on v6

--- a/solution.py
+++ b/solution.py
@@ -827,7 +827,7 @@
         + [spec(v) for v in arrays],
         out_specs=tuple(spec(v) for v in arrays) + tuple(spec(v) for v in weights),
         scratch_shapes=[pltpu.VMEM((8, query_weight.shape[1]), jnp.float32)],
-        compiler_params=pltpu.CompilerParams(vmem_limit_bytes=48 << 20),
+        compiler_params=pltpu.CompilerParams(vmem_limit_bytes=60 << 20),
     )(place, level, totals, *weights, *arrays)
 
 
@@ -1210,9 +1210,9 @@
     at_step(0, begin)
     at_step(1, first_norm)
     at_step(5, call(rows_wait, 0), call(join_start, 0), call(rows_start, 1))
-    at_step(7, call(rows_start, 2))
+    at_step(10, call(rows_start, 2))
     at_step(10, call(rows_wait, 1), call(join_start, 1), call(join_pass, 0))
-    at_step(16, call(join_pass, 1))
+    at_step(18, call(join_pass, 1))
     at_step(11, call(weights_wait, 0, 6), call(project, 0))
     at_step(12, join(0, 0).wait, call(project, 1), lambda: keep(qkv_mat, qkv_mat_out))
     at_step(13, join(0, 1).wait_send, join(0, 2).wait, call(project, 2), lambda: keep(act, act_out))
@@ -1389,8 +1389,8 @@
     gelu_hbm,
     pre_hbm,
     act_two_hbm,
-    two_part,
-    mlp_part,
+    up_hbm,
+    down_hbm,
     hidden_hbm,
     cot_hbm,
     resid_hbm,
@@ -1406,6 +1406,8 @@
     rows_out,
     rows_grad,
     small,
+    two_part,
+    mlp_part,
     engine,
     base,
     hidden_grad,
@@ -1442,6 +1444,8 @@
     small_recv,
     core_free,
     y_free,
+    low_core,
+    low_y,
 ):
     f32, bf16 = jnp.float32, jnp.bfloat16
     own_rows, width = base.shape
@@ -1573,12 +1577,72 @@
     def start():
         loads[5].start()
         strip_load(0).start()
-        sums.start(0, two_part, False)
-        for k in (0, 1, 2, 3, 4, 6):
+        low_load(0).start()
+        up_load(0).start()
+        for k in (0, 1, 3, 4):
             loads[k].start()
+        for n in range(3):
+            down_load(n).start()
         small[...] = small_in[...]
         key_sum[...] = jnp.zeros_like(key_sum)
         value_sum[...] = jnp.zeros_like(value_sum)
+
+    def low_load(k):
+        return pltpu.make_async_copy((pre_hbm, gelu_hbm)[k], low, load_sem.at[8])
+
+    def up_load(n):
+        return pltpu.make_async_copy(up_hbm.at[pl.ds(n * strip, strip), :], out_mat, load_sem.at[9])
+
+    def down_load(n):
+        return pltpu.make_async_copy(
+            down_hbm.at[:, pl.ds(n * strip, strip)],
+            qkv_mat.at[:, pl.ds((n % 3) * strip, strip)],
+            load_sem.at[10 + n % 3],
+        )
+
+    held = (keys, values)
+
+    def part_store(k, n):
+        target = (two_part, mlp_part)[k].at[:, pl.ds(n * strip, strip)]
+        return pltpu.make_async_copy(held[n % 2], target, load_sem.at[13 + n % 2])
+
+    def part_columns(k, n):
+        if n == 0:
+            low_load(k).wait()
+        (down_load(n) if k else up_load(n)).wait()
+        if n >= 2:
+            part_store(k, n - 2).wait()
+
+        @pl.loop(0, 4)
+        def _(b):
+            at = pl.ds(pl.multiple_of(b * own_rows, own_rows), own_rows)
+            if k:
+                right, side = qkv_mat[:, pl.ds((n % 3) * strip, strip)], 0
+            else:
+                right, side = out_mat[...], 1
+            held[n % 2][at, :] = lax.dot_general(
+                low[at, :], right, (((1,), (side,)), ((), ())), preferred_element_type=f32
+            ).astype(bf16)
+
+        part_store(k, n).start()
+        if k == 0 and n < 3:
+            up_load(n + 1).start()
+        if k == 0 and n == 3:
+            low_load(1).start()
+            loads[2].start()
+        if k == 1 and n == 0:
+            down_load(3).start()
+        if k == 1 and n == 3:
+            loads[6].start()
+
+    def part_end(k):
+        part_store(k, 2).wait()
+        part_store(k, 3).wait()
+        if k == 0:
+            sums.start(0, two_part, False)
+        else:
+            grant(low_core, p.over_core)
+            grant(low_y, p.over_y)
 
     def two_middle(part):
         sums.middle(two_part, False, part)
@@ -1626,6 +1690,8 @@
         )
 
     def join_start():
+        pl.semaphore_wait(low_core, 1)
+        pl.semaphore_wait(low_y, 1)
         join(0).start()
         join_y(0).start()
         sums.release(0)
@@ -1810,29 +1876,34 @@
     def at_step(step, *tasks):
         plan.setdefault(step, []).extend(tasks)
 
+    for n in range(4):
+        at_step(n, call(part_columns, 0, n))
+        at_step(5 + 2 * n, call(part_columns, 1, n))
+    at_step(4, call(part_end, 0))
+    at_step(13, call(part_end, 1))
     for k in range(4):
-        at_step(3 + k, call(two_middle, k))
-    at_step(11, two_finish, call(two_rows, 0))
+        at_step(7 + k, call(two_middle, k))
+    at_step(16, two_finish, call(two_rows, 0))
     for k in range(1, 4):
-        at_step(11 + k // 2, call(two_rows, k))
-    at_step(12, join_start)
+        at_step(16 + k // 2, call(two_rows, k))
+    at_step(17, join_start)
     for k in range(1, 4):
-        at_step(12 + k, join_y(k).start)
-    at_step(13, attend_own)
-    at_step(14, attend_peer)
-    at_step(14, head_rows)
-    at_step(19, join_pass)
-    at_step(20, attend_far)
-    at_step(21, attend_last)
-    at_step(22, call(attention_block, 0), call(attention_block, 1))
-    at_step(22 + 1, call(attention_block, 2))
-    at_step(22 + 2, call(attention_block, 3))
-    at_step(22 + 3, *(call(attention_end, k) for k in range(4)))
-    at_step(16, mlp_start)
+        at_step(17 + k, join_y(k).start)
+    at_step(18, attend_own)
+    at_step(19, attend_peer)
+    at_step(21, head_rows)
+    at_step(24, join_pass)
+    at_step(25, attend_far)
+    at_step(26, attend_last)
+    at_step(27, call(attention_block, 0), call(attention_block, 1))
+    at_step(27 + 1, call(attention_block, 2))
+    at_step(27 + 2, call(attention_block, 3))
+    at_step(27 + 3, *(call(attention_end, k) for k in range(4)))
+    at_step(21, mlp_start)
     for k in range(4):
-        at_step(19 + 1 * k, call(mlp_middle, k))
-    at_step(29, mlp_finish, loads[7].start, lambda: rows_start(0))
-    at_step(38, lambda: rows_share(0))
+        at_step(23 + 1 * k, call(mlp_middle, k))
+    at_step(33, mlp_finish, loads[7].start, lambda: rows_start(0))
+    at_step(42, lambda: rows_share(0))
     at_step(36, call(one_block, 3), call(one_block, 1), one_start)
     at_step(36 + 1, call(one_block, 2), call(one_block, 0))
     for k in range(4):
@@ -1862,8 +1933,8 @@
     gelu_low,
     pre_low,
     act_two,
-    two_part,
-    mlp_part,
+    up_mat,
+    down_mat,
     hidden,
     cot_low,
     resid,
@@ -1887,7 +1958,7 @@
 
     def kernel(*refs):
         ins, rest = refs[:16], refs[16:]
-        outs, scratch = rest[:9], rest[9:]
+        outs, scratch = rest[:11], rest[11:]
         backward_kernel(
             head_size,
             *ins,
@@ -1917,9 +1988,11 @@
             jax.ShapeDtypeStruct((slots, own_rows // depth, width), bf16),
             jax.ShapeDtypeStruct((slots, own_rows // depth, width), bf16),
             jax.ShapeDtypeStruct(small.shape, f32),
+            jax.ShapeDtypeStruct((tokens, width), bf16),
+            jax.ShapeDtypeStruct((tokens, width), bf16),
         ),
         in_specs=[pl.BlockSpec(memory_space=pltpu.SMEM), vmem, vmem] + [hbm] * 13,
-        out_specs=(hbm,) * 8 + (vmem,),
+        out_specs=(hbm,) * 8 + (vmem,) + (hbm,) * 2,
         scratch_shapes=engine
         + [
             hold((own_rows, width), f32),
@@ -1942,7 +2015,7 @@
             hold((own_rows, width)),
             hold((own_rows, width)),
             hold((5,) + small.shape, f32),
-            dma((8,)),
+            dma((15,)),
             dma((2 + PARTS,)),
             dma((2 + PARTS,)),
             dma(()),
@@ -1957,6 +2030,8 @@
             dma((5,)),
             regular,
             regular,
+            regular,
+            regular,
         ],
         compiler_params=pltpu.CompilerParams(
             collective_id=1, has_side_effects=True, vmem_limit_bytes=60 << 20
@@ -1969,8 +2044,8 @@
         gelu_low,
         pre_low,
         act_two,
-        two_part,
-        mlp_part,
+        up_mat,
+        down_mat,
         hidden,
         cot_low,
         resid,
@@ -2070,8 +2145,6 @@
     pre_grad = back.astype(f32) * slope
     pre_low = pre_grad.astype(bf16)
     up_bias_part = jnp.sum(pre_grad, 0)
-    two_part = back_product(pre_low, up_mat).astype(bf16)
-    mlp_part = matmul(gelu_low, down_mat).astype(bf16)
     column = 2 * t + y
     small = jnp.zeros((16, width), f32).at[DOWN_BIAS].set(down_bias_part[0])
     small = lax.dynamic_update_slice(small, up_bias_part[None], (UP_BIAS + column, 0))
@@ -2087,6 +2160,8 @@
         rows_out,
         rows_grad,
         totals,
+        _,
+        _,
     ) = backward_all(
         head_size,
         length[None],
@@ -2095,8 +2170,8 @@
         gelu_low,
         pre_low,
         act_two,
-        two_part,
-        mlp_part,
+        up_mat,
+        down_mat,
         hidden,
         cot_low,
         resid,

time: 729 us -> 713 us (0.978)
  matrix products: 43.1 us -> 18.8 us
  Pallas kernels: 654 us -> 667 us
    dot_general x2 -> x1, matrix products: 32.3 us -> 18.8 us  [matmul(): return jnp.dot(left, right, preferred_element_type=jnp.float32)]
    pallas_call x1, Pallas kernels: 377 us -> 389 us  [backward_all(): pl.pallas_call(kernel, out_shape=(jax.ShapeDtypeStruct((2 * down_rows, st...]
    dot_general x1 -> x0, matrix products: 10.8 us -> none  [back_product(): jnp.einsum('te,de->td', left, right, preferred_element_type=jnp.float32)]
where the time goes in v7:
time: 713 us; the launch traced here: 704 us
  Pallas kernels  667 us (94%)
  matrix products  18.8 us (3%)
  local copies, waits for them, and re-layouts  13.6 us (2%)
    pallas_call x1, Pallas kernels, backward_all(): pl.pallas_call(kernel, out_shape=(jax.ShapeDtypeStruct((2 * down_rows, st...  389 us
    pallas_call x1, Pallas kernels, forward_all(): pl.pallas_call(functools.partial(forward_kernel, head_size), out_shape=(m...  252 us
    pallas_call x1, Pallas kernels, finish_all(): pl.pallas_call(functools.partial(finish_kernel, head_size), out_shape=tup...  20.3 us
    dot_general x1, matrix products, matmul(): return jnp.dot(left, right, preferred_element_type=jnp.float32)  18.8 us

profile of v7, /device:TPU:0, one launch (start us, length us, event | category | flops | bytes accessed | tf_op | source)
XLA Modules:
  0.0 703.8 jit_solution(15600855464566944353)
XLA Ops:
  0.7 1.2 dynamic_slice.24
  3.9 1.2 dynamic_slice.25.info.refs_0_
  5.1 0.7 maximum_convert_fusion
  5.8 0.2 dynamic_update_slice.9.head_hbm
  6.0 0.0 copy-start.6
  6.1 0.0 copy-start.7
  6.1 0.0 copy-start.2
  6.1 5.2 shard_map.347
  11.4 0.3 dynamic-update-slice.6
  11.6 0.2 dynamic-update-slice.7
  11.8 0.2 dynamic-update-slice.8
  12.1 0.2 dynamic-update-slice.9
  12.3 0.2 dynamic-update-slice.10
  12.5 0.2 dynamic-update-slice.11
  12.7 0.6 reshape.97.vec_hbm
  13.4 251.9 %shard_map.348 = (bf16[2048,1536]{1,0:T(8,128)(2,1)}, bf16[512,2048]{1,0:T(8,128)(2,1)}, bf16[2048,2048]{1,0:T(8,128)(2,1)}, bf16[2048,2048]{1,0:T(8,128)(2,1)},...) custom-call(s32[1]{0:T(128)} %dynamic_slice.25.info.refs_0_, ...), custom_call_target="tpu_custom_call" | custom-call | bytes 67108864 | tf_op jit(solution)/shard_map/pallas_call | solution.py:1309
  265.3 0.9 constant_dynamic-slice_fusion.1
  266.1 18.8 %fusion.5 = (bf16[1024,2048]{1,0:T(8,128)(2,1)}, f32[2048]{0:T(1024)S(1)}, bf16[1024,2048]{1,0:T(8,128)(2,1)}) fusion(f32[2048]{0:T(1024)S(1)} %bitcast.28, bf16[1024,2048]{1,0:T(8,128)(2,1)} %get-tuple-element.84, bf16[1024,2048]{1,0:T(8,128)(2,1)} %get-tuple-element.85.refs_5_, bf16[2048,2048]{1,0:T(8,128)(2,1)} %get-tuple-element.86.refs_6_), kind=kOutput, calls=%fused_computation.18 | convolution fusion | flops 8621389824 | bytes 25182208 | tf_op jit(solution)/shard_map/dot_general | solution.py:41
  284.9 0.8 slice.59
  285.8 0.2 dynamic_update_slice.10
  286.0 0.2 scatter.9
  286.2 0.1 slice_reduce_fusion
  286.3 0.2 dynamic_update_slice.11.refs_2_
  286.6 0.0 copy-start
  286.6 0.6 copy-done
  287.2 389.4 %shard_map.349 = (bf16[4096,512]{1,0:T(8,128)(2,1)}, bf16[512,4096]{1,0:T(8,128)(2,1)}, bf16[1024,512]{1,0:T(8,128)(2,1)}, bf16[512,1024]{1,0:T(8,128)(2,1)}, bf...) custom-call(s32[1]{0:T(128)} %dynamic_slice.25.info.refs_0_, ...), custom_call_target="tpu_custom_call" | custom-call | bytes 67108864 | tf_op jit(solution)/shard_map/pallas_call | solution.py:1979
  677.3 20.3 %shard_map.350 = (f32[8,64,2048]{2,1,0:T(8,128)}, f32[8,64,2048]{2,1,0:T(8,128)}, f32[512,1024]{1,0:T(8,128)}, f32[512,1024]{1,0:T(8,128)}, f32[512,1024]{1,0:T(...) custom-call(s32[1]{0:T(128)} %bitcast.place, ...), custom_call_target="tpu_custom_call" | custom-call | tf_op jit(solution)/shard_map/pallas_call | solution.py:820
  697.6 0.8 dynamic-slice_bitcast_fusion
  698.5 0.7 dynamic-slice_bitcast_fusion.1
  699.1 1.6 fusion.7
  700.7 1.4 dynamic_slice.30
  702.1 1.3 dynamic-slice_bitcast_fusion.3
  (22 shorter events, 0.1 us)
Async XLA Ops:
  6.0 5.3 copy-start.1
  6.0 5.3 copy-start.4
  6.0 5.6 copy-start.5
  6.0 5.8 copy-start.6
  6.1 6.0 copy-start.7
  6.1 6.2 copy-start.8
  6.1 6.4 copy-start.9
  6.1 6.6 copy-start.2
  266.1 20.1 %copy-start.3 = (f32[8,128]{1,0:T(8,128)S(1)}, f32[8,128]{1,0:T(8,128)}, u32[]{:S(2)}) copy-start(f32[8,128]{1,0:T(8,128)} %get-tuple-element.87) | copy-start | bytes 12292
  286.6 0.7 copy-start

commit v8 on v7

--- a/solution.py
+++ b/solution.py
@@ -746,7 +746,7 @@
 )
 
 
-def prepare_kernel(dealing, lengths, place, rows_ref, cot_ref, rows_out, cot_out, bias_ref):
+def prepare_kernel(dealing, lengths, place, rows_ref, cot_ref, rows_out, cot_out, bias_ref, length_ref):
     step = pl.program_id(0)
     rows_out[...] = rows_ref[...]
     cot = cot_ref[...]
@@ -755,6 +755,7 @@
     @pl.when(step == 0)
     def _():
         bias_ref[...] = jnp.zeros_like(bias_ref)
+        length_ref[0] = lengths[dealing[place[1]]]
 
     bias_ref[pl.ds(0, 1), :] += jnp.sum(cot[0], 0, keepdims=True)
 
@@ -768,6 +769,7 @@
             jax.ShapeDtypeStruct((count,) + block[1:], jnp.float32),
             jax.ShapeDtypeStruct((count,) + block[1:], jnp.bfloat16),
             jax.ShapeDtypeStruct((8, width), jnp.float32),
+            jax.ShapeDtypeStruct((1,), jnp.int32),
         ),
         grid_spec=pltpu.PrefetchScalarGridSpec(
             num_scalar_prefetch=3,
@@ -780,6 +782,7 @@
                 pl.BlockSpec(block, lambda j, *_: (j, 0, 0)),
                 pl.BlockSpec(block, lambda j, *_: (j, 0, 0)),
                 pl.BlockSpec((8, width), lambda j, *_: (0, 0)),
+                pl.BlockSpec(memory_space=pltpu.SMEM),
             ),
         ),
     )(dealing, seq_lengths, place, layer_input, cotangent)
@@ -1742,7 +1745,7 @@
         sums.release(1)
 
     def row_source(k):
-        return packed.at[pl.ds(k * block_rows, block_rows), :]
+        return packed.at[pl.ds(pl.multiple_of(k * block_rows, block_rows), block_rows), :]
 
     row_ends = (rows_out, rows_grad)
 
@@ -1757,11 +1760,13 @@
     def row_stay(a, k):
         return pltpu.make_async_copy(row_source(k), row_ends[a].at[x * depth + z], row_send.at[a, k])
 
-    def rows_start(a):
-        for k in range(depth):
-            stays = (z == k) & (x == t)
-            pl.when(stays)(lambda k=k: row_stay(a, k).start())
-            pl.when(jnp.logical_not(stays))(lambda k=k: row_copy(a, k).start())
+    def rows_start(a, turn):
+        k = lax.rem(z + turn, depth)
+        if turn:
+            row_copy(a, k).start()
+        else:
+            pl.when(x == t)(lambda: row_stay(a, k).start())
+            pl.when(x != t)(lambda: row_copy(a, k).start())
 
     def share(a):
         group = row_ends[a].at[pl.ds(t * depth, depth)]
@@ -1902,7 +1907,9 @@
     at_step(21, mlp_start)
     for k in range(4):
         at_step(23 + 1 * k, call(mlp_middle, k))
-    at_step(33, mlp_finish, loads[7].start, lambda: rows_start(0))
+    at_step(33, mlp_finish, loads[7].start, call(rows_start, 0, 0))
+    for k in range(1, 4):
+        at_step(33 + k, call(rows_start, 0, k))
     at_step(42, lambda: rows_share(0))
     at_step(36, call(one_block, 3), call(one_block, 1), one_start)
     at_step(36 + 1, call(one_block, 2), call(one_block, 0))
@@ -1911,7 +1918,8 @@
     at_step(47, one_finish, share(0).wait, call(one_rows, 0))
     for k in range(1, 4):
         at_step(47 + k // 2, call(one_rows, k))
-    at_step(48, lambda: rows_start(1))
+    for k in range(4):
+        at_step(48 + k, call(rows_start, 1, k))
     at_step(49, small_copy(0).start)
     for k in range(4):
         at_step(49 + 2 + 2 * k, call(small_add, k), small_copy(k + 1).start)
@@ -2093,9 +2101,8 @@
     strip = query_weight.shape[0]
     own_rows = depth * block_rows
 
-    place = t[None]
-    length = seq_lengths[dealing[x * depth + z]]
-    arrived, cot_part, down_bias_part = prepare(
+    place = jnp.stack([t, x * depth + z])
+    arrived, cot_part, down_bias_part, length = prepare(
         dealing, seq_lengths, place, layer_input, cotangent, depth
     )
     vectors = jnp.concatenate(
@@ -2123,7 +2130,7 @@
         peaks,
     ) = forward_all(
         head_size,
-        length[None],
+        length,
         vectors,
         head_vectors,
         query_weight,
@@ -2164,7 +2171,7 @@
         _,
     ) = backward_all(
         head_size,
-        length[None],
+        length,
         vectors_whole,
         small,
         gelu_low,

time: 713 us -> 707 us (level)
  no operation moved by 1% of the time
where the time goes in v8:
time: 707 us; the launch traced here: 698 us
  Pallas kernels  666 us (94%)
  matrix products  18.8 us (3%)
  local copies, waits for them, and re-layouts  11.2 us (2%)
    pallas_call x1, Pallas kernels, backward_all(): pl.pallas_call(kernel, out_shape=(jax.ShapeDtypeStruct((2 * down_rows, st...  388 us
    pallas_call x1, Pallas kernels, forward_all(): pl.pallas_call(functools.partial(forward_kernel, head_size), out_shape=(m...  252 us
    pallas_call x1, Pallas kernels, finish_all(): pl.pallas_call(functools.partial(finish_kernel, head_size), out_shape=tup...  20.3 us
    dot_general x1, matrix products, matmul(): return jnp.dot(left, right, preferred_element_type=jnp.float32)  18.8 us

profile of v8, /device:TPU:0, one launch (start us, length us, event | category | flops | bytes accessed | tf_op | source)
XLA Modules:
  0.0 698.2 jit_solution(15006212401459396530)
XLA Ops:
  0.7 0.6 pad_add_fusion.place
  1.3 0.0 copy-start.8
  1.3 0.0 copy-start.9
  1.3 0.0 copy-start.10
  1.3 0.0 copy-start.2
  1.3 5.3 shard_map.347
  6.7 0.2 dynamic_update_slice.9.head_hbm
  6.9 0.0 copy-start.1
  6.9 0.3 dynamic-update-slice.6
  7.2 0.2 dynamic-update-slice.7
  7.4 0.2 dynamic-update-slice.8
  7.6 0.2 dynamic-update-slice.9
  7.9 0.2 dynamic-update-slice.10
  8.1 0.2 dynamic-update-slice.11
  8.3 0.6 reshape.97.vec_hbm
  8.9 251.9 %shard_map.348 = (bf16[2048,1536]{1,0:T(8,128)(2,1)}, bf16[512,2048]{1,0:T(8,128)(2,1)}, bf16[2048,2048]{1,0:T(8,128)(2,1)}, bf16[2048,2048]{1,0:T(8,128)(2,1)},...) custom-call(s32[1]{0:T(128)} %get-tuple-element.81.info.refs_0_, ...), custom_call_target="tpu_custom_call" | custom-call | bytes 67108864 | tf_op jit(solution)/shard_map/pallas_call | solution.py:1312
  260.9 0.9 constant_dynamic-slice_fusion.1
  261.7 18.8 %fusion.5 = (bf16[1024,2048]{1,0:T(8,128)(2,1)}, f32[2048]{0:T(1024)S(1)}, bf16[1024,2048]{1,0:T(8,128)(2,1)}) fusion(f32[2048]{0:T(1024)S(1)} %bitcast.28, bf16[1024,2048]{1,0:T(8,128)(2,1)} %get-tuple-element.86, bf16[1024,2048]{1,0:T(8,128)(2,1)} %get-tuple-element.87.refs_5_, bf16[2048,2048]{1,0:T(8,128)(2,1)} %get-tuple-element.88.refs_6_), kind=kOutput, calls=%fused_computation.19 | convolution fusion | flops 8621389824 | bytes 25182208 | tf_op jit(solution)/shard_map/dot_general | solution.py:41
  280.5 0.8 slice.59
  281.4 0.2 dynamic_update_slice.10
  281.6 0.2 scatter.9
  281.8 0.1 slice_reduce_fusion
  281.9 0.2 dynamic_update_slice.11.refs_2_
  282.2 0.0 copy-start
  282.2 0.6 copy-done
  282.8 388.2 %shard_map.349 = (bf16[4096,512]{1,0:T(8,128)(2,1)}, bf16[512,4096]{1,0:T(8,128)(2,1)}, bf16[1024,512]{1,0:T(8,128)(2,1)}, bf16[512,1024]{1,0:T(8,128)(2,1)}, bf...) custom-call(s32[1]{0:T(128)} %get-tuple-element.81.info.refs_0_, ...), custom_call_target="tpu_custom_call" | custom-call | bytes 67108864 | tf_op jit(solution)/shard_map/pallas_call | solution.py:1987
  671.7 20.3 %shard_map.350 = (f32[8,64,2048]{2,1,0:T(8,128)}, f32[8,64,2048]{2,1,0:T(8,128)}, f32[512,1024]{1,0:T(8,128)}, f32[512,1024]{1,0:T(8,128)}, f32[512,1024]{1,0:T(...) custom-call(s32[2]{0:T(128)} %pad_add_fusion.place, ...), custom_call_target="tpu_custom_call" | custom-call | tf_op jit(solution)/shard_map/pallas_call | solution.py:823
  692.0 0.8 dynamic-slice_bitcast_fusion
  692.9 0.7 dynamic-slice_bitcast_fusion.1
  693.5 1.6 fusion.7
  695.2 1.4 dynamic_slice.22
  696.5 1.3 dynamic-slice_bitcast_fusion.3
  (25 shorter events, 0.1 us)
Async XLA Ops:
  1.3 5.4 copy-start.3
  1.3 5.4 copy-start.4
  1.3 5.7 copy-start.6
  1.3 5.9 copy-start.7
  1.3 6.1 copy-start.8
  1.3 6.4 copy-start.9
  1.3 6.6 copy-start.10
  1.3 6.8 copy-start.11
  1.3 7.0 copy-start.2
  6.9 2.0 copy-start.1
  261.7 20.1 %copy-start.5 = (f32[8,128]{1,0:T(8,128)S(1)}, f32[8,128]{1,0:T(8,128)}, u32[]{:S(2)}) copy-start(f32[8,128]{1,0:T(8,128)} %get-tuple-element.89) | copy-start | bytes 12292
  282.2 0.7 copy-start

commit v9 on v8

--- a/solution.py
+++ b/solution.py
@@ -1237,8 +1237,10 @@
     at_step(27, call(join_pass, 2), call(back_chunk, 4))
     lag = 2
     for i in range(count + 2 * lag):
+        for k in (0, 1) if i == 0 else (i + 1,):
+            if k < count:
+                y_copy(k).start()
         if i < count:
-            y_copy(i).start()
             pl.when(even)(lambda i=i: x_copy(i, True).start())
             own_copy(i).start()
         j = i - lag

time: 707 us -> 706 us (level)
  no operation moved by 1% of the time
where the time goes in v9:
time: 706 us; the launch traced here: 697 us
  Pallas kernels  664 us (94%)
  matrix products  18.8 us (3%)
  local copies, waits for them, and re-layouts  11.2 us (2%)
    pallas_call x1, Pallas kernels, backward_all(): pl.pallas_call(kernel, out_shape=(jax.ShapeDtypeStruct((2 * down_rows, st...  389 us
    pallas_call x1, Pallas kernels, forward_all(): pl.pallas_call(functools.partial(forward_kernel, head_size), out_shape=(m...  250 us
    pallas_call x1, Pallas kernels, finish_all(): pl.pallas_call(functools.partial(finish_kernel, head_size), out_shape=tup...  20.3 us
    dot_general x1, matrix products, matmul(): return jnp.dot(left, right, preferred_element_type=jnp.float32)  18.8 us

profile of v9, /device:TPU:0, one launch (start us, length us, event | category | flops | bytes accessed | tf_op | source)
XLA Modules:
  0.0 696.7 jit_solution(8987020408092513338)
XLA Ops:
  0.7 0.6 pad_add_fusion.place
  1.3 0.0 copy-start.8
  1.3 0.0 copy-start.9
  1.3 0.0 copy-start.10
  1.3 0.0 copy-start.2
  1.3 5.3 shard_map.347
  6.7 0.2 dynamic_update_slice.9.head_hbm
  6.9 0.0 copy-start.1
  6.9 0.3 dynamic-update-slice.6
  7.2 0.2 dynamic-update-slice.7
  7.4 0.2 dynamic-update-slice.8
  7.6 0.2 dynamic-update-slice.9
  7.9 0.2 dynamic-update-slice.10
  8.1 0.2 dynamic-update-slice.11
  8.3 0.6 reshape.97.vec_hbm
  8.9 249.9 %shard_map.348 = (bf16[2048,1536]{1,0:T(8,128)(2,1)}, bf16[512,2048]{1,0:T(8,128)(2,1)}, bf16[2048,2048]{1,0:T(8,128)(2,1)}, bf16[2048,2048]{1,0:T(8,128)(2,1)},...) custom-call(s32[1]{0:T(128)} %get-tuple-element.81.info.refs_0_, ...), custom_call_target="tpu_custom_call" | custom-call | bytes 67108864 | tf_op jit(solution)/shard_map/pallas_call | solution.py:1314
  258.9 0.9 constant_dynamic-slice_fusion.1
  259.8 18.8 %fusion.5 = (bf16[1024,2048]{1,0:T(8,128)(2,1)}, f32[2048]{0:T(1024)S(1)}, bf16[1024,2048]{1,0:T(8,128)(2,1)}) fusion(f32[2048]{0:T(1024)S(1)} %bitcast.28, bf16[1024,2048]{1,0:T(8,128)(2,1)} %get-tuple-element.86, bf16[1024,2048]{1,0:T(8,128)(2,1)} %get-tuple-element.87.refs_5_, bf16[2048,2048]{1,0:T(8,128)(2,1)} %get-tuple-element.88.refs_6_), kind=kOutput, calls=%fused_computation.19 | convolution fusion | flops 8621389824 | bytes 25182208 | tf_op jit(solution)/shard_map/dot_general | solution.py:41
  278.5 0.8 slice.59
  279.4 0.2 dynamic_update_slice.10
  279.6 0.2 scatter.9
  279.9 0.1 slice_reduce_fusion
  280.0 0.2 dynamic_update_slice.11.refs_2_
  280.2 0.0 copy-start
  280.2 0.6 copy-done
  280.9 388.7 %shard_map.349 = (bf16[4096,512]{1,0:T(8,128)(2,1)}, bf16[512,4096]{1,0:T(8,128)(2,1)}, bf16[1024,512]{1,0:T(8,128)(2,1)}, bf16[512,1024]{1,0:T(8,128)(2,1)}, bf...) custom-call(s32[1]{0:T(128)} %get-tuple-element.81.info.refs_0_, ...), custom_call_target="tpu_custom_call" | custom-call | bytes 67108864 | tf_op jit(solution)/shard_map/pallas_call | solution.py:1989
  670.2 20.3 %shard_map.350 = (f32[8,64,2048]{2,1,0:T(8,128)}, f32[8,64,2048]{2,1,0:T(8,128)}, f32[512,1024]{1,0:T(8,128)}, f32[512,1024]{1,0:T(8,128)}, f32[512,1024]{1,0:T(...) custom-call(s32[2]{0:T(128)} %pad_add_fusion.place, ...), custom_call_target="tpu_custom_call" | custom-call | tf_op jit(solution)/shard_map/pallas_call | solution.py:823
  690.5 0.8 dynamic-slice_bitcast_fusion
  691.4 0.7 dynamic-slice_bitcast_fusion.1
  692.0 1.6 fusion.7
  693.7 1.4 dynamic_slice.22
  695.0 1.3 dynamic-slice_bitcast_fusion.3
  (25 shorter events, 0.1 us)
Async XLA Ops:
  1.3 5.4 copy-start.3
  1.3 5.4 copy-start.4
  1.3 5.7 copy-start.6
  1.3 5.9 copy-start.7
  1.3 6.1 copy-start.8
  1.3 6.4 copy-start.9
  1.3 6.6 copy-start.10
  1.3 6.8 copy-start.11
  1.3 7.0 %copy-start.2 = (bf16[2,512]{1,0:T(2,128)(2,1)S(1)}, bf16[2,512]{1,0:T(2,128)(2,1)}, u32[]{:S(2)}) copy-start(bf16[2,512]{1,0:T(2,128)(2,1)} %param.40) | copy-start | bytes 6148
  6.9 2.0 copy-start.1
  259.8 20.1 %copy-start.5 = (f32[8,128]{1,0:T(8,128)S(1)}, f32[8,128]{1,0:T(8,128)}, u32[]{:S(2)}) copy-start(f32[8,128]{1,0:T(8,128)} %get-tuple-element.89) | copy-start | bytes 12292
  280.2 0.7 copy-start
